TPU v7x, 32 devices: a whole 2x2x4 slice. The times are simulated.
32 devices in a mesh: blk: 4 (over y, x), grp: 8 (over z, core).
Axes of the slice: x: 2, y: 2, z: 4, core: 2. Of those that a mesh axis runs over, the one named last changes fastest.
Arguments:
- a_blocks: bfloat16 [8, 96, 27, 96, 96], P('grp', 'blk'), may hold values from -0.125 to 0.125
- col_index: int32 [8, 96, 27], P('grp', 'blk'), may hold values from 0 to 95
- prolong: bfloat16 [8, 96, 2, 96, 96], P('grp', 'blk'), may hold values from -0.625 to 0.625
- target: int32 [8, 96, 108], P('grp', 'blk'), may hold values from 0 to 127
Outputs:
- coarse: float32 [8, 16, 96, 96], P('grp', 'blk')
All inputs are finite; a program needn't handle non-finite values.
Results may differ from a plain program's by a relative error of at most 0.0029.
Values may be sent and summed in bfloat16 or wider, within the bound.
No kernel may reach another device: no remote copies, remote signals or barrier semaphores. Data moves between devices by JAX's collectives and lax.ppermute only.
A program may use at most 320 MiB of HBM per device.

v0:
```python
import math

import jax
import jax.numpy as jnp
from jax import lax
from jax.sharding import PartitionSpec as P

OWN = 4


def shards(a_blocks, col_index, prolong, target):
    rows = a_blocks.shape[1]
    nonzeros = a_blocks.shape[2]
    per_row = prolong.shape[2]
    width = a_blocks.shape[-1]
    groups = lax.axis_size("grp")
    members = lax.axis_size("blk")
    coarse_g = OWN * members
    slots = groups * coarse_g
    columns = col_index[0]
    init = jnp.zeros((rows, nonzeros, per_row, width, width), jnp.bfloat16)
    piece = lax.all_gather(prolong, "blk", axis=1, tiled=True)
    count = piece.shape[1]
    inside = (columns >= 0) & (columns < count)
    taken = jnp.take(piece[0], jnp.clip(columns, 0, count - 1), axis=0)
    chosen = jnp.where(inside[:, :, None, None, None], taken, init)
    step = math.gcd(rows, 4)
    a_rows = a_blocks[0]
    p_trans = jnp.swapaxes(prolong[0], -1, -2)
    t_rows = target[0]

    def one_block(total, index):
        low = index * step
        a_part = lax.dynamic_slice_in_dim(a_rows, low, step, 0)
        c_part = lax.dynamic_slice_in_dim(chosen, low, step, 0)
        p_part = lax.dynamic_slice_in_dim(p_trans, low, step, 0)
        t_part = lax.dynamic_slice_in_dim(t_rows, low, step, 0)
        product = jnp.einsum(
            "rkab,rkmbc->rkmac", a_part, c_part, preferred_element_type=jnp.float32
        ).astype(jnp.bfloat16)
        partial_value = jnp.einsum(
            "rnab,rkmbc->rnkmac", p_part, product, preferred_element_type=jnp.float32
        )
        partial_value = partial_value.reshape(-1, width, width)
        total = total + jax.ops.segment_sum(partial_value, t_part.reshape(-1), num_segments=slots)
        return (total, None)

    start_buf = jnp.zeros((slots, width, width), jnp.float32)
    buffer, _ = lax.scan(one_block, start_buf, jnp.arange(rows // step, dtype=jnp.int32))
    buffer = buffer.reshape(groups, coarse_g, width, width)
    received = lax.all_to_all(buffer, "grp", split_axis=0, concat_axis=0, tiled=True)
    summed = jnp.sum(received, axis=0)
    mine = lax.psum_scatter(summed, "blk", scatter_dimension=0, tiled=True)
    return mine[None]


def solution(mesh):
    return jax.shard_map(
        shards,
        mesh=mesh,
        in_specs=(
            P("grp", "blk", None, None, None),
            P("grp", "blk", None),
            P("grp", "blk", None, None, None),
            P("grp", "blk", None),
        ),
        out_specs=P("grp", "blk", None, None),
        check_vma=False,
    )
```

profile of v0, /device:TPU:0, one launch (start us, length us, event | category | flops | bytes accessed | tf_op | source)
XLA Modules:
  0.0 995.9 jit_solution(11659109190072791211)
XLA Ops:
  11.2 57.8 %all-gather.2.cloned.1.call-done = bf16[1,96,2,96,96]{4,3,2,0,1:T(8,128)(2,1)} async-done(((bf16[1,24,2,96,96]{4,3,2,0,1:T(8,128)(2,1)}), bf16[1,96,2,96,96]{4,3,2,0,1:T(8,128)(2,1)}) %all-gather.2.cloned.1.call-update) | async-done | bytes 3538960 | tf_op jit(solution)/shard_map/all_gather | solution.py:22
  69.0 23.2 %gather_fusion = bf16[648,2,96,96]{3,2,1,0:T(8,128)(2,1)} fusion(bf16[96,2,96,96]{3,2,1,0:T(8,128)(2,1)} %bitcast.56, s32[1024]{0:T(1024)S(1)} %pad_clamp_fusion), kind=kCustom, calls=%fused_computation | custom fusion | bytes 47778336 | tf_op jit(solution)/shard_map/jit(_take)/gather | solution.py:25
  92.2 38.4 %copy.10 = bf16[24,27,2,96,96]{3,4,2,1,0:T(8,128)(2,1)} copy(bf16[24,27,2,96,96]{4,3,2,1,0:T(8,128)(2,1)} %bitcast.57) | data formatting | bytes 47775744 | tf_op jit(solution)/shard_map/jit(_take)/gather | solution.py:25
  130.6 22.1 %select_select_fusion = bf16[24,27,2,96,96]{3,4,2,1,0:T(8,128)(2,1)} fusion(bf16[24,27,2,96,96]{3,4,2,1,0:T(8,128)(2,1)} %copy.10, pred[24,27]{1,0:T(8,128)(4,1)S(1)} %compare_and_fusion, pred[24,27]{1,0:T(8,128)(4,1)S(1)} %and_bitcast_fusion), kind=kLoop, calls=%fused_computation.13 | loop fusion | flops 23887872 | bytes 47777040 | tf_op jit(solution)/shard_map/jit(_where)/select_n | solution.py:26
  156.2 658.8 %while.10 = (s32[]{:T(128)}, f32[128,96,96]{2,1,0:T(8,128)}, s32[6]{0:T(128)S(1)}, s32[24,108]{1,0:T(8,128)}, bf16[24,27,2,96,96]{3,4,2,1,0:T(8,128)(2,1)}, /*in...) while((s32[]{:T(128)}, f32[128,96,96]{2,1,0:T(8,128)}, ...), condition=%wide.region_2.3_spmd, body=%wide.region_0.2_spmd.sunk | while | flops 1152589824 | bytes 103721064 | solution.py:49
  157.4 11.6 %convolution_bitcast_fusion.2 = f32[4,2,27,2,96,96]{4,5,1,3,2,0:T(8,128)} fusion(bf16[24,27,2,96,96]{3,4,2,1,0:T(8,128)(2,1)} %get-tuple-element.126, s32[]{:T(128)S(6)} %select_n.41, bf16[24,27,96,96]{3,2,1,0:T(8,128)(2,1)} %get-tuple-element.127, bf16[24,2,96,96]{3,2,1,0:T(8,128)(2,1)S(1)} %get-tuple-element.128), kind=kOutput, calls=%fused_computation.2.clone.1 | convolution fusion | flops 1148608512 | bytes 24086016 | tf_op jit(solution)/shard_map/while/body/eval_jaxpr/rnab,rkmbc->rnkmac/dot_general | solution.py:41
  169.0 21.0 %copy.16 = f32[4,2,27,2,96,96]{5,4,3,2,1,0:T(8,128)} copy(f32[4,2,27,2,96,96]{4,5,1,3,2,0:T(8,128)} %convolution_bitcast_fusion.2) | data formatting | bytes 31850496 | tf_op jit(solution)/shard_map/while/body/eval_jaxpr/rnab,rkmbc->rnkmac/transpose | solution.py:41
  190.8 75.3 %scatter_fusion = f32[128,96,96]{2,1,0:T(8,128)} fusion(f32[128,96,96]{2,1,0:T(8,128)} %get-tuple-element.112, s32[432]{0:T(512)S(1)} %reshape.84, f32[432,96,96]{2,1,0:T(8,128)} %bitcast.55), kind=kCustom, calls=%fused_computation.1.clone.1 | custom fusion | flops 3981312 | bytes 47777472 | tf_op jit(solution)/shard_map/while/body/eval_jaxpr/scatter-add | solution.py:45
  267.2 11.6 %convolution_bitcast_fusion.2 = f32[4,2,27,2,96,96]{4,5,1,3,2,0:T(8,128)} fusion(bf16[24,27,2,96,96]{3,4,2,1,0:T(8,128)(2,1)} %get-tuple-element.126, s32[]{:T(128)S(6)} %select_n.41, bf16[24,27,96,96]{3,2,1,0:T(8,128)(2,1)} %get-tuple-element.127, bf16[24,2,96,96]{3,2,1,0:T(8,128)(2,1)S(1)} %get-tuple-element.128), kind=kOutput, calls=%fused_computation.2.clone.1 | convolution fusion | flops 1148608512 | bytes 24086016 | tf_op jit(solution)/shard_map/while/body/eval_jaxpr/rnab,rkmbc->rnkmac/dot_general | solution.py:41
  278.8 21.0 %copy.16 = f32[4,2,27,2,96,96]{5,4,3,2,1,0:T(8,128)} copy(f32[4,2,27,2,96,96]{4,5,1,3,2,0:T(8,128)} %convolution_bitcast_fusion.2) | data formatting | bytes 31850496 | tf_op jit(solution)/shard_map/while/body/eval_jaxpr/rnab,rkmbc->rnkmac/transpose | solution.py:41
  300.6 75.3 %scatter_fusion = f32[128,96,96]{2,1,0:T(8,128)} fusion(f32[128,96,96]{2,1,0:T(8,128)} %get-tuple-element.112, s32[432]{0:T(512)S(1)} %reshape.84, f32[432,96,96]{2,1,0:T(8,128)} %bitcast.55), kind=kCustom, calls=%fused_computation.1.clone.1 | custom fusion | flops 3981312 | bytes 47777472 | tf_op jit(solution)/shard_map/while/body/eval_jaxpr/scatter-add | solution.py:45
  377.0 11.6 %convolution_bitcast_fusion.2 = f32[4,2,27,2,96,96]{4,5,1,3,2,0:T(8,128)} fusion(bf16[24,27,2,96,96]{3,4,2,1,0:T(8,128)(2,1)} %get-tuple-element.126, s32[]{:T(128)S(6)} %select_n.41, bf16[24,27,96,96]{3,2,1,0:T(8,128)(2,1)} %get-tuple-element.127, bf16[24,2,96,96]{3,2,1,0:T(8,128)(2,1)S(1)} %get-tuple-element.128), kind=kOutput, calls=%fused_computation.2.clone.1 | convolution fusion | flops 1148608512 | bytes 24086016 | tf_op jit(solution)/shard_map/while/body/eval_jaxpr/rnab,rkmbc->rnkmac/dot_general | solution.py:41
  388.6 21.0 %copy.16 = f32[4,2,27,2,96,96]{5,4,3,2,1,0:T(8,128)} copy(f32[4,2,27,2,96,96]{4,5,1,3,2,0:T(8,128)} %convolution_bitcast_fusion.2) | data formatting | bytes 31850496 | tf_op jit(solution)/shard_map/while/body/eval_jaxpr/rnab,rkmbc->rnkmac/transpose | solution.py:41
  410.4 75.2 %scatter_fusion = f32[128,96,96]{2,1,0:T(8,128)} fusion(f32[128,96,96]{2,1,0:T(8,128)} %get-tuple-element.112, s32[432]{0:T(512)S(1)} %reshape.84, f32[432,96,96]{2,1,0:T(8,128)} %bitcast.55), kind=kCustom, calls=%fused_computation.1.clone.1 | custom fusion | flops 3981312 | bytes 47777472 | tf_op jit(solution)/shard_map/while/body/eval_jaxpr/scatter-add | solution.py:45
  486.7 11.6 %convolution_bitcast_fusion.2 = f32[4,2,27,2,96,96]{4,5,1,3,2,0:T(8,128)} fusion(bf16[24,27,2,96,96]{3,4,2,1,0:T(8,128)(2,1)} %get-tuple-element.126, s32[]{:T(128)S(6)} %select_n.41, bf16[24,27,96,96]{3,2,1,0:T(8,128)(2,1)} %get-tuple-element.127, bf16[24,2,96,96]{3,2,1,0:T(8,128)(2,1)S(1)} %get-tuple-element.128), kind=kOutput, calls=%fused_computation.2.clone.1 | convolution fusion | flops 1148608512 | bytes 24086016 | tf_op jit(solution)/shard_map/while/body/eval_jaxpr/rnab,rkmbc->rnkmac/dot_general | solution.py:41
  498.4 21.0 %copy.16 = f32[4,2,27,2,96,96]{5,4,3,2,1,0:T(8,128)} copy(f32[4,2,27,2,96,96]{4,5,1,3,2,0:T(8,128)} %convolution_bitcast_fusion.2) | data formatting | bytes 31850496 | tf_op jit(solution)/shard_map/while/body/eval_jaxpr/rnab,rkmbc->rnkmac/transpose | solution.py:41
  520.1 75.3 %scatter_fusion = f32[128,96,96]{2,1,0:T(8,128)} fusion(f32[128,96,96]{2,1,0:T(8,128)} %get-tuple-element.112, s32[432]{0:T(512)S(1)} %reshape.84, f32[432,96,96]{2,1,0:T(8,128)} %bitcast.55), kind=kCustom, calls=%fused_computation.1.clone.1 | custom fusion | flops 3981312 | bytes 47777472 | tf_op jit(solution)/shard_map/while/body/eval_jaxpr/scatter-add | solution.py:45
  596.6 11.6 %convolution_bitcast_fusion.2 = f32[4,2,27,2,96,96]{4,5,1,3,2,0:T(8,128)} fusion(bf16[24,27,2,96,96]{3,4,2,1,0:T(8,128)(2,1)} %get-tuple-element.126, s32[]{:T(128)S(6)} %select_n.41, bf16[24,27,96,96]{3,2,1,0:T(8,128)(2,1)} %get-tuple-element.127, bf16[24,2,96,96]{3,2,1,0:T(8,128)(2,1)S(1)} %get-tuple-element.128), kind=kOutput, calls=%fused_computation.2.clone.1 | convolution fusion | flops 1148608512 | bytes 24086016 | tf_op jit(solution)/shard_map/while/body/eval_jaxpr/rnab,rkmbc->rnkmac/dot_general | solution.py:41
  608.2 21.0 %copy.16 = f32[4,2,27,2,96,96]{5,4,3,2,1,0:T(8,128)} copy(f32[4,2,27,2,96,96]{4,5,1,3,2,0:T(8,128)} %convolution_bitcast_fusion.2) | data formatting | bytes 31850496 | tf_op jit(solution)/shard_map/while/body/eval_jaxpr/rnab,rkmbc->rnkmac/transpose | solution.py:41
  630.0 75.2 %scatter_fusion = f32[128,96,96]{2,1,0:T(8,128)} fusion(f32[128,96,96]{2,1,0:T(8,128)} %get-tuple-element.112, s32[432]{0:T(512)S(1)} %reshape.84, f32[432,96,96]{2,1,0:T(8,128)} %bitcast.55), kind=kCustom, calls=%fused_computation.1.clone.1 | custom fusion | flops 3981312 | bytes 47777472 | tf_op jit(solution)/shard_map/while/body/eval_jaxpr/scatter-add | solution.py:45
  717.9 21.0 %copy.16 = f32[4,2,27,2,96,96]{5,4,3,2,1,0:T(8,128)} copy(f32[4,2,27,2,96,96]{4,5,1,3,2,0:T(8,128)} %convolution_bitcast_fusion.2) | data formatting | bytes 31850496 | tf_op jit(solution)/shard_map/while/body/eval_jaxpr/rnab,rkmbc->rnkmac/transpose | solution.py:41
  739.7 75.3 %scatter_fusion = f32[128,96,96]{2,1,0:T(8,128)} fusion(f32[128,96,96]{2,1,0:T(8,128)} %get-tuple-element.112, s32[432]{0:T(512)S(1)} %reshape.84, f32[432,96,96]{2,1,0:T(8,128)} %bitcast.55), kind=kCustom, calls=%fused_computation.1.clone.1 | custom fusion | flops 3981312 | bytes 47777472 | tf_op jit(solution)/shard_map/while/body/eval_jaxpr/scatter-add | solution.py:45
  815.0 145.5 %all_to_all.5 = f32[8,16,96,96]{3,2,1,0:T(8,128)} all-to-all(f32[8,16,96,96]{3,2,1,0:T(8,128)} %bitcast.54), channel_id=1, replica_groups=mesh['blk'=4,'grp'=8] {'grp'}, dimensions={0} | all-to-all | bytes 9437184 | tf_op jit(solution)/shard_map/all_to_all | solution.py:51
  965.0 24.0 %reduce-scatter.2.cloned.1.call-done = f32[4,96,96]{2,1,0:T(8,128)} async-done(((f32[16,96,96]{2,1,0:T(8,128)}), f32[4,96,96]{2,1,0:T(8,128)}) %reduce-scatter.2.cloned.1.call-update) | async-done | bytes 147472 | tf_op jit(solution)/shard_map/reduce_scatter | solution.py:53
  (32 shorter events, 32.4 us)
Async XLA Ops:
  6.5 62.5 %all-gather.2.cloned.1.call-start = ((), (), s32[]{:S(2)}) async-start(), calls=%async_computation.2 | async-start | bytes 5898240 | tf_op jit(solution)/shard_map/all_gather | solution.py:22
  7.3 981.8 %reduce-scatter.2.cloned.1.call-start = ((), (), s32[]{:S(2)}) async-start(), calls=%async_computation.3 | async-start | bytes 983040 | tf_op jit(solution)/shard_map/reduce_scatter | solution.py:53
Sparse Core Ops, SparseCore 0:
  9.2 59.7 all-gather.1
  965.1 23.8 reduce-scatter.1
where the time goes:
time: 1000 us; the launch traced here: 996 us
  other arithmetic  480 us (48%)
  local copies, waits for them, and re-layouts  201 us (20%)
  blocking collectives  146 us (15%)
  waiting for transfers between devices  82.5 us (8%)
  matrix products  69.6 us (7%)
  between operations  13.4 us (1%)
    scatter-add x6, other arithmetic, one_block(): jax.ops.segment_sum(partial_value, t_part.reshape(-1), num_segments=slots)  452 us
    all_to_all x1, blocking collectives, shards(): lax.all_to_all(buffer, 'grp', split_axis=0, concat_axis=0, tiled=True)  146 us
    transpose x6, local copies, waits for them, and re-layouts, one_block(): jnp.einsum('rnab,rkmbc->rnkmac', p_part, product, preferred_element_type=...  126 us
    dot_general x6, matrix products, one_block(): jnp.einsum('rnab,rkmbc->rnkmac', p_part, product, preferred_element_type=...  69.6 us
    gather x2, local copies, waits for them, and re-layouts, shards(): taken = jnp.take(piece[0], jnp.clip(columns, 0, count - 1), axis=0)  61.6 us
    all_gather x1, waiting for transfers between devices, shards(): piece = lax.all_gather(prolong, 'blk', axis=1, tiled=True)  57.8 us
    reduce_scatter x1, waiting for transfers between devices, shards(): mine = lax.psum_scatter(summed, 'blk', scatter_dimension=0, tiled=True)  24 us
    select_n x1, other arithmetic, shards(): chosen = jnp.where(inside[:, :, None, None, None], taken, init)  22.1 us
  transfers between devices with their start and end apart: 2, of which 2 were waited for; matrix products, arithmetic and copies ran while one was open for 0% of the time, Pallas kernels for 0%

commit v1 on v0

v1 whole, which is shorter than its diff:
```python
import functools

import jax
import jax.numpy as jnp
from jax import lax
from jax.experimental import pallas as pl
from jax.experimental.pallas import tpu as pltpu
from jax.sharding import PartitionSpec as P

OWN = 4
UNROLL = 8
RING = 3
LANES = 128
VMEM_LIMIT = 56 * 1024 * 1024


def pack_four(blocks, width):
    strip = LANES - width
    return [
        jnp.concatenate(
            [blocks[t][:, :width], blocks[3][:, strip * t : strip * (t + 1)]], axis=1
        )
        for t in range(3)
    ]


def unpack_last(parts, width):
    return jnp.concatenate([part[:, width:] for part in parts], axis=1)


def pack_kernel(p_ref, out_ref):
    width = p_ref.shape[-1]
    for quad in range(p_ref.shape[0]):
        packed = pack_four([p_ref[quad, t] for t in range(4)], width)
        for t in range(3):
            out_ref[quad, t] = packed[t]


def pack_prolong(prolong):
    width = prolong.shape[-1]
    quads = prolong.shape[1] * prolong.shape[2] // 4
    step = 3
    return pl.pallas_call(
        pack_kernel,
        grid=(quads // step,),
        in_specs=[pl.BlockSpec((step, 4, width, width), lambda g: (g, 0, 0, 0))],
        out_specs=pl.BlockSpec((step, 3, width, LANES), lambda g: (g, 0, 0, 0)),
        out_shape=jax.ShapeDtypeStruct((quads, 3, width, LANES), prolong.dtype),
        name="pack_prolong",
    )(prolong.reshape(quads, 4, width, width))


def work_kernel(cfg, *refs):
    first, last, phase, sources, naccs = (
        cfg["first"], cfg["last"], cfg["phase"], cfg["sources"], cfg["naccs"],
    )
    width, rows, nonzeros, per_row = cfg["width"], cfg["rows"], cfg["nonzeros"], cfg["per_row"]
    slots, members, groups = cfg["slots"], cfg["members"], cfg["groups"]
    quads = rows * per_row // 4
    refs = list(refs)
    take = lambda n: [refs.pop(0) for _ in range(n)]
    list_ref, col_ref, tgt_ref, info_ref = take(4)
    (a_hbm,) = take(1)
    p_hbm = take(sources)
    if not first:
        pt_hbm, acc_in = take(2)
    if last:
        out_refs = take(members)
    else:
        (acc_out,) = take(1)
        if first:
            (pt_out,) = take(1)
    p_vmem, pt, a_buf = take(3)
    accs = take(naccs)
    aps = take(UNROLL)
    a_sem, sem = take(2)

    base = phase * cfg["list_len"]
    turns = info_ref[phase]

    def a_copies(group, slot):
        copies = []
        for u in range(UNROLL):
            v = list_ref[base + group * UNROLL + u]
            i = jnp.minimum(v >> 5, rows - 1)
            copies.append(
                pltpu.make_async_copy(a_hbm.at[i, v & 31], a_buf.at[slot, u], a_sem.at[slot, u])
            )
        return copies

    def start(group, slot):
        for copy in a_copies(group, slot):
            copy.start()

    def wait(slot):
        for u in range(UNROLL):
            pltpu.make_async_copy(a_hbm.at[0, 0], a_buf.at[slot, u], a_sem.at[slot, u]).wait()

    copies = [
        pltpu.make_async_copy(
            p_hbm[s], p_vmem.at[pl.ds(s * quads, quads), pl.ds(0, 3)], sem.at[s]
        )
        for s in range(sources)
    ]
    if not first:
        copies.append(pltpu.make_async_copy(pt_hbm, pt.at[pl.ds(0, rows)], sem.at[sources]))
        copies.append(
            pltpu.make_async_copy(acc_in, accs[0].at[pl.ds(0, slots)], sem.at[sources + 1])
        )
    for copy in copies:
        copy.start()
    for group in range(1, RING):
        start(group, group)

    def clear(s, _):
        for acc in accs if first else accs[1:]:
            acc[s] = jnp.zeros_like(acc[s])
        return 0

    lax.fori_loop(0, slots, clear, 0)
    for copy in copies[: sources]:
        copy.wait()

    def unpack(q, _):
        fourth = unpack_last([p_vmem[q, t] for t in range(3)], width)
        p_vmem[q, 3, :, :width] = fourth
        return 0

    lax.fori_loop(0, sources * quads, unpack, 0)

    if first:

        def transpose(i, _):
            for n in range(per_row):
                block = p_vmem[i // 2, (i % 2) * 2 + n].astype(jnp.float32)
                pt[i, n * width : (n + 1) * width, :] = block.T[:width].astype(jnp.bfloat16)
            return 0

        lax.fori_loop(0, rows, transpose, 0)
    for copy in copies[sources:]:
        copy.wait()

    def turn(g, ring):
        nxt = jnp.where(ring == RING - 1, 0, ring + 1)
        start(g + RING, ring)
        wait(nxt)
        for u in range(UNROLL):
            v = list_ref[base + g * UNROLL + u]
            i = v >> 5
            t = i * (nonzeros * per_row * per_row) + (v & 31) * per_row
            result = jnp.dot(pt[i], aps[u][...], preferred_element_type=jnp.float32)
            for n in range(per_row):
                for m in range(per_row):
                    acc = accs[m % naccs]
                    s = tgt_ref[t + n * nonzeros * per_row + m]
                    acc[s] = acc[s] + result[
                        n * width : (n + 1) * width, m * LANES : (m + 1) * LANES
                    ]
            v = list_ref[base + (g + 1) * UNROLL + u]
            j = col_ref[(v >> 5) * nonzeros + (v & 31)]
            right = jnp.concatenate(
                [p_vmem[j >> 1, (j & 1) * 2 + m] for m in range(per_row)], axis=1
            )
            aps[u][...] = jnp.dot(
                a_buf[nxt, u], right, preferred_element_type=jnp.float32
            ).astype(jnp.bfloat16)
        return nxt

    ring = lax.fori_loop(0, turns + 1, turn, jnp.int32(0))
    for _ in range(RING - 1):
        ring = jnp.where(ring == RING - 1, 0, ring + 1)
        wait(ring)

    def total(s):
        value = accs[0][s]
        for acc in accs[1:]:
            value = value + acc[s]
        return value

    if last:
        me = info_ref[cfg["phases"]]

        def emit(q, _):
            for r in range(members):
                s = q * (OWN * members) + (me ^ r) * OWN
                packed = pack_four([total(s + x) for x in range(OWN)], width)
                for t in range(3):
                    out_refs[r][q, t] = packed[t].astype(out_refs[r].dtype)
            return 0

        lax.fori_loop(0, groups, emit, 0)
    else:
        if naccs > 1:

            def fold(s, _):
                accs[0][s] = total(s)
                return 0

            lax.fori_loop(0, slots, fold, 0)
        outs = [pltpu.make_async_copy(accs[0].at[pl.ds(0, slots)], acc_out, sem.at[0])]
        if first:
            outs.append(pltpu.make_async_copy(pt.at[pl.ds(0, rows)], pt_out, sem.at[1]))
        for copy in outs:
            copy.start()
        for copy in outs:
            copy.wait()


def work(cfg, tables, a_rows, packed, pt=None, acc=None):
    width, rows, per_row = cfg["width"], cfg["rows"], cfg["per_row"]
    slots, members, groups = cfg["slots"], cfg["members"], cfg["groups"]
    sources = len(packed)
    cfg = dict(cfg, sources=sources, naccs=2 if slots <= 256 else 1)
    quads = rows * per_row // 4
    hbm = pl.BlockSpec(memory_space=pl.ANY)
    vmem = pl.BlockSpec(memory_space=pltpu.VMEM)
    operands = [a_rows, *packed] + ([] if cfg["first"] else [pt, acc])
    if cfg["last"]:
        shapes = [
            jax.ShapeDtypeStruct((groups, 3, width, LANES), jnp.bfloat16 if r else jnp.float32)
            for r in range(members)
        ]
        out_specs = [vmem] * members
    else:
        shapes = [jax.ShapeDtypeStruct((slots, width, LANES), jnp.float32)]
        if cfg["first"]:
            shapes.append(jax.ShapeDtypeStruct((rows, per_row * width, width), jnp.bfloat16))
        out_specs = [hbm] * len(shapes)
    flops = 2 * rows * cfg["nonzeros"] * 3 * width * width * 2 * width // 3
    return pl.pallas_call(
        functools.partial(work_kernel, cfg),
        grid_spec=pltpu.PrefetchScalarGridSpec(
            num_scalar_prefetch=4,
            grid=(),
            in_specs=[hbm] * len(operands),
            out_specs=out_specs,
            scratch_shapes=[
                pltpu.VMEM((sources * quads, 4, width, LANES), jnp.bfloat16),
                pltpu.VMEM((rows + 1, per_row * width, width), jnp.bfloat16),
                pltpu.VMEM((RING, UNROLL, width, width), jnp.bfloat16),
            ]
            + [pltpu.VMEM((slots + 1, width, LANES), jnp.float32)] * cfg["naccs"]
            + [pltpu.VMEM((width, per_row * LANES), jnp.bfloat16)] * UNROLL
            + [
                pltpu.SemaphoreType.DMA((RING, UNROLL)),
                pltpu.SemaphoreType.DMA((sources + 2,)),
            ],
        ),
        out_shape=shapes,
        compiler_params=pltpu.CompilerParams(vmem_limit_bytes=VMEM_LIMIT),
        cost_estimate=pl.CostEstimate(
            flops=flops, bytes_accessed=20_000_000, transcendentals=0
        ),
        name="work_%d" % cfg["phase"],
    )(*tables, *operands)


def make_tables(columns, targets, me, phase_of, place_of, slots):
    rows, nonzeros = columns.shape
    entries = rows * nonzeros
    phases = max(phase_of) + 1
    list_len = (-(-entries // UNROLL) + RING + 1) * UNROLL
    relative = (columns // rows) ^ me
    phase = sum(jnp.where(relative == r, p, 0) for r, p in enumerate(phase_of))
    place = sum(jnp.where(relative == r, p, 0) for r, p in enumerate(place_of))
    col_table = jnp.pad((place * rows + columns % rows).reshape(-1), (0, nonzeros))
    tgt_table = jnp.pad(
        targets.reshape(-1), (0, targets.shape[1]), constant_values=slots
    )
    flat = phase.reshape(-1)
    order = jnp.arange(entries, dtype=jnp.int32)
    before = (flat[None, :] == flat[:, None]) & (order[None, :] < order[:, None])
    position = flat * list_len + UNROLL + jnp.sum(before.astype(jnp.int32), axis=1)
    counts = jnp.stack([jnp.sum((flat == p).astype(jnp.int32)) for p in range(phases)])
    value = (order // nonzeros) * 32 + order % nonzeros
    dummy = rows * 32
    x = jnp.arange(phases * list_len, dtype=jnp.int32)
    lists = dummy + jnp.sum(
        jnp.where(position[None, :] == x[:, None], value[None, :] - dummy, 0), axis=1
    )
    info = jnp.concatenate([-(-counts // UNROLL), me[None]])
    return (lists.astype(jnp.int32), col_table, tgt_table, info.astype(jnp.int32)), list_len


def shards(a_blocks, col_index, prolong, target):
    rows, nonzeros = a_blocks.shape[1:3]
    per_row = prolong.shape[2]
    width = a_blocks.shape[-1]
    groups = lax.axis_size("grp")
    members = lax.axis_size("blk")
    slots = groups * OWN * members
    me = lax.axis_index("blk").astype(jnp.int32)

    if members == 4:
        phase_of, place_of = [0, 1, 1, 2], [0, 0, 1, 0]
    else:
        phase_of, place_of = [0] + [1] * (members - 1), [0] + list(range(members - 1))
    phases = max(phase_of) + 1

    def exchange(x, r, axis="blk", size=members):
        return lax.ppermute(x, axis, [(d, d ^ r) for d in range(size)])

    own = pack_prolong(prolong)
    packed = [own]
    if members == 4:
        near = [exchange(own, 1), exchange(own, 2)]
        half = own.shape[0] // 2
        far = jnp.concatenate([exchange(near[0][:half], 2), exchange(near[1][half:], 1)])
        packed = [[own], near, [far]]
    else:
        packed = [[own], [exchange(own, r) for r in range(1, members)]]

    tables, list_len = make_tables(col_index[0], target[0], me, phase_of, place_of, slots)
    cfg = dict(
        width=width, rows=rows, nonzeros=nonzeros, per_row=per_row, slots=slots,
        members=members, groups=groups, phases=phases, list_len=list_len,
    )
    a_rows = a_blocks[0]
    pt = acc = None
    for p in range(phases):
        outs = work(
            dict(cfg, phase=p, first=p == 0, last=p == phases - 1),
            tables, a_rows, packed[p], pt, acc,
        )
        if p == 0:
            acc, pt = outs
        elif p < phases - 1:
            (acc,) = outs
    total = outs[0]
    for r in range(1, members):
        total = total + exchange(outs[r], r).astype(jnp.float32)

    rank = lax.axis_index("grp")
    core, chip = rank % 2, rank // 2
    chips = groups // 2
    total = total.reshape(chips, 2, 3, width, LANES)
    give = lax.dynamic_index_in_dim(total, 1 - core, 1, keepdims=False)
    keep = lax.dynamic_index_in_dim(total, core, 1, keepdims=False)
    total = keep + exchange(give, 1, "grp", groups)
    mine = lax.dynamic_index_in_dim(total, chip, 0, keepdims=False)
    for r in range(1, chips):
        part = lax.dynamic_index_in_dim(total, chip ^ r, 0, keepdims=False)
        got = exchange(part.astype(jnp.bfloat16), 2 * r, "grp", groups)
        mine = mine + got.astype(jnp.float32)
    fourth = unpack_last([mine[t] for t in range(3)], width)
    return jnp.concatenate([mine[:, :, :width], fourth[None]])[None]


def solution(mesh):
    return jax.shard_map(
        shards,
        mesh=mesh,
        in_specs=(
            P("grp", "blk", None, None, None),
            P("grp", "blk", None),
            P("grp", "blk", None, None, None),
            P("grp", "blk", None),
        ),
        out_specs=P("grp", "blk", None, None),
        check_vma=False,
    )
```

time: 1000 us -> 150 us (0.15)
  other arithmetic: 480 us -> 8.53 us
  local copies, waits for them, and re-layouts: 201 us -> 2.68 us
  blocking collectives: 146 us -> 0 us
  Pallas kernels: 0 us -> 75.8 us
  matrix products: 69.6 us -> 0 us
  waiting for transfers between devices: 82.5 us -> 45 us
  starting transfers between devices: 0.04 us -> 15.9 us
  between operations: 13.4 us -> 0.21 us
    scatter-add x6 -> x0, other arithmetic: 452 us -> none  [one_block(): jax.ops.segment_sum(partial_value, t_part.reshape(-1), num_segments=slots)]
    all_to_all x1 -> x0, blocking collectives: 146 us -> none  [shards(): lax.all_to_all(buffer, 'grp', split_axis=0, concat_axis=0, tiled=True)]
    transpose x6 -> x0, local copies, waits for them, and re-layouts: 126 us -> none  [one_block(): jnp.einsum('rnab,rkmbc->rnkmac', p_part, product, preferred_element_type=...]
    pallas_call x0 -> x4, Pallas kernels: none -> 75.8 us  [the longest x3 72.2 us: work(): pl.pallas_call(functools.partial(work_kernel, cfg), grid_spec=pltpu.Prefe...]
    dot_general x6 -> x0, matrix products: 69.6 us -> none  [one_block(): jnp.einsum('rnab,rkmbc->rnkmac', p_part, product, preferred_element_type=...]
    gather x2 -> x0, local copies, waits for them, and re-layouts: 61.6 us -> none  [shards(): taken = jnp.take(piece[0], jnp.clip(columns, 0, count - 1), axis=0)]
    all_gather x1 -> x0, waiting for transfers between devices: 57.8 us -> none  [shards(): piece = lax.all_gather(prolong, 'blk', axis=1, tiled=True)]
    ppermute x0 -> x11, waiting for transfers between devices: none -> 45 us  [exchange(): return lax.ppermute(x, axis, [(d, d ^ r) for d in range(size)])]
  transfers between devices with their start and end apart: 2 -> 11, of which waited for: 2 -> 7; matrix products, arithmetic and copies ran while one was open for 0% -> 5% of each run, Pallas kernels for 0% -> 35%
where the time goes in v1:
time: 150 us; the launch traced here: 148 us
  Pallas kernels  75.8 us (51%)
  waiting for transfers between devices  45 us (30%)
  starting transfers between devices  15.9 us (11%)
  other arithmetic  8.53 us (6%)
  local copies, waits for them, and re-layouts  2.68 us (2%)
    pallas_call x3, Pallas kernels, work(): pl.pallas_call(functools.partial(work_kernel, cfg), grid_spec=pltpu.Prefe...  72.2 us
    ppermute x11, waiting for transfers between devices, exchange(): return lax.ppermute(x, axis, [(d, d ^ r) for d in range(size)])  45 us
    ppermute x11, starting transfers between devices, exchange(): return lax.ppermute(x, axis, [(d, d ^ r) for d in range(size)])  15.9 us
    pallas_call x1, Pallas kernels, pack_prolong(): pl.pallas_call(pack_kernel, grid=(quads // step,), in_specs=[pl.BlockSpec...  3.58 us
  transfers between devices with their start and end apart: 11, of which 7 were waited for; matrix products, arithmetic and copies ran while one was open for 5% of the time, Pallas kernels for 35%

profile of v1, /device:TPU:0, one launch (start us, length us, event | category | flops | bytes accessed | tf_op | source)
XLA Modules:
  0.0 148.2 jit_solution(4826736300441939682)
XLA Ops:
  0.0 3.6 %pack_prolong.1.refs_5_ = bf16[12,3,96,128]{3,2,1,0:T(8,128)(2,1)} custom-call(bf16[12,4,96,96]{3,2,1,0:T(8,128)(2,1)} %bitcast.40), custom_call_target="tpu_custom_call" | custom-call | tf_op jit(solution)/shard_map/pack_prolong/pallas_call | solution.py:43
  3.6 2.9 %collective-permute-start = (bf16[12,3,96,128]{3,2,1,0:T(8,128)(2,1)}, bf16[12,3,96,128]{3,2,1,0:T(8,128)(2,1)S(1)}, u32[]{:S(2)}, u32[]{:S(2)}) collective-permute-start(bf16[12,3,96,128]{3,2,1,0:T(8,128)(2,1)} %pack_prolong.1.refs_5_), channel_id=1, source_target_pairs={{0,8},{8,0},{16,24},{24,16},{1,9},{9,1},{17,25},{25,17},{2,10},{10... | collective-permute-start | bytes 2654216 | tf_op jit(solution)/shard_map/ppermute | solution.py:301
  6.5 1.5 %collective-permute-start.2 = (bf16[12,3,96,128]{3,2,1,0:T(8,128)(2,1)}, bf16[12,3,96,128]{3,2,1,0:T(8,128)(2,1)S(1)}, u32[]{:S(2)}, u32[]{:S(2)}) collective-permute-start(bf16[12,3,96,128]{3,2,1,0:T(8,128)(2,1)} %pack_prolong.1.refs_5_), channel_id=1, source_target_pairs={{0,16},{8,24},{16,0},{24,8},{1,17},{9,25},{17,1},{25,9},{2,18},{10... | collective-permute-start | bytes 2654216 | tf_op jit(solution)/shard_map/ppermute | solution.py:301
  8.4 0.8 convert_reduce_fusion.3
  9.1 2.0 %fusion.21 = s32[3]{0:T(128)S(1)} fusion(s32[1]{0:T(128)} %bitcast.2, s32[1]{0:T(128)} %bitcast.1, s32[1]{0:T(128)} %bitcast), kind=kLoop, calls=%fused_computation.63 | loop fusion | flops 54 | bytes 24 | tf_op jit(solution)/shard_map/neg | solution.py:281
  12.8 13.6 %collective-permute-done.refs_5_ = bf16[12,3,96,128]{3,2,1,0:T(8,128)(2,1)S(1)} collective-permute-done((bf16[12,3,96,128]{3,2,1,0:T(8,128)(2,1)}, bf16[12,3,96,128]{3,2,1,0:T(8,128)(2,1)S(1)}, u32[]{:S(2)}, u32[]{:S(2)}) %collective-permute-start) | collective-permute-done | bytes 884768 | tf_op jit(solution)/shard_map/ppermute | solution.py:301
  26.4 1.8 %collective-permute-start.1 = (bf16[6,3,96,128]{3,2,1,0:T(8,128)(2,1)S(1)}, bf16[6,3,96,128]{3,2,1,0:T(8,128)(2,1)S(1)}, u32[]{:S(2)}, u32[]{:S(2)}) collective-permute-start(bf16[6,3,96,128]{3,2,1,0:T(8,128)(2,1)S(1)} %slice.36), channel_id=1, source_target_pairs={{0,16},{8,24},{16,0},{24,8},{1,17},{9,25},{17,1},{25,9},{2,18},{10... | collective-permute-start | bytes 1327112 | tf_op jit(solution)/shard_map/ppermute | solution.py:301
  28.3 1.6 %collective-permute-start.3 = (bf16[6,3,96,128]{3,2,1,0:T(8,128)(2,1)S(1)}, bf16[6,3,96,128]{3,2,1,0:T(8,128)(2,1)S(1)}, u32[]{:S(2)}, u32[]{:S(2)}) collective-permute-start(bf16[6,3,96,128]{3,2,1,0:T(8,128)(2,1)S(1)} %slice.37), channel_id=1, source_target_pairs={{0,8},{8,0},{16,24},{24,16},{1,9},{9,1},{17,25},{25,17},{2,10},{10... | collective-permute-start | bytes 1327112 | tf_op jit(solution)/shard_map/ppermute | solution.py:301
  30.5 0.8 reshape_squeeze.3
  32.5 30.2 %work_0.1 = (f32[128,96,128]{2,1,0:T(8,128)}, bf16[24,192,96]{2,1,0:T(8,128)(2,1)}) custom-call(s32[2040]{0:T(1024)} %broadcast_add_fusion.refs_0_, s32[675]{0:T(1024)} %pad.8.refs_1_, s32[2700]{0:T(1024)} %pad.9.refs_2_, s32[4]{0:T(128)} %pad_add_fusion.1.refs_3_, bf16[24,27,96,96]{3,2,1,0:T(8,128)(2,1)} %bitcast.34, ...), custom_call_target="tpu_custom_call" | custom-call | flops 2293235712 | bytes 20000000 | tf_op jit(solution)/shard_map/work_0/pallas_call | solution.py:230
  62.7 22.3 %work_1.1.refs_7_ = f32[128,96,128]{2,1,0:T(8,128)} custom-call(s32[2040]{0:T(1024)} %broadcast_add_fusion.refs_0_, s32[675]{0:T(1024)} %pad.8.refs_1_, s32[2700]{0:T(1024)} %pad.9.refs_2_, s32[4]{0:T(128)} %pad_add_fusion.1.refs_3_, bf16[24,27,96,96]{3,2,1,0:T(8,128)(2,1)} %bitcast.35, bf16[12,3,96,128]{3,2,1,0:T(8,128)(2,1)} %copy-done, ...), custom_call_target="tpu_custom_call" | custom-call | flops 2293235712 | bytes 20000000 | tf_op jit(solution)/shard_map/work_1/pallas_call | solution.py:230
  85.1 1.0 pad_maximum_fusion.refs_5_
  86.1 19.7 %work_2.1 = (f32[8,3,96,128]{3,2,1,0:T(8,128)}, bf16[8,3,96,128]{3,2,1,0:T(8,128)(2,1)}, bf16[8,3,96,128]{3,2,1,0:T(8,128)(2,1)}, bf16[8,3,96,128]{3,2,1,0:T(8,128)(2,1)}) custom-call(s32[2040]{0:T(1024)} %broadcast_add_fusion.refs_0_, s32[675]{0:T(1024)} %pad.8.refs_1_, s32[2700]{0:T(1024)} %pad.9.refs_2_, s32[4]{0:T(128)} %pad_add_fusion.1.refs_3_, ...), custom_call_target="tpu_custom_call" | custom-call | flops 2293235712 | bytes 20000000 | tf_op jit(solution)/shard_map/work_2/pallas_call | solution.py:230
  106.4 1.1 collective-permute-start.5
  107.6 1.8 %collective-permute-start.6 = (bf16[8,3,96,128]{3,2,1,0:T(8,128)(2,1)}, bf16[8,3,96,128]{3,2,1,0:T(8,128)(2,1)S(1)}, u32[]{:S(2)}, u32[]{:S(2)}) collective-permute-start(bf16[8,3,96,128]{3,2,1,0:T(8,128)(2,1)} %get-tuple-element.16), channel_id=1, source_target_pairs={{0,24},{8,16},{16,8},{24,0},{1,25},{9,17},{17,9},{25,1},{2,26},{10... | collective-permute-start | bytes 1769480 | tf_op jit(solution)/shard_map/ppermute | solution.py:301
  109.4 13.0 %collective-permute-done.4 = bf16[8,3,96,128]{3,2,1,0:T(8,128)(2,1)S(1)} collective-permute-done((bf16[8,3,96,128]{3,2,1,0:T(8,128)(2,1)}, bf16[8,3,96,128]{3,2,1,0:T(8,128)(2,1)S(1)}, u32[]{:S(2)}, u32[]{:S(2)}) %collective-permute-start.4) | collective-permute-done | bytes 589856 | tf_op jit(solution)/shard_map/ppermute | solution.py:301
  122.4 10.3 %collective-permute-done.5 = bf16[8,3,96,128]{3,2,1,0:T(8,128)(2,1)S(1)} collective-permute-done((bf16[8,3,96,128]{3,2,1,0:T(8,128)(2,1)}, bf16[8,3,96,128]{3,2,1,0:T(8,128)(2,1)S(1)}, u32[]{:S(2)}, u32[]{:S(2)}) %collective-permute-start.5) | collective-permute-done | bytes 589856 | tf_op jit(solution)/shard_map/ppermute | solution.py:301
  132.6 1.5 %convert_add_fusion = f32[8,3,96,128]{3,2,1,0:T(8,128)S(1)} fusion(bf16[8,3,96,128]{3,2,1,0:T(8,128)(2,1)S(1)} %collective-permute-done.6, bf16[8,3,96,128]{3,2,1,0:T(8,128)(2,1)S(1)} %collective-permute-done.5, f32[8,3,96,128]{3,2,1,0:T(8,128)} %get-tuple-element.13, bf16[8,3,96,128]{3,2,1,0:T(8,128)(2,1)S(1)} %collective-permute-done.4), kind=kLoop, calls=%fused_computation.5 | loop fusion | flops 1769472 | bytes 4128768 | tf_op jit(solution)/shard_map/add | solution.py:331
  134.4 2.0 %collective-permute-done.7 = f32[4,3,96,128]{3,2,1,0:T(8,128)S(1)} collective-permute-done((f32[4,3,96,128]{3,2,1,0:T(8,128)S(1)}, f32[4,3,96,128]{3,2,1,0:T(8,128)S(1)}, u32[]{:S(2)}, u32[]{:S(2)}) %collective-permute-start.7) | collective-permute-done | bytes 589856 | tf_op jit(solution)/shard_map/ppermute | solution.py:301
  136.4 3.7 %collective-permute-start.10 = (bf16[3,96,128]{2,1,0:T(8,128)(2,1)S(1)}, bf16[3,96,128]{2,1,0:T(8,128)(2,1)S(1)}, u32[]{:S(2)}, u32[]{:S(2)}) collective-permute-start(bf16[3,96,128]{2,1,0:T(8,128)(2,1)S(1)} %get-tuple-element.23), channel_id=1, source_target_pairs={{0,6},{1,7},{2,4},{3,5},{4,2},{5,3},{6,0},{7,1},{8,14},{9,15},{10,... | collective-permute-start | bytes 221192 | tf_op jit(solution)/shard_map/ppermute | solution.py:301
  140.1 0.8 collective-permute-start.9
  140.9 2.5 %collective-permute-done.10 = bf16[3,96,128]{2,1,0:T(8,128)(2,1)S(1)} collective-permute-done((bf16[3,96,128]{2,1,0:T(8,128)(2,1)S(1)}, bf16[3,96,128]{2,1,0:T(8,128)(2,1)S(1)}, u32[]{:S(2)}, u32[]{:S(2)}) %collective-permute-start.10) | collective-permute-done | bytes 73760 | tf_op jit(solution)/shard_map/ppermute | solution.py:301
  143.4 2.0 %collective-permute-done.8 = bf16[3,96,128]{2,1,0:T(8,128)(2,1)S(1)} collective-permute-done((bf16[3,96,128]{2,1,0:T(8,128)(2,1)S(1)}, bf16[3,96,128]{2,1,0:T(8,128)(2,1)S(1)}, u32[]{:S(2)}, u32[]{:S(2)}) %collective-permute-start.8) | collective-permute-done | bytes 73760 | tf_op jit(solution)/shard_map/ppermute | solution.py:301
  145.4 1.7 %collective-permute-done.9 = bf16[3,96,128]{2,1,0:T(8,128)(2,1)S(1)} collective-permute-done((bf16[3,96,128]{2,1,0:T(8,128)(2,1)S(1)}, bf16[3,96,128]{2,1,0:T(8,128)(2,1)S(1)}, u32[]{:S(2)}, u32[]{:S(2)}) %collective-permute-start.9) | collective-permute-done | bytes 73760 | tf_op jit(solution)/shard_map/ppermute | solution.py:301
  (37 shorter events, 5.8 us)
Async XLA Ops:
  0.0 8.0 %copy-start.2 = (s32[1,24,27]{2,1,0:T(8,128)S(1)}, s32[1,24,27]{2,1,0:T(8,128)}, u32[]{:S(2)}) copy-start(s32[1,24,27]{2,1,0:T(8,128)} %param.5) | copy-start | bytes 7780
  3.6 22.8 %collective-permute-start = (bf16[12,3,96,128]{3,2,1,0:T(8,128)(2,1)}, bf16[12,3,96,128]{3,2,1,0:T(8,128)(2,1)S(1)}, u32[]{:S(2)}, u32[]{:S(2)}) collective-permute-start(bf16[12,3,96,128]{3,2,1,0:T(8,128)(2,1)} %pack_prolong.1.refs_5_), channel_id=1, source_target_pairs={{0,8},{8,0},{16,24},{24,16},{1,9},{9,1},{17,25},{25,17},{2,10},{10... | collective-permute-start | bytes 2654216 | tf_op jit(solution)/shard_map/ppermute | solution.py:301
  6.5 21.7 %collective-permute-start.2 = (bf16[12,3,96,128]{3,2,1,0:T(8,128)(2,1)}, bf16[12,3,96,128]{3,2,1,0:T(8,128)(2,1)S(1)}, u32[]{:S(2)}, u32[]{:S(2)}) collective-permute-start(bf16[12,3,96,128]{3,2,1,0:T(8,128)(2,1)} %pack_prolong.1.refs_5_), channel_id=1, source_target_pairs={{0,16},{8,24},{16,0},{24,8},{1,17},{9,25},{17,1},{25,9},{2,18},{10... | collective-permute-start | bytes 2654216 | tf_op jit(solution)/shard_map/ppermute | solution.py:301
  26.4 36.3 %copy-start = (bf16[12,3,96,128]{3,2,1,0:T(8,128)(2,1)}, bf16[12,3,96,128]{3,2,1,0:T(8,128)(2,1)S(1)}, u32[]{:S(2)}) copy-start(bf16[12,3,96,128]{3,2,1,0:T(8,128)(2,1)S(1)} %collective-permute-done.refs_5_) | copy-start | bytes 2654212
  26.4 58.6 %collective-permute-start.1 = (bf16[6,3,96,128]{3,2,1,0:T(8,128)(2,1)S(1)}, bf16[6,3,96,128]{3,2,1,0:T(8,128)(2,1)S(1)}, u32[]{:S(2)}, u32[]{:S(2)}) collective-permute-start(bf16[6,3,96,128]{3,2,1,0:T(8,128)(2,1)S(1)} %slice.36), channel_id=1, source_target_pairs={{0,16},{8,24},{16,0},{24,8},{1,17},{9,25},{17,1},{25,9},{2,18},{10... | collective-permute-start | bytes 1327112 | tf_op jit(solution)/shard_map/ppermute | solution.py:301
  28.3 34.5 %copy-start.1 = (bf16[12,3,96,128]{3,2,1,0:T(8,128)(2,1)}, bf16[12,3,96,128]{3,2,1,0:T(8,128)(2,1)S(1)}, u32[]{:S(2)}) copy-start(bf16[12,3,96,128]{3,2,1,0:T(8,128)(2,1)S(1)} %collective-permute-done.2.refs_6_) | copy-start | bytes 2654212
  28.3 56.8 %collective-permute-start.3 = (bf16[6,3,96,128]{3,2,1,0:T(8,128)(2,1)S(1)}, bf16[6,3,96,128]{3,2,1,0:T(8,128)(2,1)S(1)}, u32[]{:S(2)}, u32[]{:S(2)}) collective-permute-start(bf16[6,3,96,128]{3,2,1,0:T(8,128)(2,1)S(1)} %slice.37), channel_id=1, source_target_pairs={{0,8},{8,0},{16,24},{24,16},{1,9},{9,1},{17,25},{25,17},{2,10},{10... | collective-permute-start | bytes 1327112 | tf_op jit(solution)/shard_map/ppermute | solution.py:301
  105.8 16.5 %collective-permute-start.4 = (bf16[8,3,96,128]{3,2,1,0:T(8,128)(2,1)}, bf16[8,3,96,128]{3,2,1,0:T(8,128)(2,1)S(1)}, u32[]{:S(2)}, u32[]{:S(2)}) collective-permute-start(bf16[8,3,96,128]{3,2,1,0:T(8,128)(2,1)} %get-tuple-element.14), channel_id=1, source_target_pairs={{0,8},{8,0},{16,24},{24,16},{1,9},{9,1},{17,25},{25,17},{2,10},{10... | collective-permute-start | bytes 1769480 | tf_op jit(solution)/shard_map/ppermute | solution.py:301
  106.4 26.2 %collective-permute-start.5 = (bf16[8,3,96,128]{3,2,1,0:T(8,128)(2,1)}, bf16[8,3,96,128]{3,2,1,0:T(8,128)(2,1)S(1)}, u32[]{:S(2)}, u32[]{:S(2)}) collective-permute-start(bf16[8,3,96,128]{3,2,1,0:T(8,128)(2,1)} %get-tuple-element.15), channel_id=1, source_target_pairs={{0,16},{8,24},{16,0},{24,8},{1,17},{9,25},{17,1},{25,9},{2,18},{10... | collective-permute-start | bytes 1769480 | tf_op jit(solution)/shard_map/ppermute | solution.py:301
  107.6 25.1 %collective-permute-start.6 = (bf16[8,3,96,128]{3,2,1,0:T(8,128)(2,1)}, bf16[8,3,96,128]{3,2,1,0:T(8,128)(2,1)S(1)}, u32[]{:S(2)}, u32[]{:S(2)}) collective-permute-start(bf16[8,3,96,128]{3,2,1,0:T(8,128)(2,1)} %get-tuple-element.16), channel_id=1, source_target_pairs={{0,24},{8,16},{16,8},{24,0},{1,25},{9,17},{17,9},{25,1},{2,26},{10... | collective-permute-start | bytes 1769480 | tf_op jit(solution)/shard_map/ppermute | solution.py:301
  134.2 2.1 %collective-permute-start.7 = (f32[4,3,96,128]{3,2,1,0:T(8,128)S(1)}, f32[4,3,96,128]{3,2,1,0:T(8,128)S(1)}, u32[]{:S(2)}, u32[]{:S(2)}) collective-permute-start(f32[4,3,96,128]{3,2,1,0:T(8,128)S(1)} %dynamic-slice_bitcast_fusion), channel_id=1, source_target_pairs={{0,1},{1,0},{2,3},{3,2},{4,5},{5,4},{6,7},{7,6},{8,9},{9,8},{10,11... | collective-permute-start | bytes 1769480 | tf_op jit(solution)/shard_map/ppermute | solution.py:301
  136.4 7.0 %collective-permute-start.10 = (bf16[3,96,128]{2,1,0:T(8,128)(2,1)S(1)}, bf16[3,96,128]{2,1,0:T(8,128)(2,1)S(1)}, u32[]{:S(2)}, u32[]{:S(2)}) collective-permute-start(bf16[3,96,128]{2,1,0:T(8,128)(2,1)S(1)} %get-tuple-element.23), channel_id=1, source_target_pairs={{0,6},{1,7},{2,4},{3,5},{4,2},{5,3},{6,0},{7,1},{8,14},{9,15},{10,... | collective-permute-start | bytes 221192 | tf_op jit(solution)/shard_map/ppermute | solution.py:301
  140.1 5.3 %collective-permute-start.8 = (bf16[3,96,128]{2,1,0:T(8,128)(2,1)S(1)}, bf16[3,96,128]{2,1,0:T(8,128)(2,1)S(1)}, u32[]{:S(2)}, u32[]{:S(2)}) collective-permute-start(bf16[3,96,128]{2,1,0:T(8,128)(2,1)S(1)} %get-tuple-element.22), channel_id=1, source_target_pairs={{0,2},{1,3},{2,0},{3,1},{4,6},{5,7},{6,4},{7,5},{8,10},{9,11},{10,... | collective-permute-start | bytes 221192 | tf_op jit(solution)/shard_map/ppermute | solution.py:301
  140.1 7.0 %collective-permute-start.9 = (bf16[3,96,128]{2,1,0:T(8,128)(2,1)S(1)}, bf16[3,96,128]{2,1,0:T(8,128)(2,1)S(1)}, u32[]{:S(2)}, u32[]{:S(2)}) collective-permute-start(bf16[3,96,128]{2,1,0:T(8,128)(2,1)S(1)} %get-tuple-element.24), channel_id=1, source_target_pairs={{0,4},{1,5},{2,6},{3,7},{4,0},{5,1},{6,2},{7,3},{8,12},{9,13},{10,... | collective-permute-start | bytes 221192 | tf_op jit(solution)/shard_map/ppermute | solution.py:301

commit v2 on v0

v2 whole, which is shorter than its diff:
```python
import functools

import jax
import jax.numpy as jnp
from jax import lax
from jax.experimental import pallas as pl
from jax.experimental.pallas import tpu as pltpu
from jax.sharding import PartitionSpec as P

OWN = 4
UNROLL = 16
LANES = 128
VMEM_LIMIT = 63 * 1024 * 1024
HBM = pl.BlockSpec(memory_space=pl.ANY)


def pack_four(blocks, width):
    strip = LANES - width
    return [
        jnp.concatenate(
            [blocks[t][:, :width], blocks[3][:, strip * t : strip * (t + 1)]], axis=1
        )
        for t in range(3)
    ]


def unpack_last(parts, width):
    return jnp.concatenate([part[:, width:] for part in parts], axis=1)


def pack_kernel(p_ref, out_ref):
    width = p_ref.shape[-1]
    for quad in range(p_ref.shape[0]):
        packed = pack_four([p_ref[quad, t] for t in range(4)], width)
        for t in range(3):
            out_ref[quad, t] = packed[t]


def pack_prolong(prolong):
    width = prolong.shape[-1]
    quads = prolong.shape[1] * prolong.shape[2] // 4
    step = 3
    return pl.pallas_call(
        pack_kernel,
        grid=(quads // step,),
        in_specs=[pl.BlockSpec((step, 4, width, width), lambda g: (g, 0, 0, 0))],
        out_specs=pl.BlockSpec((step, 3, width, LANES), lambda g: (g, 0, 0, 0)),
        out_shape=jax.ShapeDtypeStruct((quads, 3, width, LANES), prolong.dtype),
        name="pack_prolong",
    )(prolong.reshape(quads, 4, width, width))


def work_kernel(cfg, *refs):
    first, last, phase = cfg["first"], cfg["last"], cfg["phase"]
    width, rows, nonzeros, per_row = cfg["width"], cfg["rows"], cfg["nonzeros"], cfg["per_row"]
    slots, members, groups = cfg["slots"], cfg["members"], cfg["groups"]
    refs = list(refs)
    take = lambda n: [refs.pop(0) for _ in range(n)]
    list_ref, info_ref, col_ref, tgt_ref, a_hbm = take(5)
    p_hbm = take(cfg["sources"])
    if not first:
        pt_hbm, acc_in = take(2)
    out_refs = take(2 if first or last else 1)
    p_vmem, pt, a_rows, acc = take(4)
    aps = take(UNROLL)
    a_sem, sem, out_sem = take(3)
    if last:
        stages = take(2)

    base = phase * cfg["list_len"]
    turns = info_ref[phase]
    me, chip, core = [info_ref[cfg["phases"] + x] for x in range(3)]

    def a_copy(i):
        to = a_rows.at[pl.ds(i * nonzeros, nonzeros)]
        return pltpu.make_async_copy(a_hbm.at[i], to, a_sem.at[i])

    def start_row(i, _):
        a_copy(i).start()
        return 0

    def wait_row(i, _):
        a_copy(i).wait()
        return 0

    p_copies, at = [], 0
    for s, source in enumerate(p_hbm):
        to = p_vmem.at[pl.ds(at, source.shape[0]), pl.ds(0, 3)]
        p_copies.append(pltpu.make_async_copy(source, to, sem.at[s]))
        at += source.shape[0]
    others = []
    if not first:
        others.append(pltpu.make_async_copy(pt_hbm, pt, sem.at[cfg["sources"]]))
        others.append(pltpu.make_async_copy(acc_in, acc, sem.at[cfg["sources"] + 1]))
    for copy in p_copies + others:
        copy.start()
    lax.fori_loop(0, rows, start_row, 0)

    a_rows[rows * nonzeros] = jnp.zeros((width, width), a_rows.dtype)
    for ap in aps:
        ap[...] = jnp.zeros_like(ap)
    if first:

        def clear(s, _):
            for x in range(8):
                acc[s * 8 + x] = jnp.zeros((width, LANES), acc.dtype)
            return 0

        lax.fori_loop(0, slots // 8, clear, 0)
    for copy in p_copies:
        copy.wait()

    def unpack(q, _):
        for x in range(2):
            parts = [p_vmem[q * 2 + x, t] for t in range(3)]
            p_vmem[q * 2 + x, 3, :, :width] = unpack_last(parts, width)
        return 0

    lax.fori_loop(0, at // 2, unpack, 0)
    if first:

        def transpose(q, _):
            for x in range(4):
                block = p_vmem[q, x].astype(jnp.float32).T[:width].astype(pt.dtype)
                n = x % per_row
                pt[q * (4 // per_row) + x // per_row, n * width : (n + 1) * width, :] = block
            return 0

        lax.fori_loop(0, at, transpose, 0)
    for copy in others:
        copy.wait()

    scale = 65536 // rows + 1
    assert all((j * scale) >> 16 == j // rows for j in range(rows * members))

    def p_block(i, k):
        j = col_ref[jnp.minimum(i, rows - 1), k]
        member = (j * scale) >> 16
        place = ((member ^ me) - cfg["from"]) * rows + j - member * rows
        return jnp.where(i < rows, place, 0)

    def turn(g, ready):
        need = jnp.minimum((list_ref[base + (g + 2) * UNROLL - 1] >> 5) + 1, rows)
        lax.fori_loop(ready, need, wait_row, 0)

        def products(u):
            v = list_ref[base + g * UNROLL + u]
            i, k = jnp.minimum(v >> 5, rows - 1), v & 31
            partial = jnp.dot(pt[i], aps[u][...], preferred_element_type=jnp.float32)
            w = list_ref[base + (g + 1) * UNROLL + u]
            j = p_block(w >> 5, w & 31)
            right = jnp.concatenate(
                [p_vmem[j >> 1, (j & 1) * 2 + m] for m in range(per_row)], axis=1
            )
            left = a_rows[(w >> 5) * nonzeros + (w & 31)]
            ap = jnp.dot(left, right, preferred_element_type=jnp.float32)
            return u, i, k, partial, ap

        def collect(u, i, k, partial, ap):
            aps[u][...] = ap.astype(jnp.bfloat16)
            for n in range(per_row):
                for m in range(per_row):
                    s = tgt_ref[i, n * nonzeros * per_row + k * per_row + m]
                    acc[s] = acc[s] + partial[
                        n * width : (n + 1) * width, m * LANES : (m + 1) * LANES
                    ]

        held = products(0)
        for u in range(1, UNROLL):
            made = products(u)
            collect(*held)
            held = made
        collect(*held)
        return jnp.maximum(ready, need)

    ready = lax.fori_loop(0, turns + 1, turn, jnp.int32(0))
    lax.fori_loop(ready, rows, wait_row, 0)

    if last:

        def emit(rz, _):
            for rc in range(2):
                for r in range(members):
                    s = ((chip ^ rz) * 2 + (core ^ rc)) * (OWN * members) + (me ^ r) * OWN
                    packed = pack_four([acc[s + x] for x in range(OWN)], width)
                    for t in range(3):
                        stages[rc][rz, r, t] = packed[t].astype(stages[rc].dtype)
                copy = pltpu.make_async_copy(stages[rc].at[rz], out_refs[rc].at[rz], out_sem.at[rc])
                copy.start()
            return 0

        lax.fori_loop(0, groups // 2, emit, 0)
        for rc in range(2):
            pltpu.make_async_copy(stages[rc], out_refs[rc], out_sem.at[rc]).wait()
    else:
        outs = [pltpu.make_async_copy(acc, out_refs[0], out_sem.at[0])]
        if first:
            outs.append(pltpu.make_async_copy(pt, out_refs[1], out_sem.at[1]))
        for copy in outs:
            copy.start()
        for copy in outs:
            copy.wait()


def work(cfg, tables, a_rows, packed, pt=None, acc=None):
    width, rows, nonzeros, per_row = cfg["width"], cfg["rows"], cfg["nonzeros"], cfg["per_row"]
    slots, members, groups = cfg["slots"], cfg["members"], cfg["groups"]
    cfg = dict(cfg, sources=len(packed))
    quads = sum(x.shape[0] for x in packed)
    operands = [a_rows, *packed] + ([] if cfg["first"] else [pt, acc])
    pt_shape = (rows, per_row * width, width)
    stages = []
    if cfg["last"]:
        whole = (groups // 2, members, 3, width, LANES)
        shapes = [jax.ShapeDtypeStruct(whole, jnp.float32), jax.ShapeDtypeStruct(whole, jnp.bfloat16)]
        stages = [pltpu.VMEM(x.shape, x.dtype) for x in shapes]
    else:
        shapes = [jax.ShapeDtypeStruct((slots, width, LANES), jnp.float32)]
        if cfg["first"]:
            shapes.append(jax.ShapeDtypeStruct(pt_shape, jnp.bfloat16))
    return pl.pallas_call(
        functools.partial(work_kernel, cfg),
        grid_spec=pltpu.PrefetchScalarGridSpec(
            num_scalar_prefetch=4,
            grid=(),
            in_specs=[HBM] * len(operands),
            out_specs=[HBM] * len(shapes),
            scratch_shapes=[
                pltpu.VMEM((quads, 4, width, LANES), jnp.bfloat16),
                pltpu.VMEM(pt_shape, jnp.bfloat16),
                pltpu.VMEM((rows * nonzeros + 1, width, width), jnp.bfloat16),
                pltpu.VMEM((slots, width, LANES), jnp.float32),
            ]
            + [pltpu.VMEM((width, per_row * LANES), jnp.bfloat16)] * UNROLL
            + [
                pltpu.SemaphoreType.DMA((rows,)),
                pltpu.SemaphoreType.DMA((len(packed) + 2,)),
                pltpu.SemaphoreType.DMA((2,)),
            ]
            + stages,
        ),
        out_shape=shapes,
        compiler_params=pltpu.CompilerParams(vmem_limit_bytes=VMEM_LIMIT),
        cost_estimate=pl.CostEstimate(
            flops=4 * rows * nonzeros * width * width * width,
            bytes_accessed=20_000_000,
            transcendentals=0,
        ),
        name="work_%d" % cfg["phase"],
    )(*tables, *operands)


def make_lists(columns, place, phase_of):
    rows, nonzeros = columns.shape
    entries = rows * nonzeros
    phases = max(phase_of) + 1
    list_len = (-(-entries // UNROLL) + 2) * UNROLL
    relative = (columns // rows) ^ place[0]
    flat = sum(jnp.where(relative == r, p, 0) for r, p in enumerate(phase_of)).reshape(-1)
    order = jnp.arange(entries, dtype=jnp.int32)
    before = (flat[None, :] == flat[:, None]) & (order[None, :] < order[:, None])
    position = flat * list_len + UNROLL + jnp.sum(before.astype(jnp.int32), axis=1)
    counts = jnp.stack([jnp.sum((flat == p).astype(jnp.int32)) for p in range(phases)])
    value = (order // nonzeros) * 32 + order % nonzeros
    none = rows * 32
    x = jnp.arange(phases * list_len, dtype=jnp.int32)
    lists = none + jnp.sum(
        jnp.where(position[None, :] == x[:, None], value[None, :] - none, 0), axis=1
    )
    info = jnp.concatenate([-(-counts // UNROLL), jnp.stack(place)])
    return lists.astype(jnp.int32), info.astype(jnp.int32), list_len


def shards(a_blocks, col_index, prolong, target):
    rows, nonzeros = a_blocks.shape[1:3]
    per_row = prolong.shape[2]
    width = a_blocks.shape[-1]
    groups = lax.axis_size("grp")
    members = lax.axis_size("blk")
    chips = groups // 2
    slots = groups * OWN * members
    f32, bf16 = jnp.float32, jnp.bfloat16
    rank = lax.axis_index("grp").astype(jnp.int32)
    place = [lax.axis_index("blk").astype(jnp.int32), rank // 2, rank % 2]

    def exchange(x, r, axis="blk", size=members):
        return lax.ppermute(x, axis, [(d, d ^ r) for d in range(size)])

    if members == 4:
        sources = [[0], [1, 2], [3]]
    else:
        sources = [[0]] + [list(range(r, min(r + 3, members))) for r in range(1, members, 3)]
    phases = len(sources)
    phase_of = [p for p in range(phases) for _ in sources[p]]

    own = pack_prolong(prolong)
    near = [exchange(own, r) for r in range(1, 3 if members == 4 else members)]
    lists, info, list_len = make_lists(col_index[0], place, phase_of)
    cfg = dict(
        width=width, rows=rows, nonzeros=nonzeros, per_row=per_row, slots=slots,
        members=members, groups=groups, phases=phases, list_len=list_len,
    )
    packed = [[own]] + [[near[r - 1] for r in s if r <= len(near)] for s in sources[1:]]
    pt = acc = None
    for p in range(phases):
        outs = work(
            {**cfg, "phase": p, "first": p == 0, "last": p == phases - 1, "from": sources[p][0]},
            (lists, info, col_index[0], target[0]), a_blocks[0], packed[p], pt, acc,
        )
        acc = outs[0]
        if p == 0:
            pt = outs[1]
            if members == 4:
                (x, y), _ = lax.optimization_barrier((near, acc))
                half = own.shape[0] // 2
                packed = [[own], [x, y], [exchange(x[:half], 2), exchange(y[half:], 1)]]

    keep, give = outs
    total = keep + exchange(give, 1, "grp", groups).astype(f32)
    half = width // 2
    one, two = total[..., :half, :], total[..., half:, :]
    got = [exchange(one[:, r].astype(bf16), r) for r in range(1, members)]
    sent = [exchange(two[r].astype(bf16), 2 * r, "grp", groups) for r in range(1, chips)]
    got, sent = lax.optimization_barrier((got, sent))
    one, two = one[:, 0], two[0]
    for part in got:
        one = one + part.astype(f32)
    for part in sent:
        two = two + part.astype(f32)
    mine, other = one[0], two[0]
    for r in range(1, chips):
        mine = mine + exchange(one[r].astype(bf16), 2 * r, "grp", groups).astype(f32)
    for r in range(1, members):
        other = other + exchange(two[r].astype(bf16), r).astype(f32)
    mine = jnp.concatenate([mine, other], axis=1)
    fourth = unpack_last([mine[t] for t in range(3)], width)
    return jnp.concatenate([mine[:, :, :width], fourth[None]])[None]


def solution(mesh):
    return jax.shard_map(
        shards,
        mesh=mesh,
        in_specs=(
            P("grp", "blk", None, None, None),
            P("grp", "blk", None),
            P("grp", "blk", None, None, None),
            P("grp", "blk", None),
        ),
        out_specs=P("grp", "blk", None, None),
        check_vma=False,
    )
```

time: 1000 us -> 114 us (0.11)
  other arithmetic: 480 us -> 8.71 us
  local copies, waits for them, and re-layouts: 201 us -> 3.28 us
  blocking collectives: 146 us -> 0 us
  waiting for transfers between devices: 82.5 us -> 12.5 us
  matrix products: 69.6 us -> 0 us
  Pallas kernels: 0 us -> 63.7 us
  starting transfers between devices: 0.04 us -> 25.7 us
  between operations: 13.4 us -> 0.22 us
    scatter-add x6 -> x0, other arithmetic: 452 us -> none  [one_block(): jax.ops.segment_sum(partial_value, t_part.reshape(-1), num_segments=slots)]
    all_to_all x1 -> x0, blocking collectives: 146 us -> none  [shards(): lax.all_to_all(buffer, 'grp', split_axis=0, concat_axis=0, tiled=True)]
    transpose x6 -> x0, local copies, waits for them, and re-layouts: 126 us -> none  [one_block(): jnp.einsum('rnab,rkmbc->rnkmac', p_part, product, preferred_element_type=...]
    dot_general x6 -> x0, matrix products: 69.6 us -> none  [one_block(): jnp.einsum('rnab,rkmbc->rnkmac', p_part, product, preferred_element_type=...]
    pallas_call x0 -> x4, Pallas kernels: none -> 63.7 us  [the longest x3 60.1 us: work(): pl.pallas_call(functools.partial(work_kernel, cfg), grid_spec=pltpu.Prefe...]
    gather x2 -> x0, local copies, waits for them, and re-layouts: 61.6 us -> none  [shards(): taken = jnp.take(piece[0], jnp.clip(columns, 0, count - 1), axis=0)]
    all_gather x1 -> x0, waiting for transfers between devices: 57.8 us -> none  [shards(): piece = lax.all_gather(prolong, 'blk', axis=1, tiled=True)]
    ppermute x0 -> x17, starting transfers between devices: none -> 25.7 us  [exchange(): return lax.ppermute(x, axis, [(d, d ^ r) for d in range(size)])]
  transfers between devices with their start and end apart: 2 -> 17, of which waited for: 2 -> 5; matrix products, arithmetic and copies ran while one was open for 0% -> 5% of each run, Pallas kernels for 0% -> 38%
where the time goes in v2:
time: 114 us
  Pallas kernels  63.7 us (56%)
  starting transfers between devices  25.7 us (23%)
  waiting for transfers between devices  12.5 us (11%)
  other arithmetic  8.71 us (8%)
  local copies, waits for them, and re-layouts  3.28 us (3%)
    pallas_call x3, Pallas kernels, work(): pl.pallas_call(functools.partial(work_kernel, cfg), grid_spec=pltpu.Prefe...  60.1 us
    ppermute x17, starting transfers between devices, exchange(): return lax.ppermute(x, axis, [(d, d ^ r) for d in range(size)])  25.7 us
    ppermute x17, waiting for transfers between devices, exchange(): return lax.ppermute(x, axis, [(d, d ^ r) for d in range(size)])  12.5 us
    pallas_call x1, Pallas kernels, pack_prolong(): pl.pallas_call(pack_kernel, grid=(quads // step,), in_specs=[pl.BlockSpec...  3.56 us
    slice x2, local copies, waits for them, and re-layouts, shards(): packed = [[own], [x, y], [exchange(x[:half], 2), exchange(y[half:], 1)]]  2.7 us
  transfers between devices with their start and end apart: 17, of which 5 were waited for; matrix products, arithmetic and copies ran while one was open for 5% of the time, Pallas kernels for 38%

profile of v2, /device:TPU:0, one launch (start us, length us, event | category | flops | bytes accessed | tf_op | source)
XLA Modules:
  0.0 114.2 jit_solution(2250908567270552056)
XLA Ops:
  0.0 3.6 %pack_prolong.1.refs_5_ = bf16[12,3,96,128]{3,2,1,0:T(8,128)(2,1)} custom-call(bf16[12,4,96,96]{3,2,1,0:T(8,128)(2,1)} %bitcast.81), custom_call_target="tpu_custom_call" | custom-call | tf_op jit(solution)/shard_map/pack_prolong/pallas_call | solution.py:43
  3.6 3.0 %collective-permute-start.1 = (bf16[12,3,96,128]{3,2,1,0:T(8,128)(2,1)}, bf16[12,3,96,128]{3,2,1,0:T(8,128)(2,1)S(1)}, u32[]{:S(2)}, u32[]{:S(2)}) collective-permute-start(bf16[12,3,96,128]{3,2,1,0:T(8,128)(2,1)} %pack_prolong.1.refs_5_), channel_id=1, source_target_pairs={{0,16},{8,24},{16,0},{24,8},{1,17},{9,25},{17,1},{25,9},{2,18},{10... | collective-permute-start | bytes 2654216 | tf_op jit(solution)/shard_map/ppermute | solution.py:287
  6.5 1.5 %collective-permute-start = (bf16[12,3,96,128]{3,2,1,0:T(8,128)(2,1)}, bf16[12,3,96,128]{3,2,1,0:T(8,128)(2,1)}, u32[]{:S(2)}, u32[]{:S(2)}) collective-permute-start(bf16[12,3,96,128]{3,2,1,0:T(8,128)(2,1)} %pack_prolong.1.refs_5_), channel_id=1, source_target_pairs={{0,8},{8,0},{16,24},{24,16},{1,9},{9,1},{17,25},{25,17},{2,10},{10... | collective-permute-start | bytes 2654216 | tf_op jit(solution)/shard_map/ppermute | solution.py:287
  8.8 0.7 convert_reduce_fusion.3
  10.0 2.0 %fusion.32 = s32[3]{0:T(128)S(1)} fusion(s32[1]{0:T(128)} %bitcast.2, s32[1]{0:T(128)} %bitcast.1, s32[1]{0:T(128)} %bitcast), kind=kLoop, calls=%fused_computation.85 | loop fusion | flops 54 | bytes 24 | tf_op jit(solution)/shard_map/neg | solution.py:270
  12.6 0.8 select_reduce_fusion
  13.9 24.3 %work_0.1 = (f32[128,96,128]{2,1,0:T(8,128)}, bf16[24,192,96]{2,1,0:T(8,128)(2,1)}) custom-call(s32[2064]{0:T(1024)} %broadcast_add_fusion.refs_0_, s32[6]{0:T(128)} %pad_add_fusion.1.refs_1_, s32[24,27]{1,0:T(8,128)} %bitcast.82, s32[24,108]{1,0:T(8,128)} %bitcast.85, bf16[24,27,96,96]{3,2,1,0:T(8,128)(2,1)} %bitcast.78, ...), custom_call_target="tpu_custom_call" | custom-call | flops 2293235712 | bytes 20000000 | tf_op jit(solution)/shard_map/work_0/pallas_call | solution.py:221
  38.3 0.9 slice.98
  39.2 1.8 %slice.97 = bf16[6,3,96,128]{3,2,1,0:T(8,128)(2,1)} slice(bf16[12,3,96,128]{3,2,1,0:T(8,128)(2,1)} %collective-permute-done.refs_5_), slice={[0:6], [0:3], [0:96], [0:128]} | slice | bytes 884736 | tf_op jit(solution)/shard_map/slice | solution.py:316
  41.0 19.0 %work_1.1.refs_8_ = f32[128,96,128]{2,1,0:T(8,128)} custom-call(s32[2064]{0:T(1024)} %broadcast_add_fusion.refs_0_, s32[6]{0:T(128)} %pad_add_fusion.1.refs_1_, s32[24,27]{1,0:T(8,128)} %bitcast.83, s32[24,108]{1,0:T(8,128)} %bitcast.86, bf16[24,27,96,96]{3,2,1,0:T(8,128)(2,1)} %bitcast.79, bf16[12,3,96,128]{3,2,1,0:T(8,128)(2,1)} %collective-permute-done.refs_5_, ...), custom_call_target="tpu_custom_call" | custom-call | flops 2293235712 | bytes 20000000 | tf_op jit(solution)/shard_map/work_1/pallas_call | solution.py:221
  60.0 16.9 %work_2.1 = (f32[4,4,3,96,128]{4,3,2,1,0:T(8,128)}, bf16[4,4,3,96,128]{4,3,2,1,0:T(8,128)(2,1)}) custom-call(s32[2064]{0:T(1024)} %broadcast_add_fusion.refs_0_, s32[6]{0:T(128)} %pad_add_fusion.1.refs_1_, s32[24,27]{1,0:T(8,128)} %bitcast.84, s32[24,108]{1,0:T(8,128)} %bitcast.87, bf16[24,27,96,96]{3,2,1,0:T(8,128)(2,1)} %bitcast.80, ...), custom_call_target="tpu_custom_call" | custom-call | flops 2293235712 | bytes 20000000 | tf_op jit(solution)/shard_map/work_2/pallas_call | solution.py:221
  76.9 3.0 %collective-permute-done.4 = bf16[4,4,3,96,128]{4,3,2,1,0:T(8,128)(2,1)S(1)} collective-permute-done((bf16[4,4,3,96,128]{4,3,2,1,0:T(8,128)(2,1)}, bf16[4,4,3,96,128]{4,3,2,1,0:T(8,128)(2,1)S(1)}, u32[]{:S(2)}, u32[]{:S(2)}) %collective-permute-start.4) | collective-permute-done | bytes 1179680 | tf_op jit(solution)/shard_map/ppermute | solution.py:287
  80.0 2.0 %convert_add_fusion = f32[4,4,3,96,128]{4,3,2,1,0:T(8,128)S(1)} fusion(f32[4,4,3,96,128]{4,3,2,1,0:T(8,128)} %get-tuple-element.21, bf16[4,4,3,96,128]{4,3,2,1,0:T(8,128)(2,1)S(1)} %collective-permute-done.4), kind=kLoop, calls=%fused_computation.2 | loop fusion | flops 1179648 | bytes 5898240 | tf_op jit(solution)/shard_map/add | solution.py:319
  82.1 4.0 %collective-permute-start.10 = (bf16[4,3,48,128]{3,2,1,0:T(8,128)(2,1)S(1)}, bf16[4,3,48,128]{3,2,1,0:T(8,128)(2,1)S(1)}, u32[]{:S(2)}, u32[]{:S(2)}) collective-permute-start(bf16[4,3,48,128]{3,2,1,0:T(8,128)(2,1)S(1)} %get-tuple-element.38), channel_id=1, source_target_pairs={{0,6},{1,7},{2,4},{3,5},{4,2},{5,3},{6,0},{7,1},{8,14},{9,15},{10,... | collective-permute-start | bytes 442376 | tf_op jit(solution)/shard_map/ppermute | solution.py:287
  86.8 3.5 %collective-permute-start.7 = (bf16[4,3,48,128]{3,2,1,0:T(8,128)(2,1)S(1)}, bf16[4,3,48,128]{3,2,1,0:T(8,128)(2,1)S(1)}, u32[]{:S(2)}, u32[]{:S(2)}) collective-permute-start(bf16[4,3,48,128]{3,2,1,0:T(8,128)(2,1)S(1)} %get-tuple-element.41), channel_id=1, source_target_pairs={{0,24},{8,16},{16,8},{24,0},{1,25},{9,17},{17,9},{25,1},{2,26},{10... | collective-permute-start | bytes 442376 | tf_op jit(solution)/shard_map/ppermute | solution.py:287
  90.3 0.9 collective-permute-start.6
  91.2 2.6 %collective-permute-start.5 = (bf16[4,3,48,128]{3,2,1,0:T(8,128)(2,1)S(1)}, bf16[4,3,48,128]{3,2,1,0:T(8,128)(2,1)S(1)}, u32[]{:S(2)}, u32[]{:S(2)}) collective-permute-start(bf16[4,3,48,128]{3,2,1,0:T(8,128)(2,1)S(1)} %get-tuple-element.43), channel_id=1, source_target_pairs={{0,8},{8,0},{16,24},{24,16},{1,9},{9,1},{17,25},{25,17},{2,10},{10... | collective-permute-start | bytes 442376 | tf_op jit(solution)/shard_map/ppermute | solution.py:287
  93.9 5.8 %collective-permute-done.9 = bf16[4,3,48,128]{3,2,1,0:T(8,128)(2,1)S(1)} collective-permute-done((bf16[4,3,48,128]{3,2,1,0:T(8,128)(2,1)S(1)}, bf16[4,3,48,128]{3,2,1,0:T(8,128)(2,1)S(1)}, u32[]{:S(2)}, u32[]{:S(2)}) %collective-permute-start.9) | collective-permute-done | bytes 147488 | tf_op jit(solution)/shard_map/ppermute | solution.py:287
  99.8 3.2 %collective-permute-start.11 = (bf16[3,48,128]{2,1,0:T(8,128)(2,1)S(1)}, bf16[3,48,128]{2,1,0:T(8,128)(2,1)S(1)}, u32[]{:S(2)}, u32[]{:S(2)}) collective-permute-start(bf16[3,48,128]{2,1,0:T(8,128)(2,1)S(1)} %get-tuple-element.47), channel_id=1, source_target_pairs={{0,2},{1,3},{2,0},{3,1},{4,6},{5,7},{6,4},{7,5},{8,10},{9,11},{10,... | collective-permute-start | bytes 110600 | tf_op jit(solution)/shard_map/ppermute | solution.py:287
  103.1 2.6 %collective-permute-start.13 = (bf16[3,48,128]{2,1,0:T(8,128)(2,1)S(1)}, bf16[3,48,128]{2,1,0:T(8,128)(2,1)S(1)}, u32[]{:S(2)}, u32[]{:S(2)}) collective-permute-start(bf16[3,48,128]{2,1,0:T(8,128)(2,1)S(1)} %get-tuple-element.48), channel_id=1, source_target_pairs={{0,6},{1,7},{2,4},{3,5},{4,2},{5,3},{6,0},{7,1},{8,14},{9,15},{10,... | collective-permute-start | bytes 110600 | tf_op jit(solution)/shard_map/ppermute | solution.py:287
  105.8 2.1 %collective-permute-start.14 = (bf16[3,48,128]{2,1,0:T(8,128)(2,1)S(1)}, bf16[3,48,128]{2,1,0:T(8,128)(2,1)S(1)}, u32[]{:S(2)}, u32[]{:S(2)}) collective-permute-start(bf16[3,48,128]{2,1,0:T(8,128)(2,1)S(1)} %get-tuple-element.50), channel_id=1, source_target_pairs={{0,8},{8,0},{16,24},{24,16},{1,9},{9,1},{17,25},{25,17},{2,10},{10... | collective-permute-start | bytes 110600 | tf_op jit(solution)/shard_map/ppermute | solution.py:287
  107.8 0.9 collective-permute-start.16
  109.4 1.1 collective-permute-done.12
  110.5 2.3 %collective-permute-done.16 = bf16[3,48,128]{2,1,0:T(8,128)(2,1)S(1)} collective-permute-done((bf16[3,48,128]{2,1,0:T(8,128)(2,1)S(1)}, bf16[3,48,128]{2,1,0:T(8,128)(2,1)S(1)}, u32[]{:S(2)}, u32[]{:S(2)}) %collective-permute-start.16) | collective-permute-done | bytes 36896 | tf_op jit(solution)/shard_map/ppermute | solution.py:287
  (45 shorter events, 5.5 us)
Async XLA Ops:
  3.6 34.7 %collective-permute-start.1 = (bf16[12,3,96,128]{3,2,1,0:T(8,128)(2,1)}, bf16[12,3,96,128]{3,2,1,0:T(8,128)(2,1)S(1)}, u32[]{:S(2)}, u32[]{:S(2)}) collective-permute-start(bf16[12,3,96,128]{3,2,1,0:T(8,128)(2,1)} %pack_prolong.1.refs_5_), channel_id=1, source_target_pairs={{0,16},{8,24},{16,0},{24,8},{1,17},{9,25},{17,1},{25,9},{2,18},{10... | collective-permute-start | bytes 2654216 | tf_op jit(solution)/shard_map/ppermute | solution.py:287
  6.5 31.7 %collective-permute-start = (bf16[12,3,96,128]{3,2,1,0:T(8,128)(2,1)}, bf16[12,3,96,128]{3,2,1,0:T(8,128)(2,1)}, u32[]{:S(2)}, u32[]{:S(2)}) collective-permute-start(bf16[12,3,96,128]{3,2,1,0:T(8,128)(2,1)} %pack_prolong.1.refs_5_), channel_id=1, source_target_pairs={{0,8},{8,0},{16,24},{24,16},{1,9},{9,1},{17,25},{25,17},{2,10},{10... | collective-permute-start | bytes 2654216 | tf_op jit(solution)/shard_map/ppermute | solution.py:287
  38.2 2.7 %copy-start = (bf16[12,3,96,128]{3,2,1,0:T(8,128)(2,1)}, bf16[12,3,96,128]{3,2,1,0:T(8,128)(2,1)S(1)}, u32[]{:S(2)}) copy-start(bf16[12,3,96,128]{3,2,1,0:T(8,128)(2,1)S(1)} %collective-permute-done.1.refs_6_) | copy-start | bytes 2654212
  41.0 19.0 %collective-permute-start.2 = (bf16[6,3,96,128]{3,2,1,0:T(8,128)(2,1)}, bf16[6,3,96,128]{3,2,1,0:T(8,128)(2,1)}, u32[]{:S(2)}, u32[]{:S(2)}) collective-permute-start(bf16[6,3,96,128]{3,2,1,0:T(8,128)(2,1)} %slice.97), channel_id=1, source_target_pairs={{0,16},{8,24},{16,0},{24,8},{1,17},{9,25},{17,1},{25,9},{2,18},{10... | collective-permute-start | bytes 1327112 | tf_op jit(solution)/shard_map/ppermute | solution.py:287
  41.0 19.0 %collective-permute-start.3 = (bf16[6,3,96,128]{3,2,1,0:T(8,128)(2,1)}, bf16[6,3,96,128]{3,2,1,0:T(8,128)(2,1)}, u32[]{:S(2)}, u32[]{:S(2)}) collective-permute-start(bf16[6,3,96,128]{3,2,1,0:T(8,128)(2,1)} %slice.98), channel_id=1, source_target_pairs={{0,8},{8,0},{16,24},{24,16},{1,9},{9,1},{17,25},{25,17},{2,10},{10... | collective-permute-start | bytes 1327112 | tf_op jit(solution)/shard_map/ppermute | solution.py:287
  76.9 3.1 %collective-permute-start.4 = (bf16[4,4,3,96,128]{4,3,2,1,0:T(8,128)(2,1)}, bf16[4,4,3,96,128]{4,3,2,1,0:T(8,128)(2,1)S(1)}, u32[]{:S(2)}, u32[]{:S(2)}) collective-permute-start(bf16[4,4,3,96,128]{4,3,2,1,0:T(8,128)(2,1)} %get-tuple-element.22), channel_id=1, source_target_pairs={{0,1},{1,0},{2,3},{3,2},{4,5},{5,4},{6,7},{7,6},{8,9},{9,8},{10,11... | collective-permute-start | bytes 3538952 | tf_op jit(solution)/shard_map/ppermute | solution.py:287
  82.1 9.2 %collective-permute-start.10 = (bf16[4,3,48,128]{3,2,1,0:T(8,128)(2,1)S(1)}, bf16[4,3,48,128]{3,2,1,0:T(8,128)(2,1)S(1)}, u32[]{:S(2)}, u32[]{:S(2)}) collective-permute-start(bf16[4,3,48,128]{3,2,1,0:T(8,128)(2,1)S(1)} %get-tuple-element.38), channel_id=1, source_target_pairs={{0,6},{1,7},{2,4},{3,5},{4,2},{5,3},{6,0},{7,1},{8,14},{9,15},{10,... | collective-permute-start | bytes 442376 | tf_op jit(solution)/shard_map/ppermute | solution.py:287
  86.1 13.6 %collective-permute-start.9 = (bf16[4,3,48,128]{3,2,1,0:T(8,128)(2,1)S(1)}, bf16[4,3,48,128]{3,2,1,0:T(8,128)(2,1)S(1)}, u32[]{:S(2)}, u32[]{:S(2)}) collective-permute-start(bf16[4,3,48,128]{3,2,1,0:T(8,128)(2,1)S(1)} %get-tuple-element.39), channel_id=1, source_target_pairs={{0,4},{1,5},{2,6},{3,7},{4,0},{5,1},{6,2},{7,3},{8,12},{9,13},{10,... | collective-permute-start | bytes 442376 | tf_op jit(solution)/shard_map/ppermute | solution.py:287
  86.6 13.1 %collective-permute-start.8 = (bf16[4,3,48,128]{3,2,1,0:T(8,128)(2,1)S(1)}, bf16[4,3,48,128]{3,2,1,0:T(8,128)(2,1)S(1)}, u32[]{:S(2)}, u32[]{:S(2)}) collective-permute-start(bf16[4,3,48,128]{3,2,1,0:T(8,128)(2,1)S(1)} %get-tuple-element.40), channel_id=1, source_target_pairs={{0,2},{1,3},{2,0},{3,1},{4,6},{5,7},{6,4},{7,5},{8,10},{9,11},{10,... | collective-permute-start | bytes 442376 | tf_op jit(solution)/shard_map/ppermute | solution.py:287
  86.8 12.9 %collective-permute-start.7 = (bf16[4,3,48,128]{3,2,1,0:T(8,128)(2,1)S(1)}, bf16[4,3,48,128]{3,2,1,0:T(8,128)(2,1)S(1)}, u32[]{:S(2)}, u32[]{:S(2)}) collective-permute-start(bf16[4,3,48,128]{3,2,1,0:T(8,128)(2,1)S(1)} %get-tuple-element.41), channel_id=1, source_target_pairs={{0,24},{8,16},{16,8},{24,0},{1,25},{9,17},{17,9},{25,1},{2,26},{10... | collective-permute-start | bytes 442376 | tf_op jit(solution)/shard_map/ppermute | solution.py:287
  90.3 9.4 %collective-permute-start.6 = (bf16[4,3,48,128]{3,2,1,0:T(8,128)(2,1)S(1)}, bf16[4,3,48,128]{3,2,1,0:T(8,128)(2,1)S(1)}, u32[]{:S(2)}, u32[]{:S(2)}) collective-permute-start(bf16[4,3,48,128]{3,2,1,0:T(8,128)(2,1)S(1)} %get-tuple-element.42), channel_id=1, source_target_pairs={{0,16},{8,24},{16,0},{24,8},{1,17},{9,25},{17,1},{25,9},{2,18},{10... | collective-permute-start | bytes 442376 | tf_op jit(solution)/shard_map/ppermute | solution.py:287
  91.2 8.5 %collective-permute-start.5 = (bf16[4,3,48,128]{3,2,1,0:T(8,128)(2,1)S(1)}, bf16[4,3,48,128]{3,2,1,0:T(8,128)(2,1)S(1)}, u32[]{:S(2)}, u32[]{:S(2)}) collective-permute-start(bf16[4,3,48,128]{3,2,1,0:T(8,128)(2,1)S(1)} %get-tuple-element.43), channel_id=1, source_target_pairs={{0,8},{8,0},{16,24},{24,16},{1,9},{9,1},{17,25},{25,17},{2,10},{10... | collective-permute-start | bytes 442376 | tf_op jit(solution)/shard_map/ppermute | solution.py:287
  99.8 8.9 %collective-permute-start.11 = (bf16[3,48,128]{2,1,0:T(8,128)(2,1)S(1)}, bf16[3,48,128]{2,1,0:T(8,128)(2,1)S(1)}, u32[]{:S(2)}, u32[]{:S(2)}) collective-permute-start(bf16[3,48,128]{2,1,0:T(8,128)(2,1)S(1)} %get-tuple-element.47), channel_id=1, source_target_pairs={{0,2},{1,3},{2,0},{3,1},{4,6},{5,7},{6,4},{7,5},{8,10},{9,11},{10,... | collective-permute-start | bytes 110600 | tf_op jit(solution)/shard_map/ppermute | solution.py:287
  103.1 6.3 %collective-permute-start.13 = (bf16[3,48,128]{2,1,0:T(8,128)(2,1)S(1)}, bf16[3,48,128]{2,1,0:T(8,128)(2,1)S(1)}, u32[]{:S(2)}, u32[]{:S(2)}) collective-permute-start(bf16[3,48,128]{2,1,0:T(8,128)(2,1)S(1)} %get-tuple-element.48), channel_id=1, source_target_pairs={{0,6},{1,7},{2,4},{3,5},{4,2},{5,3},{6,0},{7,1},{8,14},{9,15},{10,... | collective-permute-start | bytes 110600 | tf_op jit(solution)/shard_map/ppermute | solution.py:287
  105.7 4.9 %collective-permute-start.12 = (bf16[3,48,128]{2,1,0:T(8,128)(2,1)S(1)}, bf16[3,48,128]{2,1,0:T(8,128)(2,1)S(1)}, u32[]{:S(2)}, u32[]{:S(2)}) collective-permute-start(bf16[3,48,128]{2,1,0:T(8,128)(2,1)S(1)} %get-tuple-element.49), channel_id=1, source_target_pairs={{0,4},{1,5},{2,6},{3,7},{4,0},{5,1},{6,2},{7,3},{8,12},{9,13},{10,... | collective-permute-start | bytes 110600 | tf_op jit(solution)/shard_map/ppermute | solution.py:287
  105.8 4.8 %collective-permute-start.14 = (bf16[3,48,128]{2,1,0:T(8,128)(2,1)S(1)}, bf16[3,48,128]{2,1,0:T(8,128)(2,1)S(1)}, u32[]{:S(2)}, u32[]{:S(2)}) collective-permute-start(bf16[3,48,128]{2,1,0:T(8,128)(2,1)S(1)} %get-tuple-element.50), channel_id=1, source_target_pairs={{0,8},{8,0},{16,24},{24,16},{1,9},{9,1},{17,25},{25,17},{2,10},{10... | collective-permute-start | bytes 110600 | tf_op jit(solution)/shard_map/ppermute | solution.py:287
  107.8 5.0 %collective-permute-start.16 = (bf16[3,48,128]{2,1,0:T(8,128)(2,1)S(1)}, bf16[3,48,128]{2,1,0:T(8,128)(2,1)S(1)}, u32[]{:S(2)}, u32[]{:S(2)}) collective-permute-start(bf16[3,48,128]{2,1,0:T(8,128)(2,1)S(1)} %get-tuple-element.51), channel_id=1, source_target_pairs={{0,24},{8,16},{16,8},{24,0},{1,25},{9,17},{17,9},{25,1},{2,26},{10... | collective-permute-start | bytes 110600 | tf_op jit(solution)/shard_map/ppermute | solution.py:287
  108.7 4.4 %collective-permute-start.15 = (bf16[3,48,128]{2,1,0:T(8,128)(2,1)S(1)}, bf16[3,48,128]{2,1,0:T(8,128)(2,1)S(1)}, u32[]{:S(2)}, u32[]{:S(2)}) collective-permute-start(bf16[3,48,128]{2,1,0:T(8,128)(2,1)S(1)} %get-tuple-element.52), channel_id=1, source_target_pairs={{0,16},{8,24},{16,0},{24,8},{1,17},{9,25},{17,1},{25,9},{2,18},{10... | collective-permute-start | bytes 110600 | tf_op jit(solution)/shard_map/ppermute | solution.py:287

commit v3 on v2

v3 whole, which is shorter than its diff:
```python
import functools

import jax
import jax.numpy as jnp
from jax import lax
from jax.experimental import pallas as pl
from jax.experimental.pallas import tpu as pltpu
from jax.sharding import PartitionSpec as P

OWN = 4
UNROLL = 16
LANES = 128
AHEAD = 6
VMEM_LIMIT = 63 * 1024 * 1024
HBM = pl.BlockSpec(memory_space=pl.ANY)


def pack_four(blocks, width):
    strip = LANES - width
    return [
        jnp.concatenate(
            [blocks[t][:, :width], blocks[3][:, strip * t : strip * (t + 1)]], axis=1
        )
        for t in range(3)
    ]


def unpack_last(parts, width):
    return jnp.concatenate([part[:, width:] for part in parts], axis=1)


def pack_kernel(p_hbm, *refs):
    outs, (blocks, packed, in_sem, out_sem) = refs[:2], refs[2:]
    width, quads = p_hbm.shape[-1], p_hbm.shape[0]
    steps = in_sem.shape[0]
    size = quads // steps
    half = steps // 2
    loads, stores = [], []
    for c in range(steps):
        part = pl.ds(c * size, size)
        to = outs[c // half].at[pl.ds(c % half * size, size)]
        loads.append(pltpu.make_async_copy(p_hbm.at[part], blocks.at[part], in_sem.at[c]))
        stores.append(pltpu.make_async_copy(packed.at[part], to, out_sem.at[c]))
        loads[c].start()
    for c in range(steps):
        loads[c].wait()
        for quad in range(c * size, (c + 1) * size):
            made = pack_four([blocks[quad, t] for t in range(4)], width)
            for t in range(3):
                packed[quad, t] = made[t]
        stores[c].start()
    for store in stores:
        store.wait()


def pack_prolong(prolong):
    width, dtype = prolong.shape[-1], prolong.dtype
    quads = prolong.shape[1] * prolong.shape[2] // 4
    steps = 4
    return pl.pallas_call(
        pack_kernel,
        in_specs=[HBM],
        out_specs=[HBM] * 2,
        out_shape=[jax.ShapeDtypeStruct((quads // 2, 3, width, LANES), dtype)] * 2,
        scratch_shapes=[
            pltpu.VMEM((quads, 4, width, width), dtype),
            pltpu.VMEM((quads, 3, width, LANES), dtype),
            pltpu.SemaphoreType.DMA((steps,)),
            pltpu.SemaphoreType.DMA((steps,)),
        ],
        compiler_params=pltpu.CompilerParams(vmem_limit_bytes=VMEM_LIMIT),
        name="pack_prolong",
    )(prolong.reshape(quads, 4, width, width))


def work_kernel(cfg, *refs):
    first, last, phase = cfg["first"], cfg["last"], cfg["phase"]
    width, rows, nonzeros, per_row = cfg["width"], cfg["rows"], cfg["nonzeros"], cfg["per_row"]
    slots, members, groups = cfg["slots"], cfg["members"], cfg["groups"]
    refs = list(refs)
    take = lambda n: [refs.pop(0) for _ in range(n)]
    list_ref, col_ref, tgt_ref, a_hbm = take(4)
    p_hbm = take(cfg["sources"])
    if not first:
        (pt_hbm,) = take(1)
    acc_in = take(cfg["sums"])
    out_refs = take(2 if first or last else 1)
    p_vmem, pt, a_rows, acc = take(4)
    aps = take(UNROLL)
    a_sem, sem, out_sem = take(3)
    stages = take(2 if last else 0)
    late = take(len(acc_in) if cfg["late"] else 0)

    me = lax.axis_index("blk").astype(jnp.int32)
    rank = lax.axis_index("grp").astype(jnp.int32)
    chip, core = rank >> 1, rank & 1

    def a_copy(i):
        to = a_rows.at[pl.ds(i * nonzeros, nonzeros)]
        return pltpu.make_async_copy(a_hbm.at[i], to, a_sem.at[i])

    def start_row(i, _):
        a_copy(i).start()
        return 0

    def wait_row(i, _):
        a_copy(i).wait()

        @pl.when(i + AHEAD < rows)
        def _():
            a_copy(i + AHEAD).start()

        return 0

    p_copies, at = [], 0
    for s, source in enumerate(p_hbm):
        to = p_vmem.at[pl.ds(at, source.shape[0]), pl.ds(0, 3)]
        p_copies.append(pltpu.make_async_copy(source, to, sem.at[s]))
        at += source.shape[0]
    others = []
    if not first:
        others.append(pltpu.make_async_copy(pt_hbm, pt, sem.at[cfg["sources"]]))
    sums = [
        pltpu.make_async_copy(source, to, sem.at[cfg["sources"] + 1 + s])
        for s, (source, to) in enumerate(zip(acc_in, late or [acc]))
    ]
    for copy in p_copies + others + ([] if late else sums):
        copy.start()
    lax.fori_loop(0, AHEAD, start_row, 0)

    a_rows[rows * nonzeros] = jnp.zeros((width, width), a_rows.dtype)
    if late or not acc_in:

        def clear(s, _):
            for x in range(8):
                acc[s * 8 + x] = jnp.zeros((width, LANES), acc.dtype)
            return 0

        lax.fori_loop(0, slots // 8, clear, 0)
    for copy in p_copies:
        copy.wait()

    def unpack(q, _):
        for x in range(2):
            parts = [p_vmem[q * 2 + x, t] for t in range(3)]
            p_vmem[q * 2 + x, 3, :, :width] = unpack_last(parts, width)
        return 0

    lax.fori_loop(0, at // 2, unpack, 0)
    if first:

        def transpose(q, _):
            for x in range(4):
                block = p_vmem[q, x].T[:width]
                n = x % per_row
                pt[q * (4 // per_row) + x // per_row, n * width : (n + 1) * width, :] = block
            return 0

        lax.fori_loop(0, at, transpose, 0)
    for copy in others + ([] if late else sums):
        copy.wait()
    if late:
        for copy in sums:
            copy.start()

    scale = 65536 // rows + 1
    assert all((j * scale) >> 16 == j // rows for j in range(rows * members))

    def p_block(i, k):
        j = col_ref[jnp.minimum(i, rows - 1), k]
        member = (j * scale) >> 16
        place = ((member ^ me) - cfg["from"]) * rows + j - member * rows
        return jnp.where(i < rows, place, 0)

    def first_product(g, u):
        w = list_ref[phase, g * UNROLL + u]
        j = p_block(w >> 5, w & 31)
        right = jnp.concatenate(
            [p_vmem[j >> 1, (j & 1) * 2 + m] for m in range(per_row)], axis=1
        )
        left = a_rows[(w >> 5) * nonzeros + (w & 31)]
        return jnp.dot(left, right, preferred_element_type=jnp.float32)

    def second_product(u, i):
        return jnp.dot(pt[i], aps[u][...], preferred_element_type=jnp.float32)

    def entry(g, u):
        v = list_ref[phase, g * UNROLL + u]
        return jnp.minimum(v >> 5, rows - 1), v & 31

    def keep(u, ap):
        aps[u][...] = ap.astype(jnp.bfloat16)

    def collect(i, k, partial):
        for n in range(per_row):
            for m in range(per_row):
                s = tgt_ref[i, n * nonzeros * per_row + k * per_row + m]
                acc[s] = acc[s] + partial[
                    n * width : (n + 1) * width, m * LANES : (m + 1) * LANES
                ]

    def rows_for(g, ready):
        need = jnp.minimum((list_ref[phase, (g + 1) * UNROLL - 1] >> 5) + 1, rows)
        lax.fori_loop(ready, need, wait_row, 0)
        return jnp.maximum(ready, need)

    def turn(carry):
        g, ready = carry
        ready = rows_for(g + 1, ready)
        held = None
        for u in range(UNROLL):
            i, k = entry(g, u)
            made = u, i, k, second_product(u, i), first_product(g + 1, u)
            if held is not None:
                keep(held[0], held[4])
                collect(*held[1:4])
            held = made
        keep(held[0], held[4])
        collect(*held[1:4])
        return g + 1, ready

    ready = rows_for(0, jnp.int32(0))
    for u in range(UNROLL):
        keep(u, first_product(0, u))
    g, ready = lax.while_loop(
        lambda c: list_ref[phase, (c[0] + 1) * UNROLL] < rows * 32, turn, (jnp.int32(0), ready)
    )
    for u in range(UNROLL):
        i, k = entry(g, u)
        collect(i, k, second_product(u, i))
    lax.fori_loop(ready, rows, wait_row, 0)
    if late:
        for copy in sums:
            copy.wait()

    def total(s):
        value = acc[s]
        for extra in late:
            value = value + extra[s]
        return value

    if last:

        def emit(rz, _):
            for rc in range(2):
                for r in range(members):
                    s = ((chip ^ rz) * 2 + (core ^ rc)) * (OWN * members) + (me ^ r) * OWN
                    packed = pack_four([total(s + x) for x in range(OWN)], width)
                    for t in range(3):
                        stages[rc][rz, r, t] = packed[t].astype(stages[rc].dtype)
                copy = pltpu.make_async_copy(stages[rc].at[rz], out_refs[rc].at[rz], out_sem.at[rc])
                copy.start()
            return 0

        lax.fori_loop(0, groups // 2, emit, 0)
        for rc in range(2):
            pltpu.make_async_copy(stages[rc], out_refs[rc], out_sem.at[rc]).wait()
    else:
        outs = [pltpu.make_async_copy(acc, out_refs[0], out_sem.at[0])]
        if first:
            outs.append(pltpu.make_async_copy(pt, out_refs[1], out_sem.at[1]))
        for copy in outs:
            copy.start()
        for copy in outs:
            copy.wait()


def work(cfg, tables, a_rows, packed, pt=None, sums=()):
    width, rows, nonzeros, per_row = cfg["width"], cfg["rows"], cfg["nonzeros"], cfg["per_row"]
    slots, members, groups = cfg["slots"], cfg["members"], cfg["groups"]
    late = cfg["last"] and cfg["late"]
    cfg = dict(cfg, sources=len(packed), sums=len(sums), late=late)
    quads = sum(x.shape[0] for x in packed)
    operands = [a_rows, *packed] + ([] if cfg["first"] else [pt]) + list(sums)
    pt_shape = (rows, per_row * width, width)
    stages = []
    if cfg["last"]:
        whole = (groups // 2, members, 3, width, LANES)
        shapes = [jax.ShapeDtypeStruct(whole, jnp.float32), jax.ShapeDtypeStruct(whole, jnp.bfloat16)]
        stages = [pltpu.VMEM(x.shape, x.dtype) for x in shapes]
    else:
        shapes = [jax.ShapeDtypeStruct((slots, width, LANES), jnp.float32)]
        if cfg["first"]:
            shapes.append(jax.ShapeDtypeStruct(pt_shape, jnp.bfloat16))
    return pl.pallas_call(
        functools.partial(work_kernel, cfg),
        grid_spec=pltpu.PrefetchScalarGridSpec(
            num_scalar_prefetch=3,
            grid=(),
            in_specs=[HBM] * len(operands),
            out_specs=[HBM] * len(shapes),
            scratch_shapes=[
                pltpu.VMEM((quads, 4, width, LANES), jnp.bfloat16),
                pltpu.VMEM(pt_shape, jnp.bfloat16),
                pltpu.VMEM((rows * nonzeros + 1, width, width), jnp.bfloat16),
                pltpu.VMEM((slots, width, LANES), jnp.float32),
            ]
            + [pltpu.VMEM((width, per_row * LANES), jnp.bfloat16)] * UNROLL
            + [
                pltpu.SemaphoreType.DMA((rows,)),
                pltpu.SemaphoreType.DMA((len(packed) + 1 + len(sums),)),
                pltpu.SemaphoreType.DMA((2,)),
            ]
            + stages
            + [pltpu.VMEM((slots, width, LANES), jnp.float32)] * (len(sums) if late else 0),
        ),
        out_shape=shapes,
        compiler_params=pltpu.CompilerParams(vmem_limit_bytes=VMEM_LIMIT),
        cost_estimate=pl.CostEstimate(
            flops=4 * rows * nonzeros * width * width * width,
            bytes_accessed=20_000_000,
            transcendentals=0,
        ),
        name="work_%d" % cfg["phase"],
    )(*tables, *operands)


def make_lists(columns, me, phase_of):
    rows, nonzeros = columns.shape
    entries = rows * nonzeros
    phases = max(phase_of) + 1
    list_len = (-(-entries // UNROLL) + 1) * UNROLL
    relative = (columns.reshape(-1) // rows) ^ me
    flat = sum(jnp.where(relative == r, p, 0) for r, p in enumerate(phase_of))
    order = jnp.arange(entries, dtype=jnp.int32)
    before = (flat[None, :] == flat[:, None]) & (order[None, :] < order[:, None])
    position = flat * list_len + jnp.sum(before.astype(jnp.int32), axis=1)
    value = (order // nonzeros) * 32 + order % nonzeros
    none = rows * 32
    x = jnp.arange(phases * list_len, dtype=jnp.int32).reshape(phases, list_len)
    found = jnp.where(position[:, None, None] == x[None], (value - none)[:, None, None], 0)
    return none + jnp.sum(found, axis=0)


def shards(a_blocks, col_index, prolong, target):
    rows, nonzeros = a_blocks.shape[1:3]
    per_row = prolong.shape[2]
    width = a_blocks.shape[-1]
    groups = lax.axis_size("grp")
    members = lax.axis_size("blk")
    chips = groups // 2
    slots = groups * OWN * members
    f32, bf16 = jnp.float32, jnp.bfloat16
    me = lax.axis_index("blk").astype(jnp.int32)

    def exchange(x, r, axis="blk", size=members):
        return lax.ppermute(x, axis, [(d, d ^ r) for d in range(size)])

    if members == 4:
        sources = [[0], [1, 2], [3]]
    else:
        sources = [[0]] + [list(range(r, min(r + 3, members))) for r in range(1, members, 3)]
    phases = len(sources)
    phase_of = [p for p in range(phases) for _ in sources[p]]

    own = pack_prolong(prolong)
    direct = range(1, 3 if members == 4 else members)
    packed = {0: own, **{r: [exchange(x, r) for x in own] for r in direct}}
    lists = make_lists(col_index[0], me, phase_of)
    cfg = dict(
        width=width, rows=rows, nonzeros=nonzeros, per_row=per_row, slots=slots,
        members=members, groups=groups, late=slots <= 128,
    )
    pt, sums = None, []
    for p in range(phases):
        last = p == phases - 1
        use = [x for r in sources[p] for x in packed[r]]
        before = (sums if last else []) if cfg["late"] else sums[-1:]
        outs = work(
            {**cfg, "phase": p, "first": p == 0, "last": last, "from": sources[p][0]},
            (lists, col_index[0], target[0]), a_blocks[0], use, pt, before,
        )
        sums = sums + [outs[0]]
        if p == 0:
            pt = outs[1]
            if members == 4:
                near, _ = lax.optimization_barrier((packed[1] + packed[2], outs[0]))
                packed = {0: own, 1: near[:2], 2: near[2:]}
                packed[3] = [exchange(near[0], 2), exchange(near[3], 1)]

    keep, give = outs
    total = keep + exchange(give, 1, "grp", groups).astype(f32)
    half = width // 3 * 2
    one, two = total[..., :half, :], total[..., half:, :]
    got = [exchange(one[:, r].astype(bf16), r) for r in range(1, members)]
    sent = [exchange(two[r].astype(bf16), 2 * r, "grp", groups) for r in range(1, chips)]
    got, sent = lax.optimization_barrier((got, sent))
    one, two = one[:, 0], two[0]
    for part in got:
        one = one + part.astype(f32)
    for part in sent:
        two = two + part.astype(f32)
    mine, other = one[0], two[0]
    for r in range(1, chips):
        mine = mine + exchange(one[r].astype(bf16), 2 * r, "grp", groups).astype(f32)
    for r in range(1, members):
        other = other + exchange(two[r].astype(bf16), r).astype(f32)
    mine = jnp.concatenate([mine, other], axis=1)
    fourth = unpack_last([mine[t] for t in range(3)], width)
    return jnp.concatenate([mine[:, :, :width], fourth[None]])[None]


def solution(mesh):
    return jax.shard_map(
        shards,
        mesh=mesh,
        in_specs=(
            P("grp", "blk", None, None, None),
            P("grp", "blk", None),
            P("grp", "blk", None, None, None),
            P("grp", "blk", None),
        ),
        out_specs=P("grp", "blk", None, None),
        check_vma=False,
    )
```

time: 114 us -> 106 us (0.930)
  Pallas kernels: 63.7 us -> 60.1 us
  local copies, waits for them, and re-layouts: 3.28 us -> 0.54 us
  other arithmetic: 8.71 us -> 6.25 us
  waiting for transfers between devices: 12.5 us -> 14.8 us
  starting transfers between devices: 25.7 us -> 24.5 us
    add x4 -> x2, other arithmetic: 3.34 us -> 0.61 us  [the longest x1 0.6 us: make_lists(): return none + jnp.sum(found, axis=0)]
    slice x2 -> x0, local copies, waits for them, and re-layouts: 2.7 us -> none  [shards(): packed = [[own], [x, y], [exchange(x[:half], 2), exchange(y[half:], 1)]]]
    pallas_call x3, Pallas kernels: 60.1 us -> 57.9 us  [work(): pl.pallas_call(functools.partial(work_kernel, cfg), grid_spec=pltpu.Prefe...]
    ppermute x17 -> x19, waiting for transfers between devices: 12.5 us -> 14.8 us  [exchange(): return lax.ppermute(x, axis, [(d, d ^ r) for d in range(size)])]
    another operation x2 -> x4, other arithmetic: 0.16 us -> 2.3 us
    neg x1 -> x0, other arithmetic: 1.95 us -> none  [make_lists(): info = jnp.concatenate([-(-counts // UNROLL), jnp.stack(place)])]
    pallas_call x1, Pallas kernels: 3.56 us -> 2.22 us  [pack_prolong(): pl.pallas_call(pack_kernel, in_specs=[HBM], out_specs=[HBM] * 2, out_shap...]
    ppermute x17 -> x19, starting transfers between devices: 25.7 us -> 24.5 us  [exchange(): return lax.ppermute(x, axis, [(d, d ^ r) for d in range(size)])]
  transfers between devices with their start and end apart: 17 -> 19, of which waited for: 5 -> 8; matrix products, arithmetic and copies ran while one was open for 5% -> 3% of each run, Pallas kernels for 38% -> 38%
where the time goes in v3:
time: 106 us
  Pallas kernels  60.1 us (57%)
  starting transfers between devices  24.5 us (23%)
  waiting for transfers between devices  14.8 us (14%)
  other arithmetic  6.25 us (6%)
    pallas_call x3, Pallas kernels, work(): pl.pallas_call(functools.partial(work_kernel, cfg), grid_spec=pltpu.Prefe...  57.9 us
    ppermute x19, starting transfers between devices, exchange(): return lax.ppermute(x, axis, [(d, d ^ r) for d in range(size)])  24.5 us
    ppermute x19, waiting for transfers between devices, exchange(): return lax.ppermute(x, axis, [(d, d ^ r) for d in range(size)])  14.8 us
    another operation x3, other arithmetic  2.3 us
    pallas_call x1, Pallas kernels, pack_prolong(): pl.pallas_call(pack_kernel, in_specs=[HBM], out_specs=[HBM] * 2, out_shap...  2.22 us
  transfers between devices with their start and end apart: 19, of which 8 were waited for; matrix products, arithmetic and copies ran while one was open for 3% of the time, Pallas kernels for 38%

profile of v3, /device:TPU:0, one launch (start us, length us, event | category | flops | bytes accessed | tf_op | source)
XLA Modules:
  0.0 106.4 jit_solution(9933844912935795980)
XLA Ops:
  0.0 2.2 %pack_prolong.1 = (bf16[6,3,96,128]{3,2,1,0:T(8,128)(2,1)}, bf16[6,3,96,128]{3,2,1,0:T(8,128)(2,1)}) custom-call(bf16[12,4,96,96]{3,2,1,0:T(8,128)(2,1)} %bitcast.81), custom_call_target="tpu_custom_call" | custom-call | tf_op jit(solution)/shard_map/pack_prolong/pallas_call | solution.py:60
  2.2 3.0 %collective-permute-start.2 = (bf16[6,3,96,128]{3,2,1,0:T(8,128)(2,1)}, bf16[6,3,96,128]{3,2,1,0:T(8,128)(2,1)S(1)}, u32[]{:S(2)}, u32[]{:S(2)}) collective-permute-start(bf16[6,3,96,128]{3,2,1,0:T(8,128)(2,1)} %get-tuple-element.21.refs_4_), channel_id=1, source_target_pairs={{0,16},{8,24},{16,0},{24,8},{1,17},{9,25},{17,1},{25,9},{2,18},{10... | collective-permute-start | bytes 1327112 | tf_op jit(solution)/shard_map/ppermute | solution.py:347
  5.3 1.5 %collective-permute-start = (bf16[6,3,96,128]{3,2,1,0:T(8,128)(2,1)}, bf16[6,3,96,128]{3,2,1,0:T(8,128)(2,1)S(1)}, u32[]{:S(2)}, u32[]{:S(2)}) collective-permute-start(bf16[6,3,96,128]{3,2,1,0:T(8,128)(2,1)} %get-tuple-element.21.refs_4_), channel_id=1, source_target_pairs={{0,8},{8,0},{16,24},{24,16},{1,9},{9,1},{17,25},{25,17},{2,10},{10... | collective-permute-start | bytes 1327112 | tf_op jit(solution)/shard_map/ppermute | solution.py:347
  7.4 0.7 fusion.19
  8.1 0.7 broadcast_divide_fusion
  10.7 22.8 %work_0.1 = (f32[128,96,128]{2,1,0:T(8,128)}, bf16[24,192,96]{2,1,0:T(8,128)(2,1)}) custom-call(s32[3,672]{1,0:T(4,128)} %broadcast_add_fusion.refs_0_, s32[24,27]{1,0:T(8,128)} %bitcast.82, s32[24,108]{1,0:T(8,128)} %bitcast.85, bf16[24,27,96,96]{3,2,1,0:T(8,128)(2,1)} %bitcast.78, bf16[6,3,96,128]{3,2,1,0:T(8,128)(2,1)} %get-tuple-element.21.refs_4_, ...), custom_call_target="tpu_custom_call" | custom-call | flops 2293235712 | bytes 20000000 | tf_op jit(solution)/shard_map/work_0/pallas_call | solution.py:285
  34.0 3.1 %collective-permute-start.5 = (bf16[6,3,96,128]{3,2,1,0:T(8,128)(2,1)}, bf16[6,3,96,128]{3,2,1,0:T(8,128)(2,1)}, u32[]{:S(2)}, u32[]{:S(2)}) collective-permute-start(bf16[6,3,96,128]{3,2,1,0:T(8,128)(2,1)} %collective-permute-done.3.refs_7_), channel_id=1, source_target_pairs={{0,8},{8,0},{16,24},{24,16},{1,9},{9,1},{17,25},{25,17},{2,10},{10... | collective-permute-start | bytes 1327112 | tf_op jit(solution)/shard_map/ppermute | solution.py:347
  37.1 17.7 %work_1.1.refs_8_ = f32[128,96,128]{2,1,0:T(8,128)} custom-call(s32[3,672]{1,0:T(4,128)} %broadcast_add_fusion.refs_0_, s32[24,27]{1,0:T(8,128)} %bitcast.83, s32[24,108]{1,0:T(8,128)} %bitcast.86, bf16[24,27,96,96]{3,2,1,0:T(8,128)(2,1)} %bitcast.79, bf16[6,3,96,128]{3,2,1,0:T(8,128)(2,1)} %copy-done.1, ...), custom_call_target="tpu_custom_call" | custom-call | flops 2293235712 | bytes 20000000 | tf_op jit(solution)/shard_map/work_1/pallas_call | solution.py:285
  54.8 17.4 %work_2.1 = (f32[4,4,3,96,128]{4,3,2,1,0:T(8,128)}, bf16[4,4,3,96,128]{4,3,2,1,0:T(8,128)(2,1)}) custom-call(s32[3,672]{1,0:T(4,128)} %broadcast_add_fusion.refs_0_, s32[24,27]{1,0:T(8,128)} %bitcast.84, s32[24,108]{1,0:T(8,128)} %bitcast.87, bf16[24,27,96,96]{3,2,1,0:T(8,128)(2,1)} %bitcast.80, bf16[6,3,96,128]{3,2,1,0:T(8,128)(2,1)} %collective-permute-done.4.refs_4_, ...), custom_call_target="tpu_custom_call" | custom-call | flops 2293235712 | bytes 20000000 | tf_op jit(solution)/shard_map/work_2/pallas_call | solution.py:285
  72.3 3.0 %collective-permute-done.6 = bf16[4,4,3,96,128]{4,3,2,1,0:T(8,128)(2,1)S(1)} collective-permute-done((bf16[4,4,3,96,128]{4,3,2,1,0:T(8,128)(2,1)}, bf16[4,4,3,96,128]{4,3,2,1,0:T(8,128)(2,1)S(1)}, u32[]{:S(2)}, u32[]{:S(2)}) %collective-permute-start.6) | collective-permute-done | bytes 1179680 | tf_op jit(solution)/shard_map/ppermute | solution.py:347
  75.3 2.1 %fusion.35 = (bf16[4,4,3,96,128]{4,3,2,1,0:T(8,128)(2,1)S(1)}, f32[4,4,3,96,128]{4,3,2,1,0:T(8,128)S(1)}) fusion(f32[4,4,3,96,128]{4,3,2,1,0:T(8,128)} %get-tuple-element.29, bf16[4,4,3,96,128]{4,3,2,1,0:T(8,128)(2,1)S(1)} %collective-permute-done.6), kind=kLoop, calls=%fused_computation.74 | loop fusion | flops 1769472 | bytes 7077888 | tf_op jit(solution)/shard_map/convert.11
  77.6 4.5 %collective-permute-start.12 = (bf16[4,3,32,128]{3,2,1,0:T(8,128)(2,1)S(1)}, bf16[4,3,32,128]{3,2,1,0:T(8,128)(2,1)S(1)}, u32[]{:S(2)}, u32[]{:S(2)}) collective-permute-start(bf16[4,3,32,128]{3,2,1,0:T(8,128)(2,1)S(1)} %get-tuple-element.43), channel_id=1, source_target_pairs={{0,6},{1,7},{2,4},{3,5},{4,2},{5,3},{6,0},{7,1},{8,14},{9,15},{10,... | collective-permute-start | bytes 294920 | tf_op jit(solution)/shard_map/ppermute | solution.py:347
  82.1 1.3 %collective-permute-start.9 = (bf16[4,3,64,128]{3,2,1,0:T(8,128)(2,1)S(1)}, bf16[4,3,64,128]{3,2,1,0:T(8,128)(2,1)S(1)}, u32[]{:S(2)}, u32[]{:S(2)}) collective-permute-start(bf16[4,3,64,128]{3,2,1,0:T(8,128)(2,1)S(1)} %get-tuple-element.46), channel_id=1, source_target_pairs={{0,24},{8,16},{16,8},{24,0},{1,25},{9,17},{17,9},{25,1},{2,26},{10... | collective-permute-start | bytes 589832 | tf_op jit(solution)/shard_map/ppermute | solution.py:347
  84.0 1.6 %collective-permute-start.8 = (bf16[4,3,64,128]{3,2,1,0:T(8,128)(2,1)S(1)}, bf16[4,3,64,128]{3,2,1,0:T(8,128)(2,1)S(1)}, u32[]{:S(2)}, u32[]{:S(2)}) collective-permute-start(bf16[4,3,64,128]{3,2,1,0:T(8,128)(2,1)S(1)} %get-tuple-element.48), channel_id=1, source_target_pairs={{0,16},{8,24},{16,0},{24,8},{1,17},{9,25},{17,1},{25,9},{2,18},{10... | collective-permute-start | bytes 589832 | tf_op jit(solution)/shard_map/ppermute | solution.py:347
  86.2 5.3 %collective-permute-done.11 = bf16[4,3,32,128]{3,2,1,0:T(8,128)(2,1)S(1)} collective-permute-done((bf16[4,3,32,128]{3,2,1,0:T(8,128)(2,1)S(1)}, bf16[4,3,32,128]{3,2,1,0:T(8,128)(2,1)S(1)}, u32[]{:S(2)}, u32[]{:S(2)}) %collective-permute-start.11) | collective-permute-done | bytes 98336 | tf_op jit(solution)/shard_map/ppermute | solution.py:347
  91.5 0.7 collective-permute-done.10
  92.2 0.9 collective-permute-done.7
  93.9 2.0 %collective-permute-start.16 = (bf16[3,32,128]{2,1,0:T(8,128)(2,1)S(1)}, bf16[3,32,128]{2,1,0:T(8,128)(2,1)S(1)}, u32[]{:S(2)}, u32[]{:S(2)}) collective-permute-start(bf16[3,32,128]{2,1,0:T(8,128)(2,1)S(1)} %get-tuple-element.55), channel_id=1, source_target_pairs={{0,8},{8,0},{16,24},{24,16},{1,9},{9,1},{17,25},{25,17},{2,10},{10... | collective-permute-start | bytes 73736 | tf_op jit(solution)/shard_map/ppermute | solution.py:347
  96.2 1.3 %collective-permute-start.17 = (bf16[3,32,128]{2,1,0:T(8,128)(2,1)S(1)}, bf16[3,32,128]{2,1,0:T(8,128)(2,1)S(1)}, u32[]{:S(2)}, u32[]{:S(2)}) collective-permute-start(bf16[3,32,128]{2,1,0:T(8,128)(2,1)S(1)} %get-tuple-element.57), channel_id=1, source_target_pairs={{0,16},{8,24},{16,0},{24,8},{1,17},{9,25},{17,1},{25,9},{2,18},{10... | collective-permute-start | bytes 73736 | tf_op jit(solution)/shard_map/ppermute | solution.py:347
  97.7 2.3 %collective-permute-start.15 = (bf16[3,64,128]{2,1,0:T(8,128)(2,1)S(1)}, bf16[3,64,128]{2,1,0:T(8,128)(2,1)S(1)}, u32[]{:S(2)}, u32[]{:S(2)}) collective-permute-start(bf16[3,64,128]{2,1,0:T(8,128)(2,1)S(1)} %get-tuple-element.50), channel_id=1, source_target_pairs={{0,6},{1,7},{2,4},{3,5},{4,2},{5,3},{6,0},{7,1},{8,14},{9,15},{10,... | collective-permute-start | bytes 147464 | tf_op jit(solution)/shard_map/ppermute | solution.py:347
  100.0 1.1 %collective-permute-start.14 = (bf16[3,64,128]{2,1,0:T(8,128)(2,1)S(1)}, bf16[3,64,128]{2,1,0:T(8,128)(2,1)S(1)}, u32[]{:S(2)}, u32[]{:S(2)}) collective-permute-start(bf16[3,64,128]{2,1,0:T(8,128)(2,1)S(1)} %get-tuple-element.51), channel_id=1, source_target_pairs={{0,4},{1,5},{2,6},{3,7},{4,0},{5,1},{6,2},{7,3},{8,12},{9,13},{10,... | collective-permute-start | bytes 147464 | tf_op jit(solution)/shard_map/ppermute | solution.py:347
  101.2 1.6 %collective-permute-done.13 = bf16[3,64,128]{2,1,0:T(8,128)(2,1)S(1)} collective-permute-done((bf16[3,64,128]{2,1,0:T(8,128)(2,1)S(1)}, bf16[3,64,128]{2,1,0:T(8,128)(2,1)S(1)}, u32[]{:S(2)}, u32[]{:S(2)}) %collective-permute-start.13) | collective-permute-done | bytes 49184 | tf_op jit(solution)/shard_map/ppermute | solution.py:347
  102.8 0.9 collective-permute-done.15
  103.8 1.5 %collective-permute-done.14 = bf16[3,64,128]{2,1,0:T(8,128)(2,1)S(1)} collective-permute-done((bf16[3,64,128]{2,1,0:T(8,128)(2,1)S(1)}, bf16[3,64,128]{2,1,0:T(8,128)(2,1)S(1)}, u32[]{:S(2)}, u32[]{:S(2)}) %collective-permute-start.14) | collective-permute-done | bytes 49184 | tf_op jit(solution)/shard_map/ppermute | solution.py:347
  (48 shorter events, 6.6 us)
Async XLA Ops:
  2.2 31.2 %collective-permute-start.2 = (bf16[6,3,96,128]{3,2,1,0:T(8,128)(2,1)}, bf16[6,3,96,128]{3,2,1,0:T(8,128)(2,1)S(1)}, u32[]{:S(2)}, u32[]{:S(2)}) collective-permute-start(bf16[6,3,96,128]{3,2,1,0:T(8,128)(2,1)} %get-tuple-element.21.refs_4_), channel_id=1, source_target_pairs={{0,16},{8,24},{16,0},{24,8},{1,17},{9,25},{17,1},{25,9},{2,18},{10... | collective-permute-start | bytes 1327112 | tf_op jit(solution)/shard_map/ppermute | solution.py:347
  5.3 28.2 %collective-permute-start = (bf16[6,3,96,128]{3,2,1,0:T(8,128)(2,1)}, bf16[6,3,96,128]{3,2,1,0:T(8,128)(2,1)S(1)}, u32[]{:S(2)}, u32[]{:S(2)}) collective-permute-start(bf16[6,3,96,128]{3,2,1,0:T(8,128)(2,1)} %get-tuple-element.21.refs_4_), channel_id=1, source_target_pairs={{0,8},{8,0},{16,24},{24,16},{1,9},{9,1},{17,25},{25,17},{2,10},{10... | collective-permute-start | bytes 1327112 | tf_op jit(solution)/shard_map/ppermute | solution.py:347
  6.8 26.8 %collective-permute-start.3 = (bf16[6,3,96,128]{3,2,1,0:T(8,128)(2,1)}, bf16[6,3,96,128]{3,2,1,0:T(8,128)(2,1)}, u32[]{:S(2)}, u32[]{:S(2)}) collective-permute-start(bf16[6,3,96,128]{3,2,1,0:T(8,128)(2,1)} %get-tuple-element.22.refs_5_), channel_id=1, source_target_pairs={{0,16},{8,24},{16,0},{24,8},{1,17},{9,25},{17,1},{25,9},{2,18},{10... | collective-permute-start | bytes 1327112 | tf_op jit(solution)/shard_map/ppermute | solution.py:347
  7.3 26.3 %collective-permute-start.1 = (bf16[6,3,96,128]{3,2,1,0:T(8,128)(2,1)}, bf16[6,3,96,128]{3,2,1,0:T(8,128)(2,1)}, u32[]{:S(2)}, u32[]{:S(2)}) collective-permute-start(bf16[6,3,96,128]{3,2,1,0:T(8,128)(2,1)} %get-tuple-element.22.refs_5_), channel_id=1, source_target_pairs={{0,8},{8,0},{16,24},{24,16},{1,9},{9,1},{17,25},{25,17},{2,10},{10... | collective-permute-start | bytes 1327112 | tf_op jit(solution)/shard_map/ppermute | solution.py:347
  33.5 3.6 %copy-start = (bf16[6,3,96,128]{3,2,1,0:T(8,128)(2,1)}, bf16[6,3,96,128]{3,2,1,0:T(8,128)(2,1)S(1)}, u32[]{:S(2)}) copy-start(bf16[6,3,96,128]{3,2,1,0:T(8,128)(2,1)S(1)} %collective-permute-done.2.refs_6_) | copy-start | bytes 1327108
  33.5 3.6 %copy-start.1 = (bf16[6,3,96,128]{3,2,1,0:T(8,128)(2,1)}, bf16[6,3,96,128]{3,2,1,0:T(8,128)(2,1)S(1)}, u32[]{:S(2)}) copy-start(bf16[6,3,96,128]{3,2,1,0:T(8,128)(2,1)S(1)} %collective-permute-done.refs_4_) | copy-start | bytes 1327108
  33.5 21.2 %collective-permute-start.4 = (bf16[6,3,96,128]{3,2,1,0:T(8,128)(2,1)S(1)}, bf16[6,3,96,128]{3,2,1,0:T(8,128)(2,1)}, u32[]{:S(2)}, u32[]{:S(2)}) collective-permute-start(bf16[6,3,96,128]{3,2,1,0:T(8,128)(2,1)S(1)} %collective-permute-done.refs_4_), channel_id=1, source_target_pairs={{0,16},{8,24},{16,0},{24,8},{1,17},{9,25},{17,1},{25,9},{2,18},{10... | collective-permute-start | bytes 1327112 | tf_op jit(solution)/shard_map/ppermute | solution.py:347
  34.0 20.8 %collective-permute-start.5 = (bf16[6,3,96,128]{3,2,1,0:T(8,128)(2,1)}, bf16[6,3,96,128]{3,2,1,0:T(8,128)(2,1)}, u32[]{:S(2)}, u32[]{:S(2)}) collective-permute-start(bf16[6,3,96,128]{3,2,1,0:T(8,128)(2,1)} %collective-permute-done.3.refs_7_), channel_id=1, source_target_pairs={{0,8},{8,0},{16,24},{24,16},{1,9},{9,1},{17,25},{25,17},{2,10},{10... | collective-permute-start | bytes 1327112 | tf_op jit(solution)/shard_map/ppermute | solution.py:347
  72.2 3.1 %collective-permute-start.6 = (bf16[4,4,3,96,128]{4,3,2,1,0:T(8,128)(2,1)}, bf16[4,4,3,96,128]{4,3,2,1,0:T(8,128)(2,1)S(1)}, u32[]{:S(2)}, u32[]{:S(2)}) collective-permute-start(bf16[4,4,3,96,128]{4,3,2,1,0:T(8,128)(2,1)} %get-tuple-element.30), channel_id=1, source_target_pairs={{0,1},{1,0},{2,3},{3,2},{4,5},{5,4},{6,7},{7,6},{8,9},{9,8},{10,11... | collective-permute-start | bytes 3538952 | tf_op jit(solution)/shard_map/ppermute | solution.py:347
  77.6 8.0 %collective-permute-start.12 = (bf16[4,3,32,128]{3,2,1,0:T(8,128)(2,1)S(1)}, bf16[4,3,32,128]{3,2,1,0:T(8,128)(2,1)S(1)}, u32[]{:S(2)}, u32[]{:S(2)}) collective-permute-start(bf16[4,3,32,128]{3,2,1,0:T(8,128)(2,1)S(1)} %get-tuple-element.43), channel_id=1, source_target_pairs={{0,6},{1,7},{2,4},{3,5},{4,2},{5,3},{6,0},{7,1},{8,14},{9,15},{10,... | collective-permute-start | bytes 294920 | tf_op jit(solution)/shard_map/ppermute | solution.py:347
  82.1 10.1 %collective-permute-start.9 = (bf16[4,3,64,128]{3,2,1,0:T(8,128)(2,1)S(1)}, bf16[4,3,64,128]{3,2,1,0:T(8,128)(2,1)S(1)}, u32[]{:S(2)}, u32[]{:S(2)}) collective-permute-start(bf16[4,3,64,128]{3,2,1,0:T(8,128)(2,1)S(1)} %get-tuple-element.46), channel_id=1, source_target_pairs={{0,24},{8,16},{16,8},{24,0},{1,25},{9,17},{17,9},{25,1},{2,26},{10... | collective-permute-start | bytes 589832 | tf_op jit(solution)/shard_map/ppermute | solution.py:347
  83.4 9.8 %collective-permute-start.7 = (bf16[4,3,64,128]{3,2,1,0:T(8,128)(2,1)S(1)}, bf16[4,3,64,128]{3,2,1,0:T(8,128)(2,1)S(1)}, u32[]{:S(2)}, u32[]{:S(2)}) collective-permute-start(bf16[4,3,64,128]{3,2,1,0:T(8,128)(2,1)S(1)} %get-tuple-element.47), channel_id=1, source_target_pairs={{0,8},{8,0},{16,24},{24,16},{1,9},{9,1},{17,25},{25,17},{2,10},{10... | collective-permute-start | bytes 589832 | tf_op jit(solution)/shard_map/ppermute | solution.py:347
  84.0 9.9 %collective-permute-start.8 = (bf16[4,3,64,128]{3,2,1,0:T(8,128)(2,1)S(1)}, bf16[4,3,64,128]{3,2,1,0:T(8,128)(2,1)S(1)}, u32[]{:S(2)}, u32[]{:S(2)}) collective-permute-start(bf16[4,3,64,128]{3,2,1,0:T(8,128)(2,1)S(1)} %get-tuple-element.48), channel_id=1, source_target_pairs={{0,16},{8,24},{16,0},{24,8},{1,17},{9,25},{17,1},{25,9},{2,18},{10... | collective-permute-start | bytes 589832 | tf_op jit(solution)/shard_map/ppermute | solution.py:347
  85.6 5.9 %collective-permute-start.11 = (bf16[4,3,32,128]{3,2,1,0:T(8,128)(2,1)S(1)}, bf16[4,3,32,128]{3,2,1,0:T(8,128)(2,1)S(1)}, u32[]{:S(2)}, u32[]{:S(2)}) collective-permute-start(bf16[4,3,32,128]{3,2,1,0:T(8,128)(2,1)S(1)} %get-tuple-element.44), channel_id=1, source_target_pairs={{0,4},{1,5},{2,6},{3,7},{4,0},{5,1},{6,2},{7,3},{8,12},{9,13},{10,... | collective-permute-start | bytes 294920 | tf_op jit(solution)/shard_map/ppermute | solution.py:347
  85.6 6.6 %collective-permute-start.10 = (bf16[4,3,32,128]{3,2,1,0:T(8,128)(2,1)S(1)}, bf16[4,3,32,128]{3,2,1,0:T(8,128)(2,1)S(1)}, u32[]{:S(2)}, u32[]{:S(2)}) collective-permute-start(bf16[4,3,32,128]{3,2,1,0:T(8,128)(2,1)S(1)} %get-tuple-element.45), channel_id=1, source_target_pairs={{0,2},{1,3},{2,0},{3,1},{4,6},{5,7},{6,4},{7,5},{8,10},{9,11},{10,... | collective-permute-start | bytes 294920 | tf_op jit(solution)/shard_map/ppermute | solution.py:347
  93.9 6.1 %collective-permute-start.16 = (bf16[3,32,128]{2,1,0:T(8,128)(2,1)S(1)}, bf16[3,32,128]{2,1,0:T(8,128)(2,1)S(1)}, u32[]{:S(2)}, u32[]{:S(2)}) collective-permute-start(bf16[3,32,128]{2,1,0:T(8,128)(2,1)S(1)} %get-tuple-element.55), channel_id=1, source_target_pairs={{0,8},{8,0},{16,24},{24,16},{1,9},{9,1},{17,25},{25,17},{2,10},{10... | collective-permute-start | bytes 73736 | tf_op jit(solution)/shard_map/ppermute | solution.py:347
  95.9 5.3 %collective-permute-start.18 = (bf16[3,32,128]{2,1,0:T(8,128)(2,1)S(1)}, bf16[3,32,128]{2,1,0:T(8,128)(2,1)S(1)}, u32[]{:S(2)}, u32[]{:S(2)}) collective-permute-start(bf16[3,32,128]{2,1,0:T(8,128)(2,1)S(1)} %get-tuple-element.56), channel_id=1, source_target_pairs={{0,24},{8,16},{16,8},{24,0},{1,25},{9,17},{17,9},{25,1},{2,26},{10... | collective-permute-start | bytes 73736 | tf_op jit(solution)/shard_map/ppermute | solution.py:347
  96.2 5.0 %collective-permute-start.17 = (bf16[3,32,128]{2,1,0:T(8,128)(2,1)S(1)}, bf16[3,32,128]{2,1,0:T(8,128)(2,1)S(1)}, u32[]{:S(2)}, u32[]{:S(2)}) collective-permute-start(bf16[3,32,128]{2,1,0:T(8,128)(2,1)S(1)} %get-tuple-element.57), channel_id=1, source_target_pairs={{0,16},{8,24},{16,0},{24,8},{1,17},{9,25},{17,1},{25,9},{2,18},{10... | collective-permute-start | bytes 73736 | tf_op jit(solution)/shard_map/ppermute | solution.py:347
  97.6 5.2 %collective-permute-start.13 = (bf16[3,64,128]{2,1,0:T(8,128)(2,1)S(1)}, bf16[3,64,128]{2,1,0:T(8,128)(2,1)S(1)}, u32[]{:S(2)}, u32[]{:S(2)}) collective-permute-start(bf16[3,64,128]{2,1,0:T(8,128)(2,1)S(1)} %get-tuple-element.49), channel_id=1, source_target_pairs={{0,2},{1,3},{2,0},{3,1},{4,6},{5,7},{6,4},{7,5},{8,10},{9,11},{10,... | collective-permute-start | bytes 147464 | tf_op jit(solution)/shard_map/ppermute | solution.py:347
  97.7 6.1 %collective-permute-start.15 = (bf16[3,64,128]{2,1,0:T(8,128)(2,1)S(1)}, bf16[3,64,128]{2,1,0:T(8,128)(2,1)S(1)}, u32[]{:S(2)}, u32[]{:S(2)}) collective-permute-start(bf16[3,64,128]{2,1,0:T(8,128)(2,1)S(1)} %get-tuple-element.50), channel_id=1, source_target_pairs={{0,6},{1,7},{2,4},{3,5},{4,2},{5,3},{6,0},{7,1},{8,14},{9,15},{10,... | collective-permute-start | bytes 147464 | tf_op jit(solution)/shard_map/ppermute | solution.py:347
  100.0 5.2 %collective-permute-start.14 = (bf16[3,64,128]{2,1,0:T(8,128)(2,1)S(1)}, bf16[3,64,128]{2,1,0:T(8,128)(2,1)S(1)}, u32[]{:S(2)}, u32[]{:S(2)}) collective-permute-start(bf16[3,64,128]{2,1,0:T(8,128)(2,1)S(1)} %get-tuple-element.51), channel_id=1, source_target_pairs={{0,4},{1,5},{2,6},{3,7},{4,0},{5,1},{6,2},{7,3},{8,12},{9,13},{10,... | collective-permute-start | bytes 147464 | tf_op jit(solution)/shard_map/ppermute | solution.py:347

commit v4 on v3

--- a/solution.py
+++ b/solution.py
@@ -10,7 +10,7 @@
 OWN = 4
 UNROLL = 16
 LANES = 128
-AHEAD = 6
+AHEAD = 12
 VMEM_LIMIT = 63 * 1024 * 1024
 HBM = pl.BlockSpec(memory_space=pl.ANY)
 
@@ -30,17 +30,15 @@
 
 
 def pack_kernel(p_hbm, *refs):
-    outs, (blocks, packed, in_sem, out_sem) = refs[:2], refs[2:]
+    out, blocks, packed, in_sem, out_sem = refs
     width, quads = p_hbm.shape[-1], p_hbm.shape[0]
     steps = in_sem.shape[0]
     size = quads // steps
-    half = steps // 2
     loads, stores = [], []
     for c in range(steps):
         part = pl.ds(c * size, size)
-        to = outs[c // half].at[pl.ds(c % half * size, size)]
         loads.append(pltpu.make_async_copy(p_hbm.at[part], blocks.at[part], in_sem.at[c]))
-        stores.append(pltpu.make_async_copy(packed.at[part], to, out_sem.at[c]))
+        stores.append(pltpu.make_async_copy(packed.at[part], out.at[part], out_sem.at[c]))
         loads[c].start()
     for c in range(steps):
         loads[c].wait()
@@ -60,8 +58,8 @@
     return pl.pallas_call(
         pack_kernel,
         in_specs=[HBM],
-        out_specs=[HBM] * 2,
-        out_shape=[jax.ShapeDtypeStruct((quads // 2, 3, width, LANES), dtype)] * 2,
+        out_specs=HBM,
+        out_shape=jax.ShapeDtypeStruct((quads, 3, width, LANES), dtype),
         scratch_shapes=[
             pltpu.VMEM((quads, 4, width, width), dtype),
             pltpu.VMEM((quads, 3, width, LANES), dtype),
@@ -71,6 +69,12 @@
         compiler_params=pltpu.CompilerParams(vmem_limit_bytes=VMEM_LIMIT),
         name="pack_prolong",
     )(prolong.reshape(quads, 4, width, width))
+
+
+def divider(rows, members):
+    scale = 65536 // rows + 1
+    assert all((x * scale) >> 16 == x // rows for x in range(rows * members))
+    return scale
 
 
 def work_kernel(cfg, *refs):
@@ -96,7 +100,7 @@
     chip, core = rank >> 1, rank & 1
 
     def a_copy(i):
-        to = a_rows.at[pl.ds(i * nonzeros, nonzeros)]
+        to = a_rows.at[pl.ds((i + 1) * nonzeros, nonzeros)]
         return pltpu.make_async_copy(a_hbm.at[i], to, a_sem.at[i])
 
     def start_row(i, _):
@@ -109,6 +113,13 @@
         @pl.when(i + AHEAD < rows)
         def _():
             a_copy(i + AHEAD).start()
+
+        if late:
+
+            @pl.when(i + AHEAD == rows - 1)
+            def _():
+                for copy in sums:
+                    copy.start()
 
         return 0
 
@@ -128,7 +139,7 @@
         copy.start()
     lax.fori_loop(0, AHEAD, start_row, 0)
 
-    a_rows[rows * nonzeros] = jnp.zeros((width, width), a_rows.dtype)
+    a_rows[0] = jnp.zeros((width, width), a_rows.dtype)
     if late or not acc_in:
 
         def clear(s, _):
@@ -159,22 +170,18 @@
         lax.fori_loop(0, at, transpose, 0)
     for copy in others + ([] if late else sums):
         copy.wait()
-    if late:
-        for copy in sums:
-            copy.start()
-
-    scale = 65536 // rows + 1
-    assert all((j * scale) >> 16 == j // rows for j in range(rows * members))
-
-    def p_block(i, k):
-        j = col_ref[jnp.minimum(i, rows - 1), k]
+
+    scale = divider(rows, members)
+
+    def p_block(v):
+        j = col_ref[jnp.maximum((v >> 5) - 1, 0), v & 31]
         member = (j * scale) >> 16
         place = ((member ^ me) - cfg["from"]) * rows + j - member * rows
-        return jnp.where(i < rows, place, 0)
+        return jnp.where(v > 0, place, 0)
 
     def first_product(g, u):
         w = list_ref[phase, g * UNROLL + u]
-        j = p_block(w >> 5, w & 31)
+        j = p_block(w)
         right = jnp.concatenate(
             [p_vmem[j >> 1, (j & 1) * 2 + m] for m in range(per_row)], axis=1
         )
@@ -186,7 +193,7 @@
 
     def entry(g, u):
         v = list_ref[phase, g * UNROLL + u]
-        return jnp.minimum(v >> 5, rows - 1), v & 31
+        return jnp.maximum((v >> 5) - 1, 0), v & 31
 
     def keep(u, ap):
         aps[u][...] = ap.astype(jnp.bfloat16)
@@ -200,7 +207,8 @@
                 ]
 
     def rows_for(g, ready):
-        need = jnp.minimum((list_ref[phase, (g + 1) * UNROLL - 1] >> 5) + 1, rows)
+        v = list_ref[phase, (g + 1) * UNROLL - 1]
+        need = jnp.where(v > 0, v >> 5, rows)
         lax.fori_loop(ready, need, wait_row, 0)
         return jnp.maximum(ready, need)
 
@@ -223,7 +231,7 @@
     for u in range(UNROLL):
         keep(u, first_product(0, u))
     g, ready = lax.while_loop(
-        lambda c: list_ref[phase, (c[0] + 1) * UNROLL] < rows * 32, turn, (jnp.int32(0), ready)
+        lambda c: list_ref[phase, (c[0] + 1) * UNROLL] > 0, turn, (jnp.int32(0), ready)
     )
     for u in range(UNROLL):
         i, k = entry(g, u)
@@ -292,7 +300,7 @@
             scratch_shapes=[
                 pltpu.VMEM((quads, 4, width, LANES), jnp.bfloat16),
                 pltpu.VMEM(pt_shape, jnp.bfloat16),
-                pltpu.VMEM((rows * nonzeros + 1, width, width), jnp.bfloat16),
+                pltpu.VMEM(((rows + 1) * nonzeros, width, width), jnp.bfloat16),
                 pltpu.VMEM((slots, width, LANES), jnp.float32),
             ]
             + [pltpu.VMEM((width, per_row * LANES), jnp.bfloat16)] * UNROLL
@@ -320,16 +328,15 @@
     entries = rows * nonzeros
     phases = max(phase_of) + 1
     list_len = (-(-entries // UNROLL) + 1) * UNROLL
-    relative = (columns.reshape(-1) // rows) ^ me
-    flat = sum(jnp.where(relative == r, p, 0) for r, p in enumerate(phase_of))
+    relative = ((columns * divider(rows, lax.axis_size("blk"))) >> 16) ^ me
+    flat = sum(jnp.where(relative == r, p, 0) for r, p in enumerate(phase_of)).reshape(-1)
     order = jnp.arange(entries, dtype=jnp.int32)
     before = (flat[None, :] == flat[:, None]) & (order[None, :] < order[:, None])
     position = flat * list_len + jnp.sum(before.astype(jnp.int32), axis=1)
-    value = (order // nonzeros) * 32 + order % nonzeros
-    none = rows * 32
+    value = (order // nonzeros + 1) * 32 + order % nonzeros
     x = jnp.arange(phases * list_len, dtype=jnp.int32).reshape(phases, list_len)
-    found = jnp.where(position[:, None, None] == x[None], (value - none)[:, None, None], 0)
-    return none + jnp.sum(found, axis=0)
+    found = jnp.where(position[:, None, None] == x[None], value[:, None, None], 0)
+    return jnp.sum(found, axis=0)
 
 
 def shards(a_blocks, col_index, prolong, target):
@@ -354,8 +361,7 @@
     phase_of = [p for p in range(phases) for _ in sources[p]]
 
     own = pack_prolong(prolong)
-    direct = range(1, 3 if members == 4 else members)
-    packed = {0: own, **{r: [exchange(x, r) for x in own] for r in direct}}
+    packed = [own] + [exchange(own, r) for r in range(1, members)]
     lists = make_lists(col_index[0], me, phase_of)
     cfg = dict(
         width=width, rows=rows, nonzeros=nonzeros, per_row=per_row, slots=slots,
@@ -364,7 +370,7 @@
     pt, sums = None, []
     for p in range(phases):
         last = p == phases - 1
-        use = [x for r in sources[p] for x in packed[r]]
+        use = [packed[r] for r in sources[p]]
         before = (sums if last else []) if cfg["late"] else sums[-1:]
         outs = work(
             {**cfg, "phase": p, "first": p == 0, "last": last, "from": sources[p][0]},
@@ -373,29 +379,17 @@
         sums = sums + [outs[0]]
         if p == 0:
             pt = outs[1]
-            if members == 4:
-                near, _ = lax.optimization_barrier((packed[1] + packed[2], outs[0]))
-                packed = {0: own, 1: near[:2], 2: near[2:]}
-                packed[3] = [exchange(near[0], 2), exchange(near[3], 1)]
 
     keep, give = outs
     total = keep + exchange(give, 1, "grp", groups).astype(f32)
-    half = width // 3 * 2
-    one, two = total[..., :half, :], total[..., half:, :]
-    got = [exchange(one[:, r].astype(bf16), r) for r in range(1, members)]
-    sent = [exchange(two[r].astype(bf16), 2 * r, "grp", groups) for r in range(1, chips)]
-    got, sent = lax.optimization_barrier((got, sent))
-    one, two = one[:, 0], two[0]
+    got = [exchange(total[:, r].astype(bf16), r) for r in range(1, members)]
+    total = total[:, 0]
     for part in got:
-        one = one + part.astype(f32)
-    for part in sent:
-        two = two + part.astype(f32)
-    mine, other = one[0], two[0]
-    for r in range(1, chips):
-        mine = mine + exchange(one[r].astype(bf16), 2 * r, "grp", groups).astype(f32)
-    for r in range(1, members):
-        other = other + exchange(two[r].astype(bf16), r).astype(f32)
-    mine = jnp.concatenate([mine, other], axis=1)
+        total = total + part.astype(f32)
+    got = [exchange(total[r].astype(bf16), 2 * r, "grp", groups) for r in range(1, chips)]
+    mine = total[0]
+    for part in got:
+        mine = mine + part.astype(f32)
     fourth = unpack_last([mine[t] for t in range(3)], width)
     return jnp.concatenate([mine[:, :, :width], fourth[None]])[None]
 

time: 106 us -> 102 us (0.962); the launches traced: 106 us -> 101 us
  starting transfers between devices: 24.5 us -> 13.3 us
  waiting for transfers between devices: 14.8 us -> 23.2 us
  Pallas kernels: 60.1 us -> 57.8 us
    ppermute x19 -> x10, starting transfers between devices: 24.5 us -> 13.3 us  [exchange(): return lax.ppermute(x, axis, [(d, d ^ r) for d in range(size)])]
    ppermute x19 -> x10, waiting for transfers between devices: 14.8 us -> 23.2 us  [exchange(): return lax.ppermute(x, axis, [(d, d ^ r) for d in range(size)])]
    pallas_call x3, Pallas kernels: 57.9 us -> 55.6 us  [work(): pl.pallas_call(functools.partial(work_kernel, cfg), grid_spec=pltpu.Prefe...]
    another operation x3 -> x2, other arithmetic: 2.3 us -> 2.3 us
  transfers between devices with their start and end apart: 19 -> 10, of which waited for: 8 -> 6; matrix products, arithmetic and copies ran while one was open for 3% -> 2% of each run, Pallas kernels for 38% -> 39%
where the time goes in v4:
time: 102 us; the launch traced here: 101 us
  Pallas kernels  57.8 us (57%)
  waiting for transfers between devices  23.2 us (23%)
  starting transfers between devices  13.3 us (13%)
  other arithmetic  5.5 us (5%)
  local copies, waits for them, and re-layouts  1.33 us (1%)
    pallas_call x3, Pallas kernels, work(): pl.pallas_call(functools.partial(work_kernel, cfg), grid_spec=pltpu.Prefe...  55.6 us
    ppermute x10, waiting for transfers between devices, exchange(): return lax.ppermute(x, axis, [(d, d ^ r) for d in range(size)])  23.2 us
    ppermute x10, starting transfers between devices, exchange(): return lax.ppermute(x, axis, [(d, d ^ r) for d in range(size)])  13.3 us
    another operation x2, other arithmetic  2.3 us
    pallas_call x1, Pallas kernels, pack_prolong(): pl.pallas_call(pack_kernel, in_specs=[HBM], out_specs=HBM, out_shape=jax....  2.23 us
  transfers between devices with their start and end apart: 10, of which 6 were waited for; matrix products, arithmetic and copies ran while one was open for 2% of the time, Pallas kernels for 39%

profile of v4, /device:TPU:0, one launch (start us, length us, event | category | flops | bytes accessed | tf_op | source)
XLA Modules:
  0.0 101.3 jit_solution(7360161905883785598)
XLA Ops:
  0.0 2.2 %pack_prolong.1.refs_4_ = bf16[12,3,96,128]{3,2,1,0:T(8,128)(2,1)} custom-call(bf16[12,4,96,96]{3,2,1,0:T(8,128)(2,1)} %bitcast.54), custom_call_target="tpu_custom_call" | custom-call | tf_op jit(solution)/shard_map/pack_prolong/pallas_call | solution.py:58
  2.2 3.0 %collective-permute-start.2 = (bf16[12,3,96,128]{3,2,1,0:T(8,128)(2,1)}, bf16[12,3,96,128]{3,2,1,0:T(8,128)(2,1)}, u32[]{:S(2)}, u32[]{:S(2)}) collective-permute-start(bf16[12,3,96,128]{3,2,1,0:T(8,128)(2,1)} %pack_prolong.1.refs_4_), channel_id=1, source_target_pairs={{0,16},{8,24},{16,0},{24,8},{1,17},{9,25},{17,1},{25,9},{2,18},{10... | collective-permute-start | bytes 2654216 | tf_op jit(solution)/shard_map/ppermute | solution.py:354
  5.3 1.5 %collective-permute-start.1 = (bf16[12,3,96,128]{3,2,1,0:T(8,128)(2,1)}, bf16[12,3,96,128]{3,2,1,0:T(8,128)(2,1)}, u32[]{:S(2)}, u32[]{:S(2)}) collective-permute-start(bf16[12,3,96,128]{3,2,1,0:T(8,128)(2,1)} %pack_prolong.1.refs_4_), channel_id=1, source_target_pairs={{0,8},{8,0},{16,24},{24,16},{1,9},{9,1},{17,25},{25,17},{2,10},{10... | collective-permute-start | bytes 2654216 | tf_op jit(solution)/shard_map/ppermute | solution.py:354
  6.8 0.7 add_add_fusion
  7.6 0.3 convert_reduce_fusion
  8.0 1.3 %select_reduce_fusion.refs_0_ = s32[3,672]{1,0:T(4,128)} fusion(s32[648]{0:T(1024)S(1)} %get-tuple-element.26, s32[3,672]{1,0:T(4,128)S(1)} %multiply_add_fusion, s32[648]{0:T(1024)S(1)} %get-tuple-element.27), kind=kLoop, calls=%fused_computation | loop fusion | flops 3917088 | bytes 21312 | tf_op jit(solution)/shard_map/reduce_sum | solution.py:339
  9.3 22.1 %work_0.1 = (f32[128,96,128]{2,1,0:T(8,128)}, bf16[24,192,96]{2,1,0:T(8,128)(2,1)}) custom-call(s32[3,672]{1,0:T(4,128)} %select_reduce_fusion.refs_0_, s32[24,27]{1,0:T(8,128)} %bitcast.55, s32[24,108]{1,0:T(8,128)} %bitcast.58, bf16[24,27,96,96]{3,2,1,0:T(8,128)(2,1)} %bitcast.50, bf16[12,3,96,128]{3,2,1,0:T(8,128)(2,1)} %pack_prolong.1.refs_4_), custom_call_target="tpu_custom_call" | custom-call | flops 2293235712 | bytes 20000000 | tf_op jit(solution)/shard_map/work_0/pallas_call | solution.py:293
  31.4 17.9 %work_1.1.refs_7_ = f32[128,96,128]{2,1,0:T(8,128)} custom-call(s32[3,672]{1,0:T(4,128)} %select_reduce_fusion.refs_0_, s32[24,27]{1,0:T(8,128)} %bitcast.56, s32[24,108]{1,0:T(8,128)} %bitcast.59, bf16[24,27,96,96]{3,2,1,0:T(8,128)(2,1)} %bitcast.51, bf16[12,3,96,128]{3,2,1,0:T(8,128)(2,1)} %collective-permute-done.1.refs_4_, ...), custom_call_target="tpu_custom_call" | custom-call | flops 2293235712 | bytes 20000000 | tf_op jit(solution)/shard_map/work_1/pallas_call | solution.py:293
  49.3 0.9 copy-done
  50.2 15.7 %work_2.1 = (f32[4,4,3,96,128]{4,3,2,1,0:T(8,128)}, bf16[4,4,3,96,128]{4,3,2,1,0:T(8,128)(2,1)}) custom-call(s32[3,672]{1,0:T(4,128)} %select_reduce_fusion.refs_0_, s32[24,27]{1,0:T(8,128)} %bitcast.57, s32[24,108]{1,0:T(8,128)} %bitcast.60, bf16[24,27,96,96]{3,2,1,0:T(8,128)(2,1)} %bitcast.52, bf16[12,3,96,128]{3,2,1,0:T(8,128)(2,1)} %copy-done, ...), custom_call_target="tpu_custom_call" | custom-call | flops 2293235712 | bytes 20000000 | tf_op jit(solution)/shard_map/work_2/pallas_call | solution.py:293
  66.0 3.0 %collective-permute-done.3 = bf16[4,4,3,96,128]{4,3,2,1,0:T(8,128)(2,1)S(1)} collective-permute-done((bf16[4,4,3,96,128]{4,3,2,1,0:T(8,128)(2,1)}, bf16[4,4,3,96,128]{4,3,2,1,0:T(8,128)(2,1)S(1)}, u32[]{:S(2)}, u32[]{:S(2)}) %collective-permute-start.3) | collective-permute-done | bytes 1179680 | tf_op jit(solution)/shard_map/ppermute | solution.py:354
  69.0 2.1 %fusion.19 = (bf16[4,4,3,96,128]{4,3,2,1,0:T(8,128)(2,1)S(1)}, f32[4,4,3,96,128]{4,3,2,1,0:T(8,128)S(1)}) fusion(f32[4,4,3,96,128]{4,3,2,1,0:T(8,128)} %get-tuple-element.11, bf16[4,4,3,96,128]{4,3,2,1,0:T(8,128)(2,1)S(1)} %collective-permute-done.3), kind=kLoop, calls=%fused_computation.43 | loop fusion | flops 1769472 | bytes 7077888 | tf_op jit(solution)/shard_map/convert.5
  71.2 1.9 %collective-permute-start.4 = (bf16[4,3,96,128]{3,2,1,0:T(8,128)(2,1)S(1)}, bf16[4,3,96,128]{3,2,1,0:T(8,128)(2,1)S(1)}, u32[]{:S(2)}, u32[]{:S(2)}) collective-permute-start(bf16[4,3,96,128]{3,2,1,0:T(8,128)(2,1)S(1)} %get-tuple-element.17), channel_id=1, source_target_pairs={{0,8},{8,0},{16,24},{24,16},{1,9},{9,1},{17,25},{25,17},{2,10},{10... | collective-permute-start | bytes 884744 | tf_op jit(solution)/shard_map/ppermute | solution.py:354
  73.1 1.0 collective-permute-start.6
  74.1 0.7 collective-permute-start.5
  74.8 6.4 %collective-permute-done.4 = bf16[4,3,96,128]{3,2,1,0:T(8,128)(2,1)S(1)} collective-permute-done((bf16[4,3,96,128]{3,2,1,0:T(8,128)(2,1)S(1)}, bf16[4,3,96,128]{3,2,1,0:T(8,128)(2,1)S(1)}, u32[]{:S(2)}, u32[]{:S(2)}) %collective-permute-start.4) | collective-permute-done | bytes 294944 | tf_op jit(solution)/shard_map/ppermute | solution.py:354
  81.1 6.5 %collective-permute-done.6 = bf16[4,3,96,128]{3,2,1,0:T(8,128)(2,1)S(1)} collective-permute-done((bf16[4,3,96,128]{3,2,1,0:T(8,128)(2,1)S(1)}, bf16[4,3,96,128]{3,2,1,0:T(8,128)(2,1)S(1)}, u32[]{:S(2)}, u32[]{:S(2)}) %collective-permute-start.6) | collective-permute-done | bytes 294944 | tf_op jit(solution)/shard_map/ppermute | solution.py:354
  87.6 1.4 %collective-permute-done.5 = bf16[4,3,96,128]{3,2,1,0:T(8,128)(2,1)S(1)} collective-permute-done((bf16[4,3,96,128]{3,2,1,0:T(8,128)(2,1)S(1)}, bf16[4,3,96,128]{3,2,1,0:T(8,128)(2,1)S(1)}, u32[]{:S(2)}, u32[]{:S(2)}) %collective-permute-start.5) | collective-permute-done | bytes 294944 | tf_op jit(solution)/shard_map/ppermute | solution.py:354
  89.0 0.1 fusion.17
  89.2 2.5 %collective-permute-start.7 = (bf16[3,96,128]{2,1,0:T(8,128)(2,1)S(1)}, bf16[3,96,128]{2,1,0:T(8,128)(2,1)S(1)}, u32[]{:S(2)}, u32[]{:S(2)}) collective-permute-start(bf16[3,96,128]{2,1,0:T(8,128)(2,1)S(1)} %get-tuple-element.20), channel_id=1, source_target_pairs={{0,2},{1,3},{2,0},{3,1},{4,6},{5,7},{6,4},{7,5},{8,10},{9,11},{10,... | collective-permute-start | bytes 221192 | tf_op jit(solution)/shard_map/ppermute | solution.py:354
  91.7 2.6 %collective-permute-start.9 = (bf16[3,96,128]{2,1,0:T(8,128)(2,1)S(1)}, bf16[3,96,128]{2,1,0:T(8,128)(2,1)S(1)}, u32[]{:S(2)}, u32[]{:S(2)}) collective-permute-start(bf16[3,96,128]{2,1,0:T(8,128)(2,1)S(1)} %get-tuple-element.21), channel_id=1, source_target_pairs={{0,6},{1,7},{2,4},{3,5},{4,2},{5,3},{6,0},{7,1},{8,14},{9,15},{10,... | collective-permute-start | bytes 221192 | tf_op jit(solution)/shard_map/ppermute | solution.py:354
  94.3 3.6 %collective-permute-done.9 = bf16[3,96,128]{2,1,0:T(8,128)(2,1)S(1)} collective-permute-done((bf16[3,96,128]{2,1,0:T(8,128)(2,1)S(1)}, bf16[3,96,128]{2,1,0:T(8,128)(2,1)S(1)}, u32[]{:S(2)}, u32[]{:S(2)}) %collective-permute-start.9) | collective-permute-done | bytes 73760 | tf_op jit(solution)/shard_map/ppermute | solution.py:354
  98.0 2.2 %collective-permute-done.8 = bf16[3,96,128]{2,1,0:T(8,128)(2,1)S(1)} collective-permute-done((bf16[3,96,128]{2,1,0:T(8,128)(2,1)S(1)}, bf16[3,96,128]{2,1,0:T(8,128)(2,1)S(1)}, u32[]{:S(2)}, u32[]{:S(2)}) %collective-permute-start.8) | collective-permute-done | bytes 73760 | tf_op jit(solution)/shard_map/ppermute | solution.py:354
  100.6 0.7 maximum_bitcast_fusion
  (19 shorter events, 0.7 us)
Async XLA Ops:
  2.2 29.1 %collective-permute-start.2 = (bf16[12,3,96,128]{3,2,1,0:T(8,128)(2,1)}, bf16[12,3,96,128]{3,2,1,0:T(8,128)(2,1)}, u32[]{:S(2)}, u32[]{:S(2)}) collective-permute-start(bf16[12,3,96,128]{3,2,1,0:T(8,128)(2,1)} %pack_prolong.1.refs_4_), channel_id=1, source_target_pairs={{0,16},{8,24},{16,0},{24,8},{1,17},{9,25},{17,1},{25,9},{2,18},{10... | collective-permute-start | bytes 2654216 | tf_op jit(solution)/shard_map/ppermute | solution.py:354
  5.3 26.1 %collective-permute-start.1 = (bf16[12,3,96,128]{3,2,1,0:T(8,128)(2,1)}, bf16[12,3,96,128]{3,2,1,0:T(8,128)(2,1)}, u32[]{:S(2)}, u32[]{:S(2)}) collective-permute-start(bf16[12,3,96,128]{3,2,1,0:T(8,128)(2,1)} %pack_prolong.1.refs_4_), channel_id=1, source_target_pairs={{0,8},{8,0},{16,24},{24,16},{1,9},{9,1},{17,25},{25,17},{2,10},{10... | collective-permute-start | bytes 2654216 | tf_op jit(solution)/shard_map/ppermute | solution.py:354
  6.8 42.5 %collective-permute-start = (bf16[12,3,96,128]{3,2,1,0:T(8,128)(2,1)}, bf16[12,3,96,128]{3,2,1,0:T(8,128)(2,1)S(1)}, u32[]{:S(2)}, u32[]{:S(2)}) collective-permute-start(bf16[12,3,96,128]{3,2,1,0:T(8,128)(2,1)} %pack_prolong.1.refs_4_), channel_id=1, source_target_pairs={{0,24},{8,16},{16,8},{24,0},{1,25},{9,17},{17,9},{25,1},{2,26},{10... | collective-permute-start | bytes 2654216 | tf_op jit(solution)/shard_map/ppermute | solution.py:354
  49.3 0.9 copy-start
  65.9 3.1 %collective-permute-start.3 = (bf16[4,4,3,96,128]{4,3,2,1,0:T(8,128)(2,1)}, bf16[4,4,3,96,128]{4,3,2,1,0:T(8,128)(2,1)S(1)}, u32[]{:S(2)}, u32[]{:S(2)}) collective-permute-start(bf16[4,4,3,96,128]{4,3,2,1,0:T(8,128)(2,1)} %get-tuple-element.12), channel_id=1, source_target_pairs={{0,1},{1,0},{2,3},{3,2},{4,5},{5,4},{6,7},{7,6},{8,9},{9,8},{10,11... | collective-permute-start | bytes 3538952 | tf_op jit(solution)/shard_map/ppermute | solution.py:354
  71.2 9.9 %collective-permute-start.4 = (bf16[4,3,96,128]{3,2,1,0:T(8,128)(2,1)S(1)}, bf16[4,3,96,128]{3,2,1,0:T(8,128)(2,1)S(1)}, u32[]{:S(2)}, u32[]{:S(2)}) collective-permute-start(bf16[4,3,96,128]{3,2,1,0:T(8,128)(2,1)S(1)} %get-tuple-element.17), channel_id=1, source_target_pairs={{0,8},{8,0},{16,24},{24,16},{1,9},{9,1},{17,25},{25,17},{2,10},{10... | collective-permute-start | bytes 884744 | tf_op jit(solution)/shard_map/ppermute | solution.py:354
  73.1 14.5 %collective-permute-start.6 = (bf16[4,3,96,128]{3,2,1,0:T(8,128)(2,1)S(1)}, bf16[4,3,96,128]{3,2,1,0:T(8,128)(2,1)S(1)}, u32[]{:S(2)}, u32[]{:S(2)}) collective-permute-start(bf16[4,3,96,128]{3,2,1,0:T(8,128)(2,1)S(1)} %get-tuple-element.18), channel_id=1, source_target_pairs={{0,24},{8,16},{16,8},{24,0},{1,25},{9,17},{17,9},{25,1},{2,26},{10... | collective-permute-start | bytes 884744 | tf_op jit(solution)/shard_map/ppermute | solution.py:354
  74.1 15.0 %collective-permute-start.5 = (bf16[4,3,96,128]{3,2,1,0:T(8,128)(2,1)S(1)}, bf16[4,3,96,128]{3,2,1,0:T(8,128)(2,1)S(1)}, u32[]{:S(2)}, u32[]{:S(2)}) collective-permute-start(bf16[4,3,96,128]{3,2,1,0:T(8,128)(2,1)S(1)} %get-tuple-element.19), channel_id=1, source_target_pairs={{0,16},{8,24},{16,0},{24,8},{1,17},{9,25},{17,1},{25,9},{2,18},{10... | collective-permute-start | bytes 884744 | tf_op jit(solution)/shard_map/ppermute | solution.py:354
  89.2 5.1 %collective-permute-start.7 = (bf16[3,96,128]{2,1,0:T(8,128)(2,1)S(1)}, bf16[3,96,128]{2,1,0:T(8,128)(2,1)S(1)}, u32[]{:S(2)}, u32[]{:S(2)}) collective-permute-start(bf16[3,96,128]{2,1,0:T(8,128)(2,1)S(1)} %get-tuple-element.20), channel_id=1, source_target_pairs={{0,2},{1,3},{2,0},{3,1},{4,6},{5,7},{6,4},{7,5},{8,10},{9,11},{10,... | collective-permute-start | bytes 221192 | tf_op jit(solution)/shard_map/ppermute | solution.py:354
  91.7 6.3 %collective-permute-start.9 = (bf16[3,96,128]{2,1,0:T(8,128)(2,1)S(1)}, bf16[3,96,128]{2,1,0:T(8,128)(2,1)S(1)}, u32[]{:S(2)}, u32[]{:S(2)}) collective-permute-start(bf16[3,96,128]{2,1,0:T(8,128)(2,1)S(1)} %get-tuple-element.21), channel_id=1, source_target_pairs={{0,6},{1,7},{2,4},{3,5},{4,2},{5,3},{6,0},{7,1},{8,14},{9,15},{10,... | collective-permute-start | bytes 221192 | tf_op jit(solution)/shard_map/ppermute | solution.py:354
  94.3 5.9 %collective-permute-start.8 = (bf16[3,96,128]{2,1,0:T(8,128)(2,1)S(1)}, bf16[3,96,128]{2,1,0:T(8,128)(2,1)S(1)}, u32[]{:S(2)}, u32[]{:S(2)}) collective-permute-start(bf16[3,96,128]{2,1,0:T(8,128)(2,1)S(1)} %get-tuple-element.22), channel_id=1, source_target_pairs={{0,4},{1,5},{2,6},{3,7},{4,0},{5,1},{6,2},{7,3},{8,12},{9,13},{10,... | collective-permute-start | bytes 221192 | tf_op jit(solution)/shard_map/ppermute | solution.py:354

commit v5 on v4

--- a/solution.py
+++ b/solution.py
@@ -11,7 +11,7 @@
 UNROLL = 16
 LANES = 128
 AHEAD = 12
-VMEM_LIMIT = 63 * 1024 * 1024
+VMEM_LIMIT = 65408 * 1024
 HBM = pl.BlockSpec(memory_space=pl.ANY)
 
 
@@ -97,7 +97,7 @@
 
     me = lax.axis_index("blk").astype(jnp.int32)
     rank = lax.axis_index("grp").astype(jnp.int32)
-    chip, core = rank >> 1, rank & 1
+    core = rank & 1
 
     def a_copy(i):
         to = a_rows.at[pl.ds((i + 1) * nonzeros, nonzeros)]
@@ -200,11 +200,18 @@
 
     def collect(i, k, partial):
         for n in range(per_row):
+            to, values = [], []
             for m in range(per_row):
                 s = tgt_ref[i, n * nonzeros * per_row + k * per_row + m]
-                acc[s] = acc[s] + partial[
-                    n * width : (n + 1) * width, m * LANES : (m + 1) * LANES
-                ]
+                value = acc[s]
+                for other, so_far in zip(to, values):
+                    value = jnp.where(s == other, so_far, value)
+                to.append(s)
+                values.append(
+                    value + partial[n * width : (n + 1) * width, m * LANES : (m + 1) * LANES]
+                )
+            for s, value in zip(to, values):
+                acc[s] = value
 
     def rows_for(g, ready):
         v = list_ref[phase, (g + 1) * UNROLL - 1]
@@ -252,11 +259,11 @@
         def emit(rz, _):
             for rc in range(2):
                 for r in range(members):
-                    s = ((chip ^ rz) * 2 + (core ^ rc)) * (OWN * members) + (me ^ r) * OWN
+                    s = (rz * 2 + (core ^ rc)) * (OWN * members) + r * OWN
                     packed = pack_four([total(s + x) for x in range(OWN)], width)
                     for t in range(3):
-                        stages[rc][rz, r, t] = packed[t].astype(stages[rc].dtype)
-                copy = pltpu.make_async_copy(stages[rc].at[rz], out_refs[rc].at[rz], out_sem.at[rc])
+                        stages[rc][r, rz, t] = packed[t].astype(stages[rc].dtype)
+                copy = pltpu.make_async_copy(stages[rc].at[:, rz], out_refs[rc].at[:, rz], out_sem.at[rc])
                 copy.start()
             return 0
 
@@ -283,7 +290,7 @@
     pt_shape = (rows, per_row * width, width)
     stages = []
     if cfg["last"]:
-        whole = (groups // 2, members, 3, width, LANES)
+        whole = (members, groups // 2, 3, width, LANES)
         shapes = [jax.ShapeDtypeStruct(whole, jnp.float32), jax.ShapeDtypeStruct(whole, jnp.bfloat16)]
         stages = [pltpu.VMEM(x.shape, x.dtype) for x in shapes]
     else:
@@ -382,14 +389,13 @@
 
     keep, give = outs
     total = keep + exchange(give, 1, "grp", groups).astype(f32)
-    got = [exchange(total[:, r].astype(bf16), r) for r in range(1, members)]
-    total = total[:, 0]
-    for part in got:
-        total = total + part.astype(f32)
-    got = [exchange(total[r].astype(bf16), 2 * r, "grp", groups) for r in range(1, chips)]
-    mine = total[0]
-    for part in got:
-        mine = mine + part.astype(f32)
+    got = lax.all_to_all(total.astype(bf16), "blk", 0, 0, tiled=True)
+    total = jnp.sum(got.astype(f32), axis=0)
+    same_core = [[c + 2 * z for z in range(chips)] for c in range(2)]
+    got = lax.all_to_all(
+        total.astype(bf16), "grp", 0, 0, axis_index_groups=same_core, tiled=True
+    )
+    mine = jnp.sum(got.astype(f32), axis=0)
     fourth = unpack_last([mine[t] for t in range(3)], width)
     return jnp.concatenate([mine[:, :, :width], fourth[None]])[None]
 

time: 102 us -> 104 us (1.020)
  blocking collectives: 0 us -> 33.9 us
  waiting for transfers between devices: 23.2 us -> 2.87 us
  starting transfers between devices: 13.3 us -> 4.83 us
    all_to_all x0 -> x2, blocking collectives: none -> 33.9 us  [the longest x1 20.8 us: shards(): got = lax.all_to_all(total.astype(bf16), 'blk', 0, 0, tiled=True)]
    ppermute x10 -> x4, waiting for transfers between devices: 23.2 us -> 2.87 us  [exchange(): return lax.ppermute(x, axis, [(d, d ^ r) for d in range(size)])]
    ppermute x10 -> x4, starting transfers between devices: 13.3 us -> 4.83 us  [exchange(): return lax.ppermute(x, axis, [(d, d ^ r) for d in range(size)])]
    another operation x2 -> x0, other arithmetic: 2.3 us -> none
    convert_element_type x0 -> x1, other arithmetic: none -> 1.98 us  [shards(): got = lax.all_to_all(total.astype(bf16), 'blk', 0, 0, tiled=True)]
  transfers between devices with their start and end apart: 10 -> 4, of which waited for: 6 -> 1; matrix products, arithmetic and copies ran while one was open for 2% -> 2% of each run, Pallas kernels for 39% -> 38%
where the time goes in v5:
time: 104 us
  Pallas kernels  57 us (55%)
  blocking collectives  33.9 us (33%)
  starting transfers between devices  4.83 us (5%)
  other arithmetic  4.66 us (4%)
  waiting for transfers between devices  2.87 us (3%)
    pallas_call x3, Pallas kernels, work(): pl.pallas_call(functools.partial(work_kernel, cfg), grid_spec=pltpu.Prefe...  54.8 us
    all_to_all x1, blocking collectives, shards(): got = lax.all_to_all(total.astype(bf16), 'blk', 0, 0, tiled=True)  20.8 us
    all_to_all x1, blocking collectives, shards(): lax.all_to_all(total.astype(bf16), 'grp', 0, 0, axis_index_groups=same_co...  13 us
    ppermute x4, starting transfers between devices, exchange(): return lax.ppermute(x, axis, [(d, d ^ r) for d in range(size)])  4.83 us
    ppermute x4, waiting for transfers between devices, exchange(): return lax.ppermute(x, axis, [(d, d ^ r) for d in range(size)])  2.87 us
    pallas_call x1, Pallas kernels, pack_prolong(): pl.pallas_call(pack_kernel, in_specs=[HBM], out_specs=HBM, out_shape=jax....  2.25 us
  transfers between devices with their start and end apart: 4, of which 1 were waited for; matrix products, arithmetic and copies ran while one was open for 2% of the time, Pallas kernels for 38%

profile of v5, /device:TPU:0, one launch (start us, length us, event | category | flops | bytes accessed | tf_op | source)
XLA Modules:
  0.0 103.7 jit_solution(12035640127726765963)
XLA Ops:
  0.0 2.2 %pack_prolong.1.refs_4_ = bf16[12,3,96,128]{3,2,1,0:T(8,128)(2,1)} custom-call(bf16[12,4,96,96]{3,2,1,0:T(8,128)(2,1)} %bitcast.19), custom_call_target="tpu_custom_call" | custom-call | tf_op jit(solution)/shard_map/pack_prolong/pallas_call | solution.py:58
  2.3 3.0 %collective-permute-start.2 = (bf16[12,3,96,128]{3,2,1,0:T(8,128)(2,1)}, bf16[12,3,96,128]{3,2,1,0:T(8,128)(2,1)}, u32[]{:S(2)}, u32[]{:S(2)}) collective-permute-start(bf16[12,3,96,128]{3,2,1,0:T(8,128)(2,1)} %pack_prolong.1.refs_4_), channel_id=1, source_target_pairs={{0,16},{8,24},{16,0},{24,8},{1,17},{9,25},{17,1},{25,9},{2,18},{10... | collective-permute-start | bytes 2654216 | tf_op jit(solution)/shard_map/ppermute | solution.py:361
  5.3 1.5 %collective-permute-start.1 = (bf16[12,3,96,128]{3,2,1,0:T(8,128)(2,1)}, bf16[12,3,96,128]{3,2,1,0:T(8,128)(2,1)}, u32[]{:S(2)}, u32[]{:S(2)}) collective-permute-start(bf16[12,3,96,128]{3,2,1,0:T(8,128)(2,1)} %pack_prolong.1.refs_4_), channel_id=1, source_target_pairs={{0,8},{8,0},{16,24},{24,16},{1,9},{9,1},{17,25},{25,17},{2,10},{10... | collective-permute-start | bytes 2654216 | tf_op jit(solution)/shard_map/ppermute | solution.py:361
  6.8 0.1 collective-permute-start
  6.9 0.1 reshape.107
  7.0 0.3 convert_reduce_fusion
  7.3 1.3 %select_reduce_fusion.refs_0_ = s32[3,672]{1,0:T(4,128)} fusion(s32[648]{0:T(1024)S(1)} %get-tuple-element.16, s32[3,672]{1,0:T(4,128)S(1)} %multiply_add_fusion, s32[648]{0:T(1024)S(1)} %get-tuple-element.17), kind=kLoop, calls=%fused_computation | loop fusion | flops 3917088 | bytes 21312 | tf_op jit(solution)/shard_map/reduce_sum | solution.py:346
  8.6 22.1 %work_0.1 = (f32[128,96,128]{2,1,0:T(8,128)}, bf16[24,192,96]{2,1,0:T(8,128)(2,1)}) custom-call(s32[3,672]{1,0:T(4,128)} %select_reduce_fusion.refs_0_, s32[24,27]{1,0:T(8,128)} %bitcast.20, s32[24,108]{1,0:T(8,128)} %bitcast.23, bf16[24,27,96,96]{3,2,1,0:T(8,128)(2,1)} %bitcast.15, bf16[12,3,96,128]{3,2,1,0:T(8,128)(2,1)} %pack_prolong.1.refs_4_), custom_call_target="tpu_custom_call" | custom-call | flops 2293235712 | bytes 20000000 | tf_op jit(solution)/shard_map/work_0/pallas_call | solution.py:300
  30.7 0.0 collective-permute-done.2.refs_5_
  30.7 0.0 collective-permute-done.1.refs_4_
  30.7 17.0 %work_1.1.refs_7_ = f32[128,96,128]{2,1,0:T(8,128)} custom-call(s32[3,672]{1,0:T(4,128)} %select_reduce_fusion.refs_0_, s32[24,27]{1,0:T(8,128)} %bitcast.21, s32[24,108]{1,0:T(8,128)} %bitcast.24, bf16[24,27,96,96]{3,2,1,0:T(8,128)(2,1)} %bitcast.16, bf16[12,3,96,128]{3,2,1,0:T(8,128)(2,1)} %collective-permute-done.1.refs_4_, ...), custom_call_target="tpu_custom_call" | custom-call | flops 2293235712 | bytes 20000000 | tf_op jit(solution)/shard_map/work_1/pallas_call | solution.py:300
  47.7 0.0 collective-permute-done.refs_4_
  47.7 15.7 %work_2.1 = (f32[4,4,3,96,128]{4,3,2,1,0:T(8,128)}, bf16[4,4,3,96,128]{4,3,2,1,0:T(8,128)(2,1)}) custom-call(s32[3,672]{1,0:T(4,128)} %select_reduce_fusion.refs_0_, s32[24,27]{1,0:T(8,128)} %bitcast.22, s32[24,108]{1,0:T(8,128)} %bitcast.25, bf16[24,27,96,96]{3,2,1,0:T(8,128)(2,1)} %bitcast.17, bf16[12,3,96,128]{3,2,1,0:T(8,128)(2,1)} %collective-permute-done.refs_4_, ...), custom_call_target="tpu_custom_call" | custom-call | flops 2293235712 | bytes 20000000 | tf_op jit(solution)/shard_map/work_2/pallas_call | solution.py:300
  63.4 0.3 collective-permute-start.3
  63.7 2.9 %collective-permute-done.3 = bf16[4,4,3,96,128]{4,3,2,1,0:T(8,128)(2,1)S(1)} collective-permute-done((bf16[4,4,3,96,128]{4,3,2,1,0:T(8,128)(2,1)}, bf16[4,4,3,96,128]{4,3,2,1,0:T(8,128)(2,1)S(1)}, u32[]{:S(2)}, u32[]{:S(2)}) %collective-permute-start.3) | collective-permute-done | bytes 1179680 | tf_op jit(solution)/shard_map/ppermute | solution.py:361
  66.5 2.0 %add_convert_fusion = bf16[4,4,3,96,128]{4,3,2,1,0:T(8,128)(2,1)S(1)} fusion(f32[4,4,3,96,128]{4,3,2,1,0:T(8,128)} %get-tuple-element.11, bf16[4,4,3,96,128]{4,3,2,1,0:T(8,128)(2,1)S(1)} %collective-permute-done.3), kind=kLoop, calls=%fused_computation.1 | loop fusion | flops 1769472 | bytes 4718592 | tf_op jit(solution)/shard_map/convert_element_type | solution.py:392
  68.5 20.8 %all_to_all.10 = bf16[4,4,3,96,128]{4,3,2,1,0:T(8,128)(2,1)S(1)} all-to-all(bf16[4,4,3,96,128]{4,3,2,1,0:T(8,128)(2,1)S(1)} %add_convert_fusion), channel_id=1, replica_groups=mesh['blk'=4,'grp'=8] {'blk'}, dimensions={0} | all-to-all | bytes 2359296 | tf_op jit(solution)/shard_map/all_to_all | solution.py:392
  89.3 0.2 reduce_sum.41
  89.5 13.0 %all_to_all.11 = bf16[4,3,96,128]{3,2,1,0:T(8,128)(2,1)S(1)} all-to-all(bf16[4,3,96,128]{3,2,1,0:T(8,128)(2,1)S(1)} %reduce_sum.41), channel_id=1, replica_groups={{0,2,4,6},{1,3,5,7},{8,10,12,14},{9,11,13,15},{16,18,20,22},{17,19,21,2..., dimensions={0} | all-to-all | bytes 589824 | tf_op jit(solution)/shard_map/all_to_all | solution.py:395
  102.6 0.1 slice.30
  102.7 0.1 slice.34
  102.8 0.1 slice.32
  102.9 0.1 maximum_bitcast_fusion.1
  103.0 0.7 maximum_bitcast_fusion
  (7 shorter events, 0.1 us)
Async XLA Ops:
  0.0 6.8 %copy-start = (s32[1,24,27]{2,1,0:T(8,128)S(1)}, s32[1,24,27]{2,1,0:T(8,128)}, u32[]{:S(2)}) copy-start(s32[1,24,27]{2,1,0:T(8,128)} %param.5) | copy-start | bytes 7780
  2.3 28.4 %collective-permute-start.2 = (bf16[12,3,96,128]{3,2,1,0:T(8,128)(2,1)}, bf16[12,3,96,128]{3,2,1,0:T(8,128)(2,1)}, u32[]{:S(2)}, u32[]{:S(2)}) collective-permute-start(bf16[12,3,96,128]{3,2,1,0:T(8,128)(2,1)} %pack_prolong.1.refs_4_), channel_id=1, source_target_pairs={{0,16},{8,24},{16,0},{24,8},{1,17},{9,25},{17,1},{25,9},{2,18},{10... | collective-permute-start | bytes 2654216 | tf_op jit(solution)/shard_map/ppermute | solution.py:361
  5.3 25.4 %collective-permute-start.1 = (bf16[12,3,96,128]{3,2,1,0:T(8,128)(2,1)}, bf16[12,3,96,128]{3,2,1,0:T(8,128)(2,1)}, u32[]{:S(2)}, u32[]{:S(2)}) collective-permute-start(bf16[12,3,96,128]{3,2,1,0:T(8,128)(2,1)} %pack_prolong.1.refs_4_), channel_id=1, source_target_pairs={{0,8},{8,0},{16,24},{24,16},{1,9},{9,1},{17,25},{25,17},{2,10},{10... | collective-permute-start | bytes 2654216 | tf_op jit(solution)/shard_map/ppermute | solution.py:361
  6.8 40.9 %collective-permute-start = (bf16[12,3,96,128]{3,2,1,0:T(8,128)(2,1)}, bf16[12,3,96,128]{3,2,1,0:T(8,128)(2,1)}, u32[]{:S(2)}, u32[]{:S(2)}) collective-permute-start(bf16[12,3,96,128]{3,2,1,0:T(8,128)(2,1)} %pack_prolong.1.refs_4_), channel_id=1, source_target_pairs={{0,24},{8,16},{16,8},{24,0},{1,25},{9,17},{17,9},{25,1},{2,26},{10... | collective-permute-start | bytes 2654216 | tf_op jit(solution)/shard_map/ppermute | solution.py:361
  63.4 3.1 %collective-permute-start.3 = (bf16[4,4,3,96,128]{4,3,2,1,0:T(8,128)(2,1)}, bf16[4,4,3,96,128]{4,3,2,1,0:T(8,128)(2,1)S(1)}, u32[]{:S(2)}, u32[]{:S(2)}) collective-permute-start(bf16[4,4,3,96,128]{4,3,2,1,0:T(8,128)(2,1)} %get-tuple-element.12), channel_id=1, source_target_pairs={{0,1},{1,0},{2,3},{3,2},{4,5},{5,4},{6,7},{7,6},{8,9},{9,8},{10,11... | collective-permute-start | bytes 3538952 | tf_op jit(solution)/shard_map/ppermute | solution.py:361

commit v6 on v4

--- a/solution.py
+++ b/solution.py
@@ -11,7 +11,7 @@
 UNROLL = 16
 LANES = 128
 AHEAD = 12
-VMEM_LIMIT = 63 * 1024 * 1024
+VMEM = 64 * 1024 * 1024
 HBM = pl.BlockSpec(memory_space=pl.ANY)
 
 
@@ -66,7 +66,7 @@
             pltpu.SemaphoreType.DMA((steps,)),
             pltpu.SemaphoreType.DMA((steps,)),
         ],
-        compiler_params=pltpu.CompilerParams(vmem_limit_bytes=VMEM_LIMIT),
+        compiler_params=pltpu.CompilerParams(vmem_limit_bytes=VMEM // 2),
         name="pack_prolong",
     )(prolong.reshape(quads, 4, width, width))
 
@@ -86,14 +86,15 @@
     list_ref, col_ref, tgt_ref, a_hbm = take(4)
     p_hbm = take(cfg["sources"])
     if not first:
-        (pt_hbm,) = take(1)
-    acc_in = take(cfg["sums"])
-    out_refs = take(2 if first or last else 1)
-    p_vmem, pt, a_rows, acc = take(4)
+        pt, _ = take(2)
+    out_refs = take(2 if last else 0)
+    (acc,) = take(1)
+    if first:
+        (pt,) = take(1)
+    p_vmem, a_rows = take(2)
     aps = take(UNROLL)
     a_sem, sem, out_sem = take(3)
     stages = take(2 if last else 0)
-    late = take(len(acc_in) if cfg["late"] else 0)
 
     me = lax.axis_index("blk").astype(jnp.int32)
     rank = lax.axis_index("grp").astype(jnp.int32)
@@ -113,13 +114,6 @@
         @pl.when(i + AHEAD < rows)
         def _():
             a_copy(i + AHEAD).start()
-
-        if late:
-
-            @pl.when(i + AHEAD == rows - 1)
-            def _():
-                for copy in sums:
-                    copy.start()
 
         return 0
 
@@ -128,19 +122,12 @@
         to = p_vmem.at[pl.ds(at, source.shape[0]), pl.ds(0, 3)]
         p_copies.append(pltpu.make_async_copy(source, to, sem.at[s]))
         at += source.shape[0]
-    others = []
-    if not first:
-        others.append(pltpu.make_async_copy(pt_hbm, pt, sem.at[cfg["sources"]]))
-    sums = [
-        pltpu.make_async_copy(source, to, sem.at[cfg["sources"] + 1 + s])
-        for s, (source, to) in enumerate(zip(acc_in, late or [acc]))
-    ]
-    for copy in p_copies + others + ([] if late else sums):
+    for copy in p_copies:
         copy.start()
     lax.fori_loop(0, AHEAD, start_row, 0)
 
     a_rows[0] = jnp.zeros((width, width), a_rows.dtype)
-    if late or not acc_in:
+    if first:
 
         def clear(s, _):
             for x in range(8):
@@ -168,9 +155,6 @@
             return 0
 
         lax.fori_loop(0, at, transpose, 0)
-    for copy in others + ([] if late else sums):
-        copy.wait()
-
     scale = divider(rows, members)
 
     def p_block(v):
@@ -237,23 +221,13 @@
         i, k = entry(g, u)
         collect(i, k, second_product(u, i))
     lax.fori_loop(ready, rows, wait_row, 0)
-    if late:
-        for copy in sums:
-            copy.wait()
-
-    def total(s):
-        value = acc[s]
-        for extra in late:
-            value = value + extra[s]
-        return value
-
     if last:
 
         def emit(rz, _):
             for rc in range(2):
                 for r in range(members):
                     s = ((chip ^ rz) * 2 + (core ^ rc)) * (OWN * members) + (me ^ r) * OWN
-                    packed = pack_four([total(s + x) for x in range(OWN)], width)
+                    packed = pack_four([acc[s + x] for x in range(OWN)], width)
                     for t in range(3):
                         stages[rc][rz, r, t] = packed[t].astype(stages[rc].dtype)
                 copy = pltpu.make_async_copy(stages[rc].at[rz], out_refs[rc].at[rz], out_sem.at[rc])
@@ -263,57 +237,54 @@
         lax.fori_loop(0, groups // 2, emit, 0)
         for rc in range(2):
             pltpu.make_async_copy(stages[rc], out_refs[rc], out_sem.at[rc]).wait()
-    else:
-        outs = [pltpu.make_async_copy(acc, out_refs[0], out_sem.at[0])]
-        if first:
-            outs.append(pltpu.make_async_copy(pt, out_refs[1], out_sem.at[1]))
-        for copy in outs:
-            copy.start()
-        for copy in outs:
-            copy.wait()
-
-
-def work(cfg, tables, a_rows, packed, pt=None, sums=()):
+
+
+def work(cfg, tables, a_rows, packed, pt=None, acc=None):
     width, rows, nonzeros, per_row = cfg["width"], cfg["rows"], cfg["nonzeros"], cfg["per_row"]
     slots, members, groups = cfg["slots"], cfg["members"], cfg["groups"]
-    late = cfg["last"] and cfg["late"]
-    cfg = dict(cfg, sources=len(packed), sums=len(sums), late=late)
+    first, last = cfg["first"], cfg["last"]
+    cfg = dict(cfg, sources=len(packed))
     quads = sum(x.shape[0] for x in packed)
-    operands = [a_rows, *packed] + ([] if cfg["first"] else [pt]) + list(sums)
-    pt_shape = (rows, per_row * width, width)
-    stages = []
-    if cfg["last"]:
+    vmem = pl.BlockSpec(memory_space=pltpu.VMEM)
+    operands = [a_rows, *packed]
+    in_specs, out_specs = [HBM] * len(operands), [vmem]
+    shapes, stages, aliases = [pltpu.VMEM((slots, width, LANES), jnp.float32)], [], {}
+    resident = slots * width * LANES * 4 + rows * per_row * width * LANES * 2
+    if first:
+        shapes.append(pltpu.VMEM((rows, per_row * width, width), jnp.bfloat16))
+        out_specs.append(vmem)
+    else:
+        operands += [pt, acc]
+        in_specs += [vmem, vmem]
+    if last:
         whole = (groups // 2, members, 3, width, LANES)
-        shapes = [jax.ShapeDtypeStruct(whole, jnp.float32), jax.ShapeDtypeStruct(whole, jnp.bfloat16)]
-        stages = [pltpu.VMEM(x.shape, x.dtype) for x in shapes]
-    else:
-        shapes = [jax.ShapeDtypeStruct((slots, width, LANES), jnp.float32)]
-        if cfg["first"]:
-            shapes.append(jax.ShapeDtypeStruct(pt_shape, jnp.bfloat16))
+        made = [jax.ShapeDtypeStruct(whole, jnp.float32), jax.ShapeDtypeStruct(whole, jnp.bfloat16)]
+        stages = [pltpu.VMEM(x.shape, x.dtype) for x in made]
+        shapes, out_specs = made + shapes, [HBM] * 2 + out_specs
+    if not first:
+        aliases = {len(tables) + len(operands) - 1: len(shapes) - 1}
     return pl.pallas_call(
         functools.partial(work_kernel, cfg),
         grid_spec=pltpu.PrefetchScalarGridSpec(
-            num_scalar_prefetch=3,
+            num_scalar_prefetch=len(tables),
             grid=(),
-            in_specs=[HBM] * len(operands),
-            out_specs=[HBM] * len(shapes),
+            in_specs=in_specs,
+            out_specs=out_specs,
             scratch_shapes=[
                 pltpu.VMEM((quads, 4, width, LANES), jnp.bfloat16),
-                pltpu.VMEM(pt_shape, jnp.bfloat16),
                 pltpu.VMEM(((rows + 1) * nonzeros, width, width), jnp.bfloat16),
-                pltpu.VMEM((slots, width, LANES), jnp.float32),
             ]
             + [pltpu.VMEM((width, per_row * LANES), jnp.bfloat16)] * UNROLL
             + [
                 pltpu.SemaphoreType.DMA((rows,)),
-                pltpu.SemaphoreType.DMA((len(packed) + 1 + len(sums),)),
+                pltpu.SemaphoreType.DMA((len(packed),)),
                 pltpu.SemaphoreType.DMA((2,)),
             ]
-            + stages
-            + [pltpu.VMEM((slots, width, LANES), jnp.float32)] * (len(sums) if late else 0),
+            + stages,
         ),
         out_shape=shapes,
-        compiler_params=pltpu.CompilerParams(vmem_limit_bytes=VMEM_LIMIT),
+        input_output_aliases=aliases,
+        compiler_params=pltpu.CompilerParams(vmem_limit_bytes=VMEM - resident - 1024 * 1024),
         cost_estimate=pl.CostEstimate(
             flops=4 * rows * nonzeros * width * width * width,
             bytes_accessed=20_000_000,
@@ -365,22 +336,20 @@
     lists = make_lists(col_index[0], me, phase_of)
     cfg = dict(
         width=width, rows=rows, nonzeros=nonzeros, per_row=per_row, slots=slots,
-        members=members, groups=groups, late=slots <= 128,
+        members=members, groups=groups,
     )
-    pt, sums = None, []
+    pt = acc = None
     for p in range(phases):
-        last = p == phases - 1
-        use = [packed[r] for r in sources[p]]
-        before = (sums if last else []) if cfg["late"] else sums[-1:]
         outs = work(
-            {**cfg, "phase": p, "first": p == 0, "last": last, "from": sources[p][0]},
-            (lists, col_index[0], target[0]), a_blocks[0], use, pt, before,
+            {**cfg, "phase": p, "first": p == 0, "last": p == phases - 1, "from": sources[p][0]},
+            (lists, col_index[0], target[0]), a_blocks[0], [packed[r] for r in sources[p]], pt, acc,
         )
-        sums = sums + [outs[0]]
         if p == 0:
-            pt = outs[1]
-
-    keep, give = outs
+            acc, pt = outs
+        elif p < phases - 1:
+            (acc,) = outs
+
+    keep, give = outs[:2]
     total = keep + exchange(give, 1, "grp", groups).astype(f32)
     got = [exchange(total[:, r].astype(bf16), r) for r in range(1, members)]
     total = total[:, 0]

time: 102 us -> 99.1 us (0.972)
  Pallas kernels: 57.8 us -> 52.3 us
  local copies, waits for them, and re-layouts: 1.33 us -> 2.71 us
    pallas_call x3, Pallas kernels: 55.6 us -> 50.4 us  [work(): pl.pallas_call(functools.partial(work_kernel, cfg), grid_spec=pltpu.Prefe...]
    unnamed x2 -> x6, local copies, waits for them, and re-layouts: 0.92 us -> 2.3 us
  transfers between devices with their start and end apart: 10 -> 10, of which waited for: 6 -> 7; matrix products, arithmetic and copies ran while one was open for 2% -> 2% of each run, Pallas kernels for 39% -> 36%
where the time goes in v6:
time: 99.1 us; the launch traced here: 98.4 us
  Pallas kernels  52.3 us (53%)
  waiting for transfers between devices  24 us (24%)
  starting transfers between devices  13.7 us (14%)
  other arithmetic  5.49 us (6%)
  local copies, waits for them, and re-layouts  2.71 us (3%)
    pallas_call x3, Pallas kernels, work(): pl.pallas_call(functools.partial(work_kernel, cfg), grid_spec=pltpu.Prefe...  50.4 us
    ppermute x10, waiting for transfers between devices, exchange(): return lax.ppermute(x, axis, [(d, d ^ r) for d in range(size)])  24 us
    ppermute x10, starting transfers between devices, exchange(): return lax.ppermute(x, axis, [(d, d ^ r) for d in range(size)])  13.7 us
    unnamed x6, local copies, waits for them, and re-layouts  2.3 us
    another operation x2, other arithmetic  2.3 us
  transfers between devices with their start and end apart: 10, of which 7 were waited for; matrix products, arithmetic and copies ran while one was open for 2% of the time, Pallas kernels for 36%

profile of v6, /device:TPU:0, one launch (start us, length us, event | category | flops | bytes accessed | tf_op | source)
XLA Modules:
  0.0 98.4 jit_solution(10588863731306803819)
XLA Ops:
  0.0 1.3 %copy-done.2 = bf16[1,24,2,96,96]{4,3,2,1,0:T(8,128)(2,1)S(1)} copy-done((bf16[1,24,2,96,96]{4,3,2,1,0:T(8,128)(2,1)S(1)}, bf16[1,24,2,96,96]{4,3,2,1,0:T(8,128)(2,1)}, u32[]{:S(2)}) %copy-start.2) | copy-done | bytes 884760
  1.3 1.9 %pack_prolong.1.refs_4_ = bf16[12,3,96,128]{3,2,1,0:T(8,128)(2,1)S(1)} custom-call(bf16[12,4,96,96]{3,2,1,0:T(8,128)(2,1)S(1)} %bitcast.50), custom_call_target="tpu_custom_call" | custom-call | tf_op jit(solution)/shard_map/pack_prolong/pallas_call | solution.py:58
  3.2 3.0 %collective-permute-start.2 = (bf16[12,3,96,128]{3,2,1,0:T(8,128)(2,1)S(1)}, bf16[12,3,96,128]{3,2,1,0:T(8,128)(2,1)}, u32[]{:S(2)}, u32[]{:S(2)}) collective-permute-start(bf16[12,3,96,128]{3,2,1,0:T(8,128)(2,1)S(1)} %pack_prolong.1.refs_4_), channel_id=1, source_target_pairs={{0,16},{8,24},{16,0},{24,8},{1,17},{9,25},{17,1},{25,9},{2,18},{10... | collective-permute-start | bytes 2654216 | tf_op jit(solution)/shard_map/ppermute | solution.py:325
  6.2 1.5 %collective-permute-start.1 = (bf16[12,3,96,128]{3,2,1,0:T(8,128)(2,1)S(1)}, bf16[12,3,96,128]{3,2,1,0:T(8,128)(2,1)}, u32[]{:S(2)}, u32[]{:S(2)}) collective-permute-start(bf16[12,3,96,128]{3,2,1,0:T(8,128)(2,1)S(1)} %pack_prolong.1.refs_4_), channel_id=1, source_target_pairs={{0,8},{8,0},{16,24},{24,16},{1,9},{9,1},{17,25},{25,17},{2,10},{10... | collective-permute-start | bytes 2654216 | tf_op jit(solution)/shard_map/ppermute | solution.py:325
  7.8 0.7 add_add_fusion
  8.9 1.3 %select_reduce_fusion.refs_0_ = s32[3,672]{1,0:T(4,128)} fusion(s32[648]{0:T(1024)S(1)} %get-tuple-element.26, s32[3,672]{1,0:T(4,128)S(1)} %multiply_add_fusion, s32[648]{0:T(1024)S(1)} %get-tuple-element.27), kind=kLoop, calls=%fused_computation | loop fusion | flops 3917088 | bytes 21312 | tf_op jit(solution)/shard_map/reduce_sum | solution.py:310
  10.3 19.7 %work_0.1 = (f32[128,96,128]{2,1,0:T(8,128)S(1)}, bf16[24,192,96]{2,1,0:T(8,128)(2,1)S(1)}) custom-call(s32[3,672]{1,0:T(4,128)} %select_reduce_fusion.refs_0_, s32[24,27]{1,0:T(8,128)} %bitcast.55, s32[24,108]{1,0:T(8,128)} %bitcast.58, bf16[24,27,96,96]{3,2,1,0:T(8,128)(2,1)} %bitcast.51, bf16[12,3,96,128]{3,2,1,0:T(8,128)(2,1)} %copy-done.1), custom_call_target="tpu_custom_call" | custom-call | flops 2293235712 | bytes 20000000 | tf_op jit(solution)/shard_map/work_0/pallas_call | solution.py:266
  30.0 1.0 %copy-done = bf16[24,192,96]{2,1,0:T(8,128)(2,1)} copy-done((bf16[24,192,96]{2,1,0:T(8,128)(2,1)}, bf16[24,192,96]{2,1,0:T(8,128)(2,1)S(1)}, u32[]{:S(2)}) %copy-start) | copy-done | bytes 884760
  31.0 15.5 %work_1.1.refs_6_ = f32[128,96,128]{2,1,0:T(8,128)S(1)} custom-call(s32[3,672]{1,0:T(4,128)} %select_reduce_fusion.refs_0_, s32[24,27]{1,0:T(8,128)} %bitcast.56, s32[24,108]{1,0:T(8,128)} %bitcast.59, bf16[24,27,96,96]{3,2,1,0:T(8,128)(2,1)} %bitcast.52, bf16[12,3,96,128]{3,2,1,0:T(8,128)(2,1)} %collective-permute-done.1.refs_4_, ...), custom_call_target="tpu_custom_call", output_to_operand_aliasing={{}: (7, {})} | custom-call | flops 2293235712 | bytes 20000000 | tf_op jit(solution)/shard_map/work_1/pallas_call | solution.py:266
  46.6 15.1 %work_2.1 = (f32[4,4,3,96,128]{4,3,2,1,0:T(8,128)}, bf16[4,4,3,96,128]{4,3,2,1,0:T(8,128)(2,1)}, f32[128,96,128]{2,1,0:T(8,128)S(1)}) custom-call(s32[3,672]{1,0:T(4,128)} %select_reduce_fusion.refs_0_, s32[24,27]{1,0:T(8,128)} %bitcast.57, s32[24,108]{1,0:T(8,128)} %bitcast.60, bf16[24,27,96,96]{3,2,1,0:T(8,128)(2,1)} %bitcast.53, ...), custom_call_target="tpu_custom_call", output_to_operand_aliasing={{2}: (6, {})} | custom-call | flops 2293235712 | bytes 20000000 | tf_op jit(solution)/shard_map/work_2/pallas_call | solution.py:266
  61.8 3.0 %collective-permute-done.3 = bf16[4,4,3,96,128]{4,3,2,1,0:T(8,128)(2,1)S(1)} collective-permute-done((bf16[4,4,3,96,128]{4,3,2,1,0:T(8,128)(2,1)}, bf16[4,4,3,96,128]{4,3,2,1,0:T(8,128)(2,1)S(1)}, u32[]{:S(2)}, u32[]{:S(2)}) %collective-permute-start.3) | collective-permute-done | bytes 1179680 | tf_op jit(solution)/shard_map/ppermute | solution.py:325
  64.9 2.1 %fusion.19 = (bf16[4,4,3,96,128]{4,3,2,1,0:T(8,128)(2,1)S(1)}, f32[4,4,3,96,128]{4,3,2,1,0:T(8,128)S(1)}) fusion(f32[4,4,3,96,128]{4,3,2,1,0:T(8,128)} %get-tuple-element.11, bf16[4,4,3,96,128]{4,3,2,1,0:T(8,128)(2,1)S(1)} %collective-permute-done.3), kind=kLoop, calls=%fused_computation.43 | loop fusion | flops 1769472 | bytes 7077888 | tf_op jit(solution)/shard_map/convert.5
  67.1 3.6 %collective-permute-start.4 = (bf16[4,3,96,128]{3,2,1,0:T(8,128)(2,1)S(1)}, bf16[4,3,96,128]{3,2,1,0:T(8,128)(2,1)S(1)}, u32[]{:S(2)}, u32[]{:S(2)}) collective-permute-start(bf16[4,3,96,128]{3,2,1,0:T(8,128)(2,1)S(1)} %get-tuple-element.17), channel_id=1, source_target_pairs={{0,8},{8,0},{16,24},{24,16},{1,9},{9,1},{17,25},{25,17},{2,10},{10... | collective-permute-start | bytes 884744 | tf_op jit(solution)/shard_map/ppermute | solution.py:325
  70.7 1.2 %collective-permute-start.6 = (bf16[4,3,96,128]{3,2,1,0:T(8,128)(2,1)S(1)}, bf16[4,3,96,128]{3,2,1,0:T(8,128)(2,1)S(1)}, u32[]{:S(2)}, u32[]{:S(2)}) collective-permute-start(bf16[4,3,96,128]{3,2,1,0:T(8,128)(2,1)S(1)} %get-tuple-element.18), channel_id=1, source_target_pairs={{0,24},{8,16},{16,8},{24,0},{1,25},{9,17},{17,9},{25,1},{2,26},{10... | collective-permute-start | bytes 884744 | tf_op jit(solution)/shard_map/ppermute | solution.py:325
  72.0 0.5 collective-permute-start.5
  72.4 6.1 %collective-permute-done.4 = bf16[4,3,96,128]{3,2,1,0:T(8,128)(2,1)S(1)} collective-permute-done((bf16[4,3,96,128]{3,2,1,0:T(8,128)(2,1)S(1)}, bf16[4,3,96,128]{3,2,1,0:T(8,128)(2,1)S(1)}, u32[]{:S(2)}, u32[]{:S(2)}) %collective-permute-start.4) | collective-permute-done | bytes 294944 | tf_op jit(solution)/shard_map/ppermute | solution.py:325
  78.5 7.1 %collective-permute-done.6 = bf16[4,3,96,128]{3,2,1,0:T(8,128)(2,1)S(1)} collective-permute-done((bf16[4,3,96,128]{3,2,1,0:T(8,128)(2,1)S(1)}, bf16[4,3,96,128]{3,2,1,0:T(8,128)(2,1)S(1)}, u32[]{:S(2)}, u32[]{:S(2)}) %collective-permute-start.6) | collective-permute-done | bytes 294944 | tf_op jit(solution)/shard_map/ppermute | solution.py:325
  85.6 1.4 %collective-permute-done.5 = bf16[4,3,96,128]{3,2,1,0:T(8,128)(2,1)S(1)} collective-permute-done((bf16[4,3,96,128]{3,2,1,0:T(8,128)(2,1)S(1)}, bf16[4,3,96,128]{3,2,1,0:T(8,128)(2,1)S(1)}, u32[]{:S(2)}, u32[]{:S(2)}) %collective-permute-start.5) | collective-permute-done | bytes 294944 | tf_op jit(solution)/shard_map/ppermute | solution.py:325
  87.2 1.4 %collective-permute-start.7 = (bf16[3,96,128]{2,1,0:T(8,128)(2,1)S(1)}, bf16[3,96,128]{2,1,0:T(8,128)(2,1)S(1)}, u32[]{:S(2)}, u32[]{:S(2)}) collective-permute-start(bf16[3,96,128]{2,1,0:T(8,128)(2,1)S(1)} %get-tuple-element.20), channel_id=1, source_target_pairs={{0,2},{1,3},{2,0},{3,1},{4,6},{5,7},{6,4},{7,5},{8,10},{9,11},{10,... | collective-permute-start | bytes 221192 | tf_op jit(solution)/shard_map/ppermute | solution.py:325
  88.6 2.3 %collective-permute-start.9 = (bf16[3,96,128]{2,1,0:T(8,128)(2,1)S(1)}, bf16[3,96,128]{2,1,0:T(8,128)(2,1)S(1)}, u32[]{:S(2)}, u32[]{:S(2)}) collective-permute-start(bf16[3,96,128]{2,1,0:T(8,128)(2,1)S(1)} %get-tuple-element.21), channel_id=1, source_target_pairs={{0,6},{1,7},{2,4},{3,5},{4,2},{5,3},{6,0},{7,1},{8,14},{9,15},{10,... | collective-permute-start | bytes 221192 | tf_op jit(solution)/shard_map/ppermute | solution.py:325
  91.0 0.7 collective-permute-done.7
  91.6 3.3 %collective-permute-done.9 = bf16[3,96,128]{2,1,0:T(8,128)(2,1)S(1)} collective-permute-done((bf16[3,96,128]{2,1,0:T(8,128)(2,1)S(1)}, bf16[3,96,128]{2,1,0:T(8,128)(2,1)S(1)}, u32[]{:S(2)}, u32[]{:S(2)}) %collective-permute-start.9) | collective-permute-done | bytes 73760 | tf_op jit(solution)/shard_map/ppermute | solution.py:325
  94.9 2.4 %collective-permute-done.8 = bf16[3,96,128]{2,1,0:T(8,128)(2,1)S(1)} collective-permute-done((bf16[3,96,128]{2,1,0:T(8,128)(2,1)S(1)}, bf16[3,96,128]{2,1,0:T(8,128)(2,1)S(1)}, u32[]{:S(2)}, u32[]{:S(2)}) %collective-permute-start.8) | collective-permute-done | bytes 73760 | tf_op jit(solution)/shard_map/ppermute | solution.py:325
  97.7 0.7 maximum_bitcast_fusion
  (23 shorter events, 1.2 us)
Async XLA Ops:
  0.0 1.3 %copy-start.2 = (bf16[1,24,2,96,96]{4,3,2,1,0:T(8,128)(2,1)S(1)}, bf16[1,24,2,96,96]{4,3,2,1,0:T(8,128)(2,1)}, u32[]{:S(2)}) copy-start(bf16[1,24,2,96,96]{4,3,2,1,0:T(8,128)(2,1)} %param.6) | copy-start | bytes 2654212
  3.2 7.1 %copy-start.1 = (bf16[12,3,96,128]{3,2,1,0:T(8,128)(2,1)}, bf16[12,3,96,128]{3,2,1,0:T(8,128)(2,1)S(1)}, u32[]{:S(2)}) copy-start(bf16[12,3,96,128]{3,2,1,0:T(8,128)(2,1)S(1)} %pack_prolong.1.refs_4_) | copy-start | bytes 2654212
  3.2 27.8 %collective-permute-start.2 = (bf16[12,3,96,128]{3,2,1,0:T(8,128)(2,1)S(1)}, bf16[12,3,96,128]{3,2,1,0:T(8,128)(2,1)}, u32[]{:S(2)}, u32[]{:S(2)}) collective-permute-start(bf16[12,3,96,128]{3,2,1,0:T(8,128)(2,1)S(1)} %pack_prolong.1.refs_4_), channel_id=1, source_target_pairs={{0,16},{8,24},{16,0},{24,8},{1,17},{9,25},{17,1},{25,9},{2,18},{10... | collective-permute-start | bytes 2654216 | tf_op jit(solution)/shard_map/ppermute | solution.py:325
  6.2 24.8 %collective-permute-start.1 = (bf16[12,3,96,128]{3,2,1,0:T(8,128)(2,1)S(1)}, bf16[12,3,96,128]{3,2,1,0:T(8,128)(2,1)}, u32[]{:S(2)}, u32[]{:S(2)}) collective-permute-start(bf16[12,3,96,128]{3,2,1,0:T(8,128)(2,1)S(1)} %pack_prolong.1.refs_4_), channel_id=1, source_target_pairs={{0,8},{8,0},{16,24},{24,16},{1,9},{9,1},{17,25},{25,17},{2,10},{10... | collective-permute-start | bytes 2654216 | tf_op jit(solution)/shard_map/ppermute | solution.py:325
  7.7 38.8 %collective-permute-start = (bf16[12,3,96,128]{3,2,1,0:T(8,128)(2,1)S(1)}, bf16[12,3,96,128]{3,2,1,0:T(8,128)(2,1)}, u32[]{:S(2)}, u32[]{:S(2)}) collective-permute-start(bf16[12,3,96,128]{3,2,1,0:T(8,128)(2,1)S(1)} %pack_prolong.1.refs_4_), channel_id=1, source_target_pairs={{0,24},{8,16},{16,8},{24,0},{1,25},{9,17},{17,9},{25,1},{2,26},{10... | collective-permute-start | bytes 2654216 | tf_op jit(solution)/shard_map/ppermute | solution.py:325
  30.0 1.0 %copy-start = (bf16[24,192,96]{2,1,0:T(8,128)(2,1)}, bf16[24,192,96]{2,1,0:T(8,128)(2,1)S(1)}, u32[]{:S(2)}) copy-start(bf16[24,192,96]{2,1,0:T(8,128)(2,1)S(1)} %get-tuple-element.9.refs_6_.refs_5_) | copy-start | bytes 2654212
  61.7 3.1 %collective-permute-start.3 = (bf16[4,4,3,96,128]{4,3,2,1,0:T(8,128)(2,1)}, bf16[4,4,3,96,128]{4,3,2,1,0:T(8,128)(2,1)S(1)}, u32[]{:S(2)}, u32[]{:S(2)}) collective-permute-start(bf16[4,4,3,96,128]{4,3,2,1,0:T(8,128)(2,1)} %get-tuple-element.12), channel_id=1, source_target_pairs={{0,1},{1,0},{2,3},{3,2},{4,5},{5,4},{6,7},{7,6},{8,9},{9,8},{10,11... | collective-permute-start | bytes 3538952 | tf_op jit(solution)/shard_map/ppermute | solution.py:325
  67.1 11.4 %collective-permute-start.4 = (bf16[4,3,96,128]{3,2,1,0:T(8,128)(2,1)S(1)}, bf16[4,3,96,128]{3,2,1,0:T(8,128)(2,1)S(1)}, u32[]{:S(2)}, u32[]{:S(2)}) collective-permute-start(bf16[4,3,96,128]{3,2,1,0:T(8,128)(2,1)S(1)} %get-tuple-element.17), channel_id=1, source_target_pairs={{0,8},{8,0},{16,24},{24,16},{1,9},{9,1},{17,25},{25,17},{2,10},{10... | collective-permute-start | bytes 884744 | tf_op jit(solution)/shard_map/ppermute | solution.py:325
  70.7 14.9 %collective-permute-start.6 = (bf16[4,3,96,128]{3,2,1,0:T(8,128)(2,1)S(1)}, bf16[4,3,96,128]{3,2,1,0:T(8,128)(2,1)S(1)}, u32[]{:S(2)}, u32[]{:S(2)}) collective-permute-start(bf16[4,3,96,128]{3,2,1,0:T(8,128)(2,1)S(1)} %get-tuple-element.18), channel_id=1, source_target_pairs={{0,24},{8,16},{16,8},{24,0},{1,25},{9,17},{17,9},{25,1},{2,26},{10... | collective-permute-start | bytes 884744 | tf_op jit(solution)/shard_map/ppermute | solution.py:325
  72.0 15.1 %collective-permute-start.5 = (bf16[4,3,96,128]{3,2,1,0:T(8,128)(2,1)S(1)}, bf16[4,3,96,128]{3,2,1,0:T(8,128)(2,1)S(1)}, u32[]{:S(2)}, u32[]{:S(2)}) collective-permute-start(bf16[4,3,96,128]{3,2,1,0:T(8,128)(2,1)S(1)} %get-tuple-element.19), channel_id=1, source_target_pairs={{0,16},{8,24},{16,0},{24,8},{1,17},{9,25},{17,1},{25,9},{2,18},{10... | collective-permute-start | bytes 884744 | tf_op jit(solution)/shard_map/ppermute | solution.py:325
  87.2 4.4 %collective-permute-start.7 = (bf16[3,96,128]{2,1,0:T(8,128)(2,1)S(1)}, bf16[3,96,128]{2,1,0:T(8,128)(2,1)S(1)}, u32[]{:S(2)}, u32[]{:S(2)}) collective-permute-start(bf16[3,96,128]{2,1,0:T(8,128)(2,1)S(1)} %get-tuple-element.20), channel_id=1, source_target_pairs={{0,2},{1,3},{2,0},{3,1},{4,6},{5,7},{6,4},{7,5},{8,10},{9,11},{10,... | collective-permute-start | bytes 221192 | tf_op jit(solution)/shard_map/ppermute | solution.py:325
  88.6 6.3 %collective-permute-start.9 = (bf16[3,96,128]{2,1,0:T(8,128)(2,1)S(1)}, bf16[3,96,128]{2,1,0:T(8,128)(2,1)S(1)}, u32[]{:S(2)}, u32[]{:S(2)}) collective-permute-start(bf16[3,96,128]{2,1,0:T(8,128)(2,1)S(1)} %get-tuple-element.21), channel_id=1, source_target_pairs={{0,6},{1,7},{2,4},{3,5},{4,2},{5,3},{6,0},{7,1},{8,14},{9,15},{10,... | collective-permute-start | bytes 221192 | tf_op jit(solution)/shard_map/ppermute | solution.py:325
  91.0 6.3 %collective-permute-start.8 = (bf16[3,96,128]{2,1,0:T(8,128)(2,1)S(1)}, bf16[3,96,128]{2,1,0:T(8,128)(2,1)S(1)}, u32[]{:S(2)}, u32[]{:S(2)}) collective-permute-start(bf16[3,96,128]{2,1,0:T(8,128)(2,1)S(1)} %get-tuple-element.22), channel_id=1, source_target_pairs={{0,4},{1,5},{2,6},{3,7},{4,0},{5,1},{6,2},{7,3},{8,12},{9,13},{10,... | collective-permute-start | bytes 221192 | tf_op jit(solution)/shard_map/ppermute | solution.py:325

commit v7 on v6

--- a/solution.py
+++ b/solution.py
@@ -8,7 +8,7 @@
 from jax.sharding import PartitionSpec as P
 
 OWN = 4
-UNROLL = 16
+UNROLL = 24
 LANES = 128
 AHEAD = 12
 VMEM = 64 * 1024 * 1024
@@ -66,7 +66,7 @@
             pltpu.SemaphoreType.DMA((steps,)),
             pltpu.SemaphoreType.DMA((steps,)),
         ],
-        compiler_params=pltpu.CompilerParams(vmem_limit_bytes=VMEM // 2),
+        compiler_params=pltpu.CompilerParams(vmem_limit_bytes=VMEM - 128 * 1024),
         name="pack_prolong",
     )(prolong.reshape(quads, 4, width, width))
 
@@ -85,12 +85,9 @@
     take = lambda n: [refs.pop(0) for _ in range(n)]
     list_ref, col_ref, tgt_ref, a_hbm = take(4)
     p_hbm = take(cfg["sources"])
-    if not first:
-        pt, _ = take(2)
+    take(0 if first else 2)
     out_refs = take(2 if last else 0)
-    (acc,) = take(1)
-    if first:
-        (pt,) = take(1)
+    acc, pt = take(2)
     p_vmem, a_rows = take(2)
     aps = take(UNROLL)
     a_sem, sem, out_sem = take(3)
@@ -239,7 +236,7 @@
             pltpu.make_async_copy(stages[rc], out_refs[rc], out_sem.at[rc]).wait()
 
 
-def work(cfg, tables, a_rows, packed, pt=None, acc=None):
+def work(cfg, tables, a_rows, packed, acc=None, pt=None):
     width, rows, nonzeros, per_row = cfg["width"], cfg["rows"], cfg["nonzeros"], cfg["per_row"]
     slots, members, groups = cfg["slots"], cfg["members"], cfg["groups"]
     first, last = cfg["first"], cfg["last"]
@@ -247,22 +244,22 @@
     quads = sum(x.shape[0] for x in packed)
     vmem = pl.BlockSpec(memory_space=pltpu.VMEM)
     operands = [a_rows, *packed]
-    in_specs, out_specs = [HBM] * len(operands), [vmem]
-    shapes, stages, aliases = [pltpu.VMEM((slots, width, LANES), jnp.float32)], [], {}
+    in_specs, out_specs = [HBM] * len(operands), [vmem] * 2
+    shapes, stages, aliases = [
+        pltpu.VMEM((slots, width, LANES), jnp.float32),
+        pltpu.VMEM((rows, per_row * width, width), jnp.bfloat16),
+    ], [], {}
     resident = slots * width * LANES * 4 + rows * per_row * width * LANES * 2
-    if first:
-        shapes.append(pltpu.VMEM((rows, per_row * width, width), jnp.bfloat16))
-        out_specs.append(vmem)
-    else:
-        operands += [pt, acc]
-        in_specs += [vmem, vmem]
+    if not first:
+        operands += [acc, pt]
+        in_specs += [vmem] * 2
     if last:
         whole = (groups // 2, members, 3, width, LANES)
         made = [jax.ShapeDtypeStruct(whole, jnp.float32), jax.ShapeDtypeStruct(whole, jnp.bfloat16)]
         stages = [pltpu.VMEM(x.shape, x.dtype) for x in made]
         shapes, out_specs = made + shapes, [HBM] * 2 + out_specs
     if not first:
-        aliases = {len(tables) + len(operands) - 1: len(shapes) - 1}
+        aliases = {len(tables) + len(operands) - x: len(shapes) - x for x in (1, 2)}
     return pl.pallas_call(
         functools.partial(work_kernel, cfg),
         grid_spec=pltpu.PrefetchScalarGridSpec(
@@ -338,16 +335,13 @@
         width=width, rows=rows, nonzeros=nonzeros, per_row=per_row, slots=slots,
         members=members, groups=groups,
     )
-    pt = acc = None
+    acc = pt = None
     for p in range(phases):
         outs = work(
             {**cfg, "phase": p, "first": p == 0, "last": p == phases - 1, "from": sources[p][0]},
-            (lists, col_index[0], target[0]), a_blocks[0], [packed[r] for r in sources[p]], pt, acc,
+            (lists, col_index[0], target[0]), a_blocks[0], [packed[r] for r in sources[p]], acc, pt,
         )
-        if p == 0:
-            acc, pt = outs
-        elif p < phases - 1:
-            (acc,) = outs
+        acc, pt = outs[-2:]
 
     keep, give = outs[:2]
     total = keep + exchange(give, 1, "grp", groups).astype(f32)

time: 99.1 us -> 96.8 us (0.977)
  Pallas kernels: 52.3 us -> 48.5 us
  waiting for transfers between devices: 24 us -> 27.1 us
  local copies, waits for them, and re-layouts: 2.71 us -> 1.32 us
    pallas_call x3, Pallas kernels: 50.4 us -> 46.3 us  [work(): pl.pallas_call(functools.partial(work_kernel, cfg), grid_spec=pltpu.Prefe...]
    ppermute x10, waiting for transfers between devices: 24 us -> 27.1 us  [exchange(): return lax.ppermute(x, axis, [(d, d ^ r) for d in range(size)])]
    unnamed x6 -> x4, local copies, waits for them, and re-layouts: 2.3 us -> 0.91 us
  transfers between devices with their start and end apart: 10 -> 10, of which waited for: 7 -> 8; matrix products, arithmetic and copies ran while one was open for 2% -> 2% of each run, Pallas kernels for 36% -> 34%
where the time goes in v7:
time: 96.8 us; the launch traced here: 96.4 us
  Pallas kernels  48.5 us (50%)
  waiting for transfers between devices  27.1 us (28%)
  starting transfers between devices  14.5 us (15%)
  other arithmetic  4.79 us (5%)
  local copies, waits for them, and re-layouts  1.32 us (1%)
    pallas_call x3, Pallas kernels, work(): pl.pallas_call(functools.partial(work_kernel, cfg), grid_spec=pltpu.Prefe...  46.3 us
    ppermute x10, waiting for transfers between devices, exchange(): return lax.ppermute(x, axis, [(d, d ^ r) for d in range(size)])  27.1 us
    ppermute x10, starting transfers between devices, exchange(): return lax.ppermute(x, axis, [(d, d ^ r) for d in range(size)])  14.5 us
    another operation x2, other arithmetic  2.3 us
    pallas_call x1, Pallas kernels, pack_prolong(): pl.pallas_call(pack_kernel, in_specs=[HBM], out_specs=HBM, out_shape=jax....  2.24 us
  transfers between devices with their start and end apart: 10, of which 8 were waited for; matrix products, arithmetic and copies ran while one was open for 2% of the time, Pallas kernels for 34%

profile of v7, /device:TPU:0, one launch (start us, length us, event | category | flops | bytes accessed | tf_op | source)
XLA Modules:
  0.0 96.4 jit_solution(16171676954242927147)
XLA Ops:
  0.0 2.2 %pack_prolong.1.refs_4_ = bf16[12,3,96,128]{3,2,1,0:T(8,128)(2,1)} custom-call(bf16[12,4,96,96]{3,2,1,0:T(8,128)(2,1)} %bitcast.54), custom_call_target="tpu_custom_call" | custom-call | tf_op jit(solution)/shard_map/pack_prolong/pallas_call | solution.py:58
  2.2 3.0 %collective-permute-start.2 = (bf16[12,3,96,128]{3,2,1,0:T(8,128)(2,1)}, bf16[12,3,96,128]{3,2,1,0:T(8,128)(2,1)}, u32[]{:S(2)}, u32[]{:S(2)}) collective-permute-start(bf16[12,3,96,128]{3,2,1,0:T(8,128)(2,1)} %pack_prolong.1.refs_4_), channel_id=1, source_target_pairs={{0,16},{8,24},{16,0},{24,8},{1,17},{9,25},{17,1},{25,9},{2,18},{10... | collective-permute-start | bytes 2654216 | tf_op jit(solution)/shard_map/ppermute | solution.py:322
  5.3 1.5 %collective-permute-start.1 = (bf16[12,3,96,128]{3,2,1,0:T(8,128)(2,1)}, bf16[12,3,96,128]{3,2,1,0:T(8,128)(2,1)}, u32[]{:S(2)}, u32[]{:S(2)}) collective-permute-start(bf16[12,3,96,128]{3,2,1,0:T(8,128)(2,1)} %pack_prolong.1.refs_4_), channel_id=1, source_target_pairs={{0,8},{8,0},{16,24},{24,16},{1,9},{9,1},{17,25},{25,17},{2,10},{10... | collective-permute-start | bytes 2654216 | tf_op jit(solution)/shard_map/ppermute | solution.py:322
  6.9 0.3 convert_reduce_fusion
  7.3 1.3 %select_reduce_fusion.refs_0_ = s32[3,672]{1,0:T(4,128)} fusion(s32[648]{0:T(1024)S(1)} %get-tuple-element.30, s32[3,672]{1,0:T(4,128)S(1)} %multiply_add_fusion, s32[648]{0:T(1024)S(1)} %get-tuple-element.31), kind=kLoop, calls=%fused_computation | loop fusion | flops 3917088 | bytes 21312 | tf_op jit(solution)/shard_map/reduce_sum | solution.py:307
  8.6 19.0 %work_0.1 = (f32[128,96,128]{2,1,0:T(8,128)S(1)}, bf16[24,192,96]{2,1,0:T(8,128)(2,1)S(1)}) custom-call(s32[3,672]{1,0:T(4,128)} %select_reduce_fusion.refs_0_, s32[24,27]{1,0:T(8,128)} %bitcast.55, s32[24,108]{1,0:T(8,128)} %bitcast.58, bf16[24,27,96,96]{3,2,1,0:T(8,128)(2,1)} %bitcast.50, bf16[12,3,96,128]{3,2,1,0:T(8,128)(2,1)} %pack_prolong.1.refs_4_), custom_call_target="tpu_custom_call" | custom-call | flops 2293235712 | bytes 20000000 | tf_op jit(solution)/shard_map/work_0/pallas_call | solution.py:263
  27.6 0.5 collective-permute-done.1.refs_4_
  28.2 13.7 %work_1.1 = (f32[128,96,128]{2,1,0:T(8,128)S(1)}, bf16[24,192,96]{2,1,0:T(8,128)(2,1)S(1)}) custom-call(s32[3,672]{1,0:T(4,128)} %select_reduce_fusion.refs_0_, s32[24,27]{1,0:T(8,128)} %bitcast.56, s32[24,108]{1,0:T(8,128)} %bitcast.59, bf16[24,27,96,96]{3,2,1,0:T(8,128)(2,1)} %bitcast.51, ...), custom_call_target="tpu_custom_call", output_to_operand_aliasing={{1}: (7, {}), {0}: (6, {})} | custom-call | flops 2293235712 | bytes 20000000 | tf_op jit(solution)/shard_map/work_1/pallas_call | solution.py:263
  41.8 3.5 %collective-permute-done.refs_4_ = bf16[12,3,96,128]{3,2,1,0:T(8,128)(2,1)S(1)} collective-permute-done((bf16[12,3,96,128]{3,2,1,0:T(8,128)(2,1)}, bf16[12,3,96,128]{3,2,1,0:T(8,128)(2,1)S(1)}, u32[]{:S(2)}, u32[]{:S(2)}) %collective-permute-start) | collective-permute-done | bytes 884768 | tf_op jit(solution)/shard_map/ppermute | solution.py:322
  45.4 0.9 copy-done
  46.3 13.6 %work_2.1 = (f32[4,4,3,96,128]{4,3,2,1,0:T(8,128)}, bf16[4,4,3,96,128]{4,3,2,1,0:T(8,128)(2,1)}, f32[128,96,128]{2,1,0:T(8,128)S(1)}, bf16[24,192,96]{2,1,0:T(8,128)(2,1)S(1)}) custom-call(s32[3,672]{1,0:T(4,128)} %select_reduce_fusion.refs_0_, s32[24,27]{1,0:T(8,128)} %bitcast.57, ...), custom_call_target="tpu_custom_call", output_to_operand_aliasing={{3}: (6, {}), {2}: (5, {})} | custom-call | flops 2293235712 | bytes 20000000 | tf_op jit(solution)/shard_map/work_2/pallas_call | solution.py:263
  60.0 3.0 %collective-permute-done.3 = bf16[4,4,3,96,128]{4,3,2,1,0:T(8,128)(2,1)S(1)} collective-permute-done((bf16[4,4,3,96,128]{4,3,2,1,0:T(8,128)(2,1)}, bf16[4,4,3,96,128]{4,3,2,1,0:T(8,128)(2,1)S(1)}, u32[]{:S(2)}, u32[]{:S(2)}) %collective-permute-start.3) | collective-permute-done | bytes 1179680 | tf_op jit(solution)/shard_map/ppermute | solution.py:322
  63.0 2.1 %fusion.19 = (bf16[4,4,3,96,128]{4,3,2,1,0:T(8,128)(2,1)S(1)}, f32[4,4,3,96,128]{4,3,2,1,0:T(8,128)S(1)}) fusion(f32[4,4,3,96,128]{4,3,2,1,0:T(8,128)} %get-tuple-element.15, bf16[4,4,3,96,128]{4,3,2,1,0:T(8,128)(2,1)S(1)} %collective-permute-done.3), kind=kLoop, calls=%fused_computation.43 | loop fusion | flops 1769472 | bytes 7077888 | tf_op jit(solution)/shard_map/convert.5
  65.2 3.4 %collective-permute-start.4 = (bf16[4,3,96,128]{3,2,1,0:T(8,128)(2,1)S(1)}, bf16[4,3,96,128]{3,2,1,0:T(8,128)(2,1)S(1)}, u32[]{:S(2)}, u32[]{:S(2)}) collective-permute-start(bf16[4,3,96,128]{3,2,1,0:T(8,128)(2,1)S(1)} %get-tuple-element.21), channel_id=1, source_target_pairs={{0,8},{8,0},{16,24},{24,16},{1,9},{9,1},{17,25},{25,17},{2,10},{10... | collective-permute-start | bytes 884744 | tf_op jit(solution)/shard_map/ppermute | solution.py:322
  68.6 0.9 collective-permute-start.6
  69.5 0.6 collective-permute-start.5
  70.2 6.3 %collective-permute-done.4 = bf16[4,3,96,128]{3,2,1,0:T(8,128)(2,1)S(1)} collective-permute-done((bf16[4,3,96,128]{3,2,1,0:T(8,128)(2,1)S(1)}, bf16[4,3,96,128]{3,2,1,0:T(8,128)(2,1)S(1)}, u32[]{:S(2)}, u32[]{:S(2)}) %collective-permute-start.4) | collective-permute-done | bytes 294944 | tf_op jit(solution)/shard_map/ppermute | solution.py:322
  76.4 6.6 %collective-permute-done.6 = bf16[4,3,96,128]{3,2,1,0:T(8,128)(2,1)S(1)} collective-permute-done((bf16[4,3,96,128]{3,2,1,0:T(8,128)(2,1)S(1)}, bf16[4,3,96,128]{3,2,1,0:T(8,128)(2,1)S(1)}, u32[]{:S(2)}, u32[]{:S(2)}) %collective-permute-start.6) | collective-permute-done | bytes 294944 | tf_op jit(solution)/shard_map/ppermute | solution.py:322
  83.0 1.4 %collective-permute-done.5 = bf16[4,3,96,128]{3,2,1,0:T(8,128)(2,1)S(1)} collective-permute-done((bf16[4,3,96,128]{3,2,1,0:T(8,128)(2,1)S(1)}, bf16[4,3,96,128]{3,2,1,0:T(8,128)(2,1)S(1)}, u32[]{:S(2)}, u32[]{:S(2)}) %collective-permute-start.5) | collective-permute-done | bytes 294944 | tf_op jit(solution)/shard_map/ppermute | solution.py:322
  84.5 1.5 %collective-permute-start.7 = (bf16[3,96,128]{2,1,0:T(8,128)(2,1)S(1)}, bf16[3,96,128]{2,1,0:T(8,128)(2,1)S(1)}, u32[]{:S(2)}, u32[]{:S(2)}) collective-permute-start(bf16[3,96,128]{2,1,0:T(8,128)(2,1)S(1)} %get-tuple-element.24), channel_id=1, source_target_pairs={{0,2},{1,3},{2,0},{3,1},{4,6},{5,7},{6,4},{7,5},{8,10},{9,11},{10,... | collective-permute-start | bytes 221192 | tf_op jit(solution)/shard_map/ppermute | solution.py:322
  86.0 3.4 %collective-permute-start.9 = (bf16[3,96,128]{2,1,0:T(8,128)(2,1)S(1)}, bf16[3,96,128]{2,1,0:T(8,128)(2,1)S(1)}, u32[]{:S(2)}, u32[]{:S(2)}) collective-permute-start(bf16[3,96,128]{2,1,0:T(8,128)(2,1)S(1)} %get-tuple-element.25), channel_id=1, source_target_pairs={{0,6},{1,7},{2,4},{3,5},{4,2},{5,3},{6,0},{7,1},{8,14},{9,15},{10,... | collective-permute-start | bytes 221192 | tf_op jit(solution)/shard_map/ppermute | solution.py:322
  89.4 3.6 %collective-permute-done.9 = bf16[3,96,128]{2,1,0:T(8,128)(2,1)S(1)} collective-permute-done((bf16[3,96,128]{2,1,0:T(8,128)(2,1)S(1)}, bf16[3,96,128]{2,1,0:T(8,128)(2,1)S(1)}, u32[]{:S(2)}, u32[]{:S(2)}) %collective-permute-start.9) | collective-permute-done | bytes 73760 | tf_op jit(solution)/shard_map/ppermute | solution.py:322
  93.0 2.3 %collective-permute-done.8 = bf16[3,96,128]{2,1,0:T(8,128)(2,1)S(1)} collective-permute-done((bf16[3,96,128]{2,1,0:T(8,128)(2,1)S(1)}, bf16[3,96,128]{2,1,0:T(8,128)(2,1)S(1)}, u32[]{:S(2)}, u32[]{:S(2)}) %collective-permute-start.8) | collective-permute-done | bytes 73760 | tf_op jit(solution)/shard_map/ppermute | solution.py:322
  95.7 0.7 maximum_bitcast_fusion
  (21 shorter events, 0.9 us)
Async XLA Ops:
  0.0 6.8 %copy-start.1 = (s32[1,24,27]{2,1,0:T(8,128)S(1)}, s32[1,24,27]{2,1,0:T(8,128)}, u32[]{:S(2)}) copy-start(s32[1,24,27]{2,1,0:T(8,128)} %param.5) | copy-start | bytes 7780
  2.2 25.4 %collective-permute-start.2 = (bf16[12,3,96,128]{3,2,1,0:T(8,128)(2,1)}, bf16[12,3,96,128]{3,2,1,0:T(8,128)(2,1)}, u32[]{:S(2)}, u32[]{:S(2)}) collective-permute-start(bf16[12,3,96,128]{3,2,1,0:T(8,128)(2,1)} %pack_prolong.1.refs_4_), channel_id=1, source_target_pairs={{0,16},{8,24},{16,0},{24,8},{1,17},{9,25},{17,1},{25,9},{2,18},{10... | collective-permute-start | bytes 2654216 | tf_op jit(solution)/shard_map/ppermute | solution.py:322
  5.3 22.9 %collective-permute-start.1 = (bf16[12,3,96,128]{3,2,1,0:T(8,128)(2,1)}, bf16[12,3,96,128]{3,2,1,0:T(8,128)(2,1)}, u32[]{:S(2)}, u32[]{:S(2)}) collective-permute-start(bf16[12,3,96,128]{3,2,1,0:T(8,128)(2,1)} %pack_prolong.1.refs_4_), channel_id=1, source_target_pairs={{0,8},{8,0},{16,24},{24,16},{1,9},{9,1},{17,25},{25,17},{2,10},{10... | collective-permute-start | bytes 2654216 | tf_op jit(solution)/shard_map/ppermute | solution.py:322
  6.8 38.6 %collective-permute-start = (bf16[12,3,96,128]{3,2,1,0:T(8,128)(2,1)}, bf16[12,3,96,128]{3,2,1,0:T(8,128)(2,1)S(1)}, u32[]{:S(2)}, u32[]{:S(2)}) collective-permute-start(bf16[12,3,96,128]{3,2,1,0:T(8,128)(2,1)} %pack_prolong.1.refs_4_), channel_id=1, source_target_pairs={{0,24},{8,16},{16,8},{24,0},{1,25},{9,17},{17,9},{25,1},{2,26},{10... | collective-permute-start | bytes 2654216 | tf_op jit(solution)/shard_map/ppermute | solution.py:322
  45.4 0.9 copy-start
  59.9 3.1 %collective-permute-start.3 = (bf16[4,4,3,96,128]{4,3,2,1,0:T(8,128)(2,1)}, bf16[4,4,3,96,128]{4,3,2,1,0:T(8,128)(2,1)S(1)}, u32[]{:S(2)}, u32[]{:S(2)}) collective-permute-start(bf16[4,4,3,96,128]{4,3,2,1,0:T(8,128)(2,1)} %get-tuple-element.16), channel_id=1, source_target_pairs={{0,1},{1,0},{2,3},{3,2},{4,5},{5,4},{6,7},{7,6},{8,9},{9,8},{10,11... | collective-permute-start | bytes 3538952 | tf_op jit(solution)/shard_map/ppermute | solution.py:322
  65.2 11.2 %collective-permute-start.4 = (bf16[4,3,96,128]{3,2,1,0:T(8,128)(2,1)S(1)}, bf16[4,3,96,128]{3,2,1,0:T(8,128)(2,1)S(1)}, u32[]{:S(2)}, u32[]{:S(2)}) collective-permute-start(bf16[4,3,96,128]{3,2,1,0:T(8,128)(2,1)S(1)} %get-tuple-element.21), channel_id=1, source_target_pairs={{0,8},{8,0},{16,24},{24,16},{1,9},{9,1},{17,25},{25,17},{2,10},{10... | collective-permute-start | bytes 884744 | tf_op jit(solution)/shard_map/ppermute | solution.py:322
  68.6 14.4 %collective-permute-start.6 = (bf16[4,3,96,128]{3,2,1,0:T(8,128)(2,1)S(1)}, bf16[4,3,96,128]{3,2,1,0:T(8,128)(2,1)S(1)}, u32[]{:S(2)}, u32[]{:S(2)}) collective-permute-start(bf16[4,3,96,128]{3,2,1,0:T(8,128)(2,1)S(1)} %get-tuple-element.22), channel_id=1, source_target_pairs={{0,24},{8,16},{16,8},{24,0},{1,25},{9,17},{17,9},{25,1},{2,26},{10... | collective-permute-start | bytes 884744 | tf_op jit(solution)/shard_map/ppermute | solution.py:322
  69.5 14.8 %collective-permute-start.5 = (bf16[4,3,96,128]{3,2,1,0:T(8,128)(2,1)S(1)}, bf16[4,3,96,128]{3,2,1,0:T(8,128)(2,1)S(1)}, u32[]{:S(2)}, u32[]{:S(2)}) collective-permute-start(bf16[4,3,96,128]{3,2,1,0:T(8,128)(2,1)S(1)} %get-tuple-element.23), channel_id=1, source_target_pairs={{0,16},{8,24},{16,0},{24,8},{1,17},{9,25},{17,1},{25,9},{2,18},{10... | collective-permute-start | bytes 884744 | tf_op jit(solution)/shard_map/ppermute | solution.py:322
  84.5 4.9 %collective-permute-start.7 = (bf16[3,96,128]{2,1,0:T(8,128)(2,1)S(1)}, bf16[3,96,128]{2,1,0:T(8,128)(2,1)S(1)}, u32[]{:S(2)}, u32[]{:S(2)}) collective-permute-start(bf16[3,96,128]{2,1,0:T(8,128)(2,1)S(1)} %get-tuple-element.24), channel_id=1, source_target_pairs={{0,2},{1,3},{2,0},{3,1},{4,6},{5,7},{6,4},{7,5},{8,10},{9,11},{10,... | collective-permute-start | bytes 221192 | tf_op jit(solution)/shard_map/ppermute | solution.py:322
  86.0 7.0 %collective-permute-start.9 = (bf16[3,96,128]{2,1,0:T(8,128)(2,1)S(1)}, bf16[3,96,128]{2,1,0:T(8,128)(2,1)S(1)}, u32[]{:S(2)}, u32[]{:S(2)}) collective-permute-start(bf16[3,96,128]{2,1,0:T(8,128)(2,1)S(1)} %get-tuple-element.25), channel_id=1, source_target_pairs={{0,6},{1,7},{2,4},{3,5},{4,2},{5,3},{6,0},{7,1},{8,14},{9,15},{10,... | collective-permute-start | bytes 221192 | tf_op jit(solution)/shard_map/ppermute | solution.py:322
  89.4 5.9 %collective-permute-start.8 = (bf16[3,96,128]{2,1,0:T(8,128)(2,1)S(1)}, bf16[3,96,128]{2,1,0:T(8,128)(2,1)S(1)}, u32[]{:S(2)}, u32[]{:S(2)}) collective-permute-start(bf16[3,96,128]{2,1,0:T(8,128)(2,1)S(1)} %get-tuple-element.26), channel_id=1, source_target_pairs={{0,4},{1,5},{2,6},{3,7},{4,0},{5,1},{6,2},{7,3},{8,12},{9,13},{10,... | collective-permute-start | bytes 221192 | tf_op jit(solution)/shard_map/ppermute | solution.py:322

commit v8 on v7

--- a/solution.py
+++ b/solution.py
@@ -8,9 +8,10 @@
 from jax.sharding import PartitionSpec as P
 
 OWN = 4
-UNROLL = 24
+UNROLL = 32
 LANES = 128
-AHEAD = 12
+CHUNK = 3
+AHEAD = 4
 VMEM = 64 * 1024 * 1024
 HBM = pl.BlockSpec(memory_space=pl.ANY)
 
@@ -30,15 +31,17 @@
 
 
 def pack_kernel(p_hbm, *refs):
-    out, blocks, packed, in_sem, out_sem = refs
+    outs, (blocks, packed, in_sem, out_sem) = refs[:2], refs[2:]
     width, quads = p_hbm.shape[-1], p_hbm.shape[0]
     steps = in_sem.shape[0]
     size = quads // steps
+    half = steps // 2
     loads, stores = [], []
     for c in range(steps):
         part = pl.ds(c * size, size)
+        to = outs[c // half].at[pl.ds(c % half * size, size)]
         loads.append(pltpu.make_async_copy(p_hbm.at[part], blocks.at[part], in_sem.at[c]))
-        stores.append(pltpu.make_async_copy(packed.at[part], out.at[part], out_sem.at[c]))
+        stores.append(pltpu.make_async_copy(packed.at[part], to, out_sem.at[c]))
         loads[c].start()
     for c in range(steps):
         loads[c].wait()
@@ -58,8 +61,8 @@
     return pl.pallas_call(
         pack_kernel,
         in_specs=[HBM],
-        out_specs=HBM,
-        out_shape=jax.ShapeDtypeStruct((quads, 3, width, LANES), dtype),
+        out_specs=[HBM] * 2,
+        out_shape=[jax.ShapeDtypeStruct((quads // 2, 3, width, LANES), dtype)] * 2,
         scratch_shapes=[
             pltpu.VMEM((quads, 4, width, width), dtype),
             pltpu.VMEM((quads, 3, width, LANES), dtype),
@@ -97,20 +100,23 @@
     rank = lax.axis_index("grp").astype(jnp.int32)
     chip, core = rank >> 1, rank & 1
 
-    def a_copy(i):
-        to = a_rows.at[pl.ds((i + 1) * nonzeros, nonzeros)]
-        return pltpu.make_async_copy(a_hbm.at[i], to, a_sem.at[i])
-
-    def start_row(i, _):
-        a_copy(i).start()
+    chunks = rows // CHUNK
+
+    def a_copy(c):
+        blocks = CHUNK * nonzeros
+        to = a_rows.at[pl.ds(nonzeros + c * blocks, blocks)]
+        return pltpu.make_async_copy(a_hbm.at[pl.ds(c * blocks, blocks)], to, a_sem.at[c])
+
+    def start_chunk(c, _):
+        a_copy(c).start()
         return 0
 
-    def wait_row(i, _):
-        a_copy(i).wait()
-
-        @pl.when(i + AHEAD < rows)
+    def wait_chunk(c, _):
+        a_copy(c).wait()
+
+        @pl.when(c + AHEAD < chunks)
         def _():
-            a_copy(i + AHEAD).start()
+            a_copy(c + AHEAD).start()
 
         return 0
 
@@ -121,7 +127,7 @@
         at += source.shape[0]
     for copy in p_copies:
         copy.start()
-    lax.fori_loop(0, AHEAD, start_row, 0)
+    lax.fori_loop(0, AHEAD, start_chunk, 0)
 
     a_rows[0] = jnp.zeros((width, width), a_rows.dtype)
     if first:
@@ -189,8 +195,9 @@
 
     def rows_for(g, ready):
         v = list_ref[phase, (g + 1) * UNROLL - 1]
-        need = jnp.where(v > 0, v >> 5, rows)
-        lax.fori_loop(ready, need, wait_row, 0)
+        whole = divider(CHUNK, rows // CHUNK + 1)
+        need = jnp.where(v > 0, ((v >> 5) + CHUNK - 1) * whole >> 16, chunks)
+        lax.fori_loop(ready, need, wait_chunk, 0)
         return jnp.maximum(ready, need)
 
     def turn(carry):
@@ -217,7 +224,7 @@
     for u in range(UNROLL):
         i, k = entry(g, u)
         collect(i, k, second_product(u, i))
-    lax.fori_loop(ready, rows, wait_row, 0)
+    lax.fori_loop(ready, chunks, wait_chunk, 0)
     if last:
 
         def emit(rz, _):
@@ -243,7 +250,7 @@
     cfg = dict(cfg, sources=len(packed))
     quads = sum(x.shape[0] for x in packed)
     vmem = pl.BlockSpec(memory_space=pltpu.VMEM)
-    operands = [a_rows, *packed]
+    operands = [a_rows.reshape(rows * nonzeros, width, width), *packed]
     in_specs, out_specs = [HBM] * len(operands), [vmem] * 2
     shapes, stages, aliases = [
         pltpu.VMEM((slots, width, LANES), jnp.float32),
@@ -273,7 +280,7 @@
             ]
             + [pltpu.VMEM((width, per_row * LANES), jnp.bfloat16)] * UNROLL
             + [
-                pltpu.SemaphoreType.DMA((rows,)),
+                pltpu.SemaphoreType.DMA((rows // CHUNK,)),
                 pltpu.SemaphoreType.DMA((len(packed),)),
                 pltpu.SemaphoreType.DMA((2,)),
             ]
@@ -281,7 +288,7 @@
         ),
         out_shape=shapes,
         input_output_aliases=aliases,
-        compiler_params=pltpu.CompilerParams(vmem_limit_bytes=VMEM - resident - 1024 * 1024),
+        compiler_params=pltpu.CompilerParams(vmem_limit_bytes=VMEM - resident - 256 * 1024),
         cost_estimate=pl.CostEstimate(
             flops=4 * rows * nonzeros * width * width * width,
             bytes_accessed=20_000_000,
@@ -329,7 +336,8 @@
     phase_of = [p for p in range(phases) for _ in sources[p]]
 
     own = pack_prolong(prolong)
-    packed = [own] + [exchange(own, r) for r in range(1, members)]
+    direct = range(1, 3 if members == 4 else members)
+    packed = {0: own, **{r: [exchange(x, r) for x in own] for r in direct}}
     lists = make_lists(col_index[0], me, phase_of)
     cfg = dict(
         width=width, rows=rows, nonzeros=nonzeros, per_row=per_row, slots=slots,
@@ -339,9 +347,13 @@
     for p in range(phases):
         outs = work(
             {**cfg, "phase": p, "first": p == 0, "last": p == phases - 1, "from": sources[p][0]},
-            (lists, col_index[0], target[0]), a_blocks[0], [packed[r] for r in sources[p]], acc, pt,
+            (lists, col_index[0], target[0]), a_blocks[0], [x for r in sources[p] for x in packed[r]], acc, pt,
         )
         acc, pt = outs[-2:]
+        if p == 0 and members == 4:
+            near, acc = lax.optimization_barrier((packed[1] + packed[2], acc))
+            packed = {0: own, 1: near[:2], 2: near[2:]}
+            packed[3] = [exchange(near[0], 2), exchange(near[3], 1)]
 
     keep, give = outs[:2]
     total = keep + exchange(give, 1, "grp", groups).astype(f32)

time: 96.8 us -> 95.7 us (0.989)
  waiting for transfers between devices: 27.1 us -> 23.2 us
  starting transfers between devices: 14.5 us -> 16.9 us
    ppermute x10 -> x13, waiting for transfers between devices: 27.1 us -> 23.2 us  [exchange(): return lax.ppermute(x, axis, [(d, d ^ r) for d in range(size)])]
    ppermute x10 -> x13, starting transfers between devices: 14.5 us -> 16.9 us  [exchange(): return lax.ppermute(x, axis, [(d, d ^ r) for d in range(size)])]
  transfers between devices with their start and end apart: 10 -> 13, of which waited for: 8 -> 7; matrix products, arithmetic and copies ran while one was open for 2% -> 3% of each run, Pallas kernels for 34% -> 35%
where the time goes in v8:
time: 95.7 us; the launch traced here: 95.5 us
  Pallas kernels  49.3 us (52%)
  waiting for transfers between devices  23.2 us (24%)
  starting transfers between devices  16.9 us (18%)
  other arithmetic  5.5 us (6%)
    pallas_call x3, Pallas kernels, work(): pl.pallas_call(functools.partial(work_kernel, cfg), grid_spec=pltpu.Prefe...  47.1 us
    ppermute x13, waiting for transfers between devices, exchange(): return lax.ppermute(x, axis, [(d, d ^ r) for d in range(size)])  23.2 us
    ppermute x13, starting transfers between devices, exchange(): return lax.ppermute(x, axis, [(d, d ^ r) for d in range(size)])  16.9 us
    another operation x2, other arithmetic  2.3 us
    pallas_call x1, Pallas kernels, pack_prolong(): pl.pallas_call(pack_kernel, in_specs=[HBM], out_specs=[HBM] * 2, out_shap...  2.22 us
  transfers between devices with their start and end apart: 13, of which 7 were waited for; matrix products, arithmetic and copies ran while one was open for 3% of the time, Pallas kernels for 35%

profile of v8, /device:TPU:0, one launch (start us, length us, event | category | flops | bytes accessed | tf_op | source)
XLA Modules:
  0.0 95.5 jit_solution(12221835364458773133)
XLA Ops:
  0.0 2.2 %pack_prolong.1 = (bf16[6,3,96,128]{3,2,1,0:T(8,128)(2,1)}, bf16[6,3,96,128]{3,2,1,0:T(8,128)(2,1)}) custom-call(bf16[12,4,96,96]{3,2,1,0:T(8,128)(2,1)} %bitcast.54), custom_call_target="tpu_custom_call" | custom-call | tf_op jit(solution)/shard_map/pack_prolong/pallas_call | solution.py:61
  2.2 3.0 %collective-permute-start.2 = (bf16[6,3,96,128]{3,2,1,0:T(8,128)(2,1)}, bf16[6,3,96,128]{3,2,1,0:T(8,128)(2,1)}, u32[]{:S(2)}, u32[]{:S(2)}) collective-permute-start(bf16[6,3,96,128]{3,2,1,0:T(8,128)(2,1)} %get-tuple-element.18.refs_4_), channel_id=1, source_target_pairs={{0,16},{8,24},{16,0},{24,8},{1,17},{9,25},{17,1},{25,9},{2,18},{10... | collective-permute-start | bytes 1327112 | tf_op jit(solution)/shard_map/ppermute | solution.py:329
  5.3 1.5 %collective-permute-start = (bf16[6,3,96,128]{3,2,1,0:T(8,128)(2,1)}, bf16[6,3,96,128]{3,2,1,0:T(8,128)(2,1)}, u32[]{:S(2)}, u32[]{:S(2)}) collective-permute-start(bf16[6,3,96,128]{3,2,1,0:T(8,128)(2,1)} %get-tuple-element.18.refs_4_), channel_id=1, source_target_pairs={{0,8},{8,0},{16,24},{24,16},{1,9},{9,1},{17,25},{25,17},{2,10},{10... | collective-permute-start | bytes 1327112 | tf_op jit(solution)/shard_map/ppermute | solution.py:329
  6.8 0.5 collective-permute-start.3
  7.4 0.7 add_add_fusion
  8.5 1.3 %select_reduce_fusion.refs_0_ = s32[3,704]{1,0:T(4,128)} fusion(s32[648]{0:T(1024)S(1)} %get-tuple-element.44, s32[3,704]{1,0:T(4,128)S(1)} %multiply_add_fusion, s32[648]{0:T(1024)S(1)} %get-tuple-element.45), kind=kLoop, calls=%fused_computation | loop fusion | flops 4103616 | bytes 22080 | tf_op jit(solution)/shard_map/reduce_sum | solution.py:314
  9.8 18.7 %work_0.1 = (f32[128,96,128]{2,1,0:T(8,128)S(1)}, bf16[24,192,96]{2,1,0:T(8,128)(2,1)S(1)}) custom-call(s32[3,704]{1,0:T(4,128)} %select_reduce_fusion.refs_0_, s32[24,27]{1,0:T(8,128)} %bitcast.55, s32[24,108]{1,0:T(8,128)} %bitcast.58, bf16[648,96,96]{2,1,0:T(8,128)(2,1)} %bitcast.50, bf16[6,3,96,128]{3,2,1,0:T(8,128)(2,1)} %get-tuple-element.18.refs_4_, ...), custom_call_target="tpu_custom_call" | custom-call | flops 2293235712 | bytes 20000000 | tf_op jit(solution)/shard_map/work_0/pallas_call | solution.py:270
  28.6 2.0 %collective-permute-start.4 = (bf16[6,3,96,128]{3,2,1,0:T(8,128)(2,1)}, bf16[6,3,96,128]{3,2,1,0:T(8,128)(2,1)}, u32[]{:S(2)}, u32[]{:S(2)}) collective-permute-start(bf16[6,3,96,128]{3,2,1,0:T(8,128)(2,1)} %collective-permute-done.refs_4_), channel_id=1, source_target_pairs={{0,16},{8,24},{16,0},{24,8},{1,17},{9,25},{17,1},{25,9},{2,18},{10... | collective-permute-start | bytes 1327112 | tf_op jit(solution)/shard_map/ppermute | solution.py:329
  30.7 15.0 %work_1.1 = (f32[128,96,128]{2,1,0:T(8,128)S(1)}, bf16[24,192,96]{2,1,0:T(8,128)(2,1)S(1)}) custom-call(s32[3,704]{1,0:T(4,128)} %select_reduce_fusion.refs_0_, s32[24,27]{1,0:T(8,128)} %bitcast.56, s32[24,108]{1,0:T(8,128)} %bitcast.59, bf16[648,96,96]{2,1,0:T(8,128)(2,1)} %bitcast.51, ...), custom_call_target="tpu_custom_call", output_to_operand_aliasing={{1}: (9, {}), {0}: (8, {})} | custom-call | flops 2293235712 | bytes 20000000 | tf_op jit(solution)/shard_map/work_1/pallas_call | solution.py:270
  45.7 13.4 %work_2.1 = (f32[4,4,3,96,128]{4,3,2,1,0:T(8,128)}, bf16[4,4,3,96,128]{4,3,2,1,0:T(8,128)(2,1)}, f32[128,96,128]{2,1,0:T(8,128)S(1)}, bf16[24,192,96]{2,1,0:T(8,128)(2,1)S(1)}) custom-call(s32[3,704]{1,0:T(4,128)} %select_reduce_fusion.refs_0_, s32[24,27]{1,0:T(8,128)} %bitcast.57, ...), custom_call_target="tpu_custom_call", output_to_operand_aliasing={{3}: (7, {}), {2}: (6, {})} | custom-call | flops 2293235712 | bytes 20000000 | tf_op jit(solution)/shard_map/work_2/pallas_call | solution.py:270
  59.1 3.0 %collective-permute-done.6 = bf16[4,4,3,96,128]{4,3,2,1,0:T(8,128)(2,1)S(1)} collective-permute-done((bf16[4,4,3,96,128]{4,3,2,1,0:T(8,128)(2,1)}, bf16[4,4,3,96,128]{4,3,2,1,0:T(8,128)(2,1)S(1)}, u32[]{:S(2)}, u32[]{:S(2)}) %collective-permute-start.6) | collective-permute-done | bytes 1179680 | tf_op jit(solution)/shard_map/ppermute | solution.py:329
  62.2 2.1 %fusion.19 = (bf16[4,4,3,96,128]{4,3,2,1,0:T(8,128)(2,1)S(1)}, f32[4,4,3,96,128]{4,3,2,1,0:T(8,128)S(1)}) fusion(f32[4,4,3,96,128]{4,3,2,1,0:T(8,128)} %get-tuple-element.29, bf16[4,4,3,96,128]{4,3,2,1,0:T(8,128)(2,1)S(1)} %collective-permute-done.6), kind=kLoop, calls=%fused_computation.43 | loop fusion | flops 1769472 | bytes 7077888 | tf_op jit(solution)/shard_map/convert.5
  64.4 2.1 %collective-permute-start.7 = (bf16[4,3,96,128]{3,2,1,0:T(8,128)(2,1)S(1)}, bf16[4,3,96,128]{3,2,1,0:T(8,128)(2,1)S(1)}, u32[]{:S(2)}, u32[]{:S(2)}) collective-permute-start(bf16[4,3,96,128]{3,2,1,0:T(8,128)(2,1)S(1)} %get-tuple-element.35), channel_id=1, source_target_pairs={{0,8},{8,0},{16,24},{24,16},{1,9},{9,1},{17,25},{25,17},{2,10},{10... | collective-permute-start | bytes 884744 | tf_op jit(solution)/shard_map/ppermute | solution.py:329
  66.5 0.3 collective-permute-start.9
  66.8 1.2 %collective-permute-start.8 = (bf16[4,3,96,128]{3,2,1,0:T(8,128)(2,1)S(1)}, bf16[4,3,96,128]{3,2,1,0:T(8,128)(2,1)S(1)}, u32[]{:S(2)}, u32[]{:S(2)}) collective-permute-start(bf16[4,3,96,128]{3,2,1,0:T(8,128)(2,1)S(1)} %get-tuple-element.37), channel_id=1, source_target_pairs={{0,16},{8,24},{16,0},{24,8},{1,17},{9,25},{17,1},{25,9},{2,18},{10... | collective-permute-start | bytes 884744 | tf_op jit(solution)/shard_map/ppermute | solution.py:329
  68.0 6.3 %collective-permute-done.7 = bf16[4,3,96,128]{3,2,1,0:T(8,128)(2,1)S(1)} collective-permute-done((bf16[4,3,96,128]{3,2,1,0:T(8,128)(2,1)S(1)}, bf16[4,3,96,128]{3,2,1,0:T(8,128)(2,1)S(1)}, u32[]{:S(2)}, u32[]{:S(2)}) %collective-permute-start.7) | collective-permute-done | bytes 294944 | tf_op jit(solution)/shard_map/ppermute | solution.py:329
  74.3 6.2 %collective-permute-done.9 = bf16[4,3,96,128]{3,2,1,0:T(8,128)(2,1)S(1)} collective-permute-done((bf16[4,3,96,128]{3,2,1,0:T(8,128)(2,1)S(1)}, bf16[4,3,96,128]{3,2,1,0:T(8,128)(2,1)S(1)}, u32[]{:S(2)}, u32[]{:S(2)}) %collective-permute-start.9) | collective-permute-done | bytes 294944 | tf_op jit(solution)/shard_map/ppermute | solution.py:329
  80.5 1.4 %collective-permute-done.8 = bf16[4,3,96,128]{3,2,1,0:T(8,128)(2,1)S(1)} collective-permute-done((bf16[4,3,96,128]{3,2,1,0:T(8,128)(2,1)S(1)}, bf16[4,3,96,128]{3,2,1,0:T(8,128)(2,1)S(1)}, u32[]{:S(2)}, u32[]{:S(2)}) %collective-permute-start.8) | collective-permute-done | bytes 294944 | tf_op jit(solution)/shard_map/ppermute | solution.py:329
  82.1 4.0 %collective-permute-start.10 = (bf16[3,96,128]{2,1,0:T(8,128)(2,1)S(1)}, bf16[3,96,128]{2,1,0:T(8,128)(2,1)S(1)}, u32[]{:S(2)}, u32[]{:S(2)}) collective-permute-start(bf16[3,96,128]{2,1,0:T(8,128)(2,1)S(1)} %get-tuple-element.38), channel_id=1, source_target_pairs={{0,2},{1,3},{2,0},{3,1},{4,6},{5,7},{6,4},{7,5},{8,10},{9,11},{10,... | collective-permute-start | bytes 221192 | tf_op jit(solution)/shard_map/ppermute | solution.py:329
  86.1 1.9 %collective-permute-start.12 = (bf16[3,96,128]{2,1,0:T(8,128)(2,1)S(1)}, bf16[3,96,128]{2,1,0:T(8,128)(2,1)S(1)}, u32[]{:S(2)}, u32[]{:S(2)}) collective-permute-start(bf16[3,96,128]{2,1,0:T(8,128)(2,1)S(1)} %get-tuple-element.39), channel_id=1, source_target_pairs={{0,6},{1,7},{2,4},{3,5},{4,2},{5,3},{6,0},{7,1},{8,14},{9,15},{10,... | collective-permute-start | bytes 221192 | tf_op jit(solution)/shard_map/ppermute | solution.py:329
  88.1 1.1 %collective-permute-done.10 = bf16[3,96,128]{2,1,0:T(8,128)(2,1)S(1)} collective-permute-done((bf16[3,96,128]{2,1,0:T(8,128)(2,1)S(1)}, bf16[3,96,128]{2,1,0:T(8,128)(2,1)S(1)}, u32[]{:S(2)}, u32[]{:S(2)}) %collective-permute-start.10) | collective-permute-done | bytes 73760 | tf_op jit(solution)/shard_map/ppermute | solution.py:329
  89.2 3.0 %collective-permute-done.12 = bf16[3,96,128]{2,1,0:T(8,128)(2,1)S(1)} collective-permute-done((bf16[3,96,128]{2,1,0:T(8,128)(2,1)S(1)}, bf16[3,96,128]{2,1,0:T(8,128)(2,1)S(1)}, u32[]{:S(2)}, u32[]{:S(2)}) %collective-permute-start.12) | collective-permute-done | bytes 73760 | tf_op jit(solution)/shard_map/ppermute | solution.py:329
  92.2 2.2 %collective-permute-done.11 = bf16[3,96,128]{2,1,0:T(8,128)(2,1)S(1)} collective-permute-done((bf16[3,96,128]{2,1,0:T(8,128)(2,1)S(1)}, bf16[3,96,128]{2,1,0:T(8,128)(2,1)S(1)}, u32[]{:S(2)}, u32[]{:S(2)}) %collective-permute-start.11) | collective-permute-done | bytes 73760 | tf_op jit(solution)/shard_map/ppermute | solution.py:329
  94.8 0.7 maximum_bitcast_fusion
  (23 shorter events, 1.4 us)
Async XLA Ops:
  2.2 26.3 %collective-permute-start.2 = (bf16[6,3,96,128]{3,2,1,0:T(8,128)(2,1)}, bf16[6,3,96,128]{3,2,1,0:T(8,128)(2,1)}, u32[]{:S(2)}, u32[]{:S(2)}) collective-permute-start(bf16[6,3,96,128]{3,2,1,0:T(8,128)(2,1)} %get-tuple-element.18.refs_4_), channel_id=1, source_target_pairs={{0,16},{8,24},{16,0},{24,8},{1,17},{9,25},{17,1},{25,9},{2,18},{10... | collective-permute-start | bytes 1327112 | tf_op jit(solution)/shard_map/ppermute | solution.py:329
  5.3 23.3 %collective-permute-start = (bf16[6,3,96,128]{3,2,1,0:T(8,128)(2,1)}, bf16[6,3,96,128]{3,2,1,0:T(8,128)(2,1)}, u32[]{:S(2)}, u32[]{:S(2)}) collective-permute-start(bf16[6,3,96,128]{3,2,1,0:T(8,128)(2,1)} %get-tuple-element.18.refs_4_), channel_id=1, source_target_pairs={{0,8},{8,0},{16,24},{24,16},{1,9},{9,1},{17,25},{25,17},{2,10},{10... | collective-permute-start | bytes 1327112 | tf_op jit(solution)/shard_map/ppermute | solution.py:329
  6.8 21.8 %collective-permute-start.3 = (bf16[6,3,96,128]{3,2,1,0:T(8,128)(2,1)}, bf16[6,3,96,128]{3,2,1,0:T(8,128)(2,1)}, u32[]{:S(2)}, u32[]{:S(2)}) collective-permute-start(bf16[6,3,96,128]{3,2,1,0:T(8,128)(2,1)} %get-tuple-element.19.refs_5_), channel_id=1, source_target_pairs={{0,16},{8,24},{16,0},{24,8},{1,17},{9,25},{17,1},{25,9},{2,18},{10... | collective-permute-start | bytes 1327112 | tf_op jit(solution)/shard_map/ppermute | solution.py:329
  7.3 21.3 %collective-permute-start.1 = (bf16[6,3,96,128]{3,2,1,0:T(8,128)(2,1)}, bf16[6,3,96,128]{3,2,1,0:T(8,128)(2,1)}, u32[]{:S(2)}, u32[]{:S(2)}) collective-permute-start(bf16[6,3,96,128]{3,2,1,0:T(8,128)(2,1)} %get-tuple-element.19.refs_5_), channel_id=1, source_target_pairs={{0,8},{8,0},{16,24},{24,16},{1,9},{9,1},{17,25},{25,17},{2,10},{10... | collective-permute-start | bytes 1327112 | tf_op jit(solution)/shard_map/ppermute | solution.py:329
  28.6 17.0 %collective-permute-start.4 = (bf16[6,3,96,128]{3,2,1,0:T(8,128)(2,1)}, bf16[6,3,96,128]{3,2,1,0:T(8,128)(2,1)}, u32[]{:S(2)}, u32[]{:S(2)}) collective-permute-start(bf16[6,3,96,128]{3,2,1,0:T(8,128)(2,1)} %collective-permute-done.refs_4_), channel_id=1, source_target_pairs={{0,16},{8,24},{16,0},{24,8},{1,17},{9,25},{17,1},{25,9},{2,18},{10... | collective-permute-start | bytes 1327112 | tf_op jit(solution)/shard_map/ppermute | solution.py:329
  30.6 15.0 %collective-permute-start.5 = (bf16[6,3,96,128]{3,2,1,0:T(8,128)(2,1)}, bf16[6,3,96,128]{3,2,1,0:T(8,128)(2,1)}, u32[]{:S(2)}, u32[]{:S(2)}) collective-permute-start(bf16[6,3,96,128]{3,2,1,0:T(8,128)(2,1)} %collective-permute-done.3.refs_7_), channel_id=1, source_target_pairs={{0,8},{8,0},{16,24},{24,16},{1,9},{9,1},{17,25},{25,17},{2,10},{10... | collective-permute-start | bytes 1327112 | tf_op jit(solution)/shard_map/ppermute | solution.py:329
  59.1 3.1 %collective-permute-start.6 = (bf16[4,4,3,96,128]{4,3,2,1,0:T(8,128)(2,1)}, bf16[4,4,3,96,128]{4,3,2,1,0:T(8,128)(2,1)S(1)}, u32[]{:S(2)}, u32[]{:S(2)}) collective-permute-start(bf16[4,4,3,96,128]{4,3,2,1,0:T(8,128)(2,1)} %get-tuple-element.30), channel_id=1, source_target_pairs={{0,1},{1,0},{2,3},{3,2},{4,5},{5,4},{6,7},{7,6},{8,9},{9,8},{10,11... | collective-permute-start | bytes 3538952 | tf_op jit(solution)/shard_map/ppermute | solution.py:329
  64.4 9.9 %collective-permute-start.7 = (bf16[4,3,96,128]{3,2,1,0:T(8,128)(2,1)S(1)}, bf16[4,3,96,128]{3,2,1,0:T(8,128)(2,1)S(1)}, u32[]{:S(2)}, u32[]{:S(2)}) collective-permute-start(bf16[4,3,96,128]{3,2,1,0:T(8,128)(2,1)S(1)} %get-tuple-element.35), channel_id=1, source_target_pairs={{0,8},{8,0},{16,24},{24,16},{1,9},{9,1},{17,25},{25,17},{2,10},{10... | collective-permute-start | bytes 884744 | tf_op jit(solution)/shard_map/ppermute | solution.py:329
  66.5 14.0 %collective-permute-start.9 = (bf16[4,3,96,128]{3,2,1,0:T(8,128)(2,1)S(1)}, bf16[4,3,96,128]{3,2,1,0:T(8,128)(2,1)S(1)}, u32[]{:S(2)}, u32[]{:S(2)}) collective-permute-start(bf16[4,3,96,128]{3,2,1,0:T(8,128)(2,1)S(1)} %get-tuple-element.36), channel_id=1, source_target_pairs={{0,24},{8,16},{16,8},{24,0},{1,25},{9,17},{17,9},{25,1},{2,26},{10... | collective-permute-start | bytes 884744 | tf_op jit(solution)/shard_map/ppermute | solution.py:329
  66.8 15.1 %collective-permute-start.8 = (bf16[4,3,96,128]{3,2,1,0:T(8,128)(2,1)S(1)}, bf16[4,3,96,128]{3,2,1,0:T(8,128)(2,1)S(1)}, u32[]{:S(2)}, u32[]{:S(2)}) collective-permute-start(bf16[4,3,96,128]{3,2,1,0:T(8,128)(2,1)S(1)} %get-tuple-element.37), channel_id=1, source_target_pairs={{0,16},{8,24},{16,0},{24,8},{1,17},{9,25},{17,1},{25,9},{2,18},{10... | collective-permute-start | bytes 884744 | tf_op jit(solution)/shard_map/ppermute | solution.py:329
  82.1 7.1 %collective-permute-start.10 = (bf16[3,96,128]{2,1,0:T(8,128)(2,1)S(1)}, bf16[3,96,128]{2,1,0:T(8,128)(2,1)S(1)}, u32[]{:S(2)}, u32[]{:S(2)}) collective-permute-start(bf16[3,96,128]{2,1,0:T(8,128)(2,1)S(1)} %get-tuple-element.38), channel_id=1, source_target_pairs={{0,2},{1,3},{2,0},{3,1},{4,6},{5,7},{6,4},{7,5},{8,10},{9,11},{10,... | collective-permute-start | bytes 221192 | tf_op jit(solution)/shard_map/ppermute | solution.py:329
  86.1 6.2 %collective-permute-start.12 = (bf16[3,96,128]{2,1,0:T(8,128)(2,1)S(1)}, bf16[3,96,128]{2,1,0:T(8,128)(2,1)S(1)}, u32[]{:S(2)}, u32[]{:S(2)}) collective-permute-start(bf16[3,96,128]{2,1,0:T(8,128)(2,1)S(1)} %get-tuple-element.39), channel_id=1, source_target_pairs={{0,6},{1,7},{2,4},{3,5},{4,2},{5,3},{6,0},{7,1},{8,14},{9,15},{10,... | collective-permute-start | bytes 221192 | tf_op jit(solution)/shard_map/ppermute | solution.py:329
  88.0 6.4 %collective-permute-start.11 = (bf16[3,96,128]{2,1,0:T(8,128)(2,1)S(1)}, bf16[3,96,128]{2,1,0:T(8,128)(2,1)S(1)}, u32[]{:S(2)}, u32[]{:S(2)}) collective-permute-start(bf16[3,96,128]{2,1,0:T(8,128)(2,1)S(1)} %get-tuple-element.40), channel_id=1, source_target_pairs={{0,4},{1,5},{2,6},{3,7},{4,0},{5,1},{6,2},{7,3},{8,12},{9,13},{10,... | collective-permute-start | bytes 221192 | tf_op jit(solution)/shard_map/ppermute | solution.py:329

commit v9 on v8

--- a/solution.py
+++ b/solution.py
@@ -89,16 +89,14 @@
     list_ref, col_ref, tgt_ref, a_hbm = take(4)
     p_hbm = take(cfg["sources"])
     take(0 if first else 2)
-    out_refs = take(2 if last else 0)
+    give_out = take(1 if last else 0)
     acc, pt = take(2)
     p_vmem, a_rows = take(2)
     aps = take(UNROLL)
     a_sem, sem, out_sem = take(3)
-    stages = take(2 if last else 0)
+    stages = take(1 if last else 0)
 
     me = lax.axis_index("blk").astype(jnp.int32)
-    rank = lax.axis_index("grp").astype(jnp.int32)
-    chip, core = rank >> 1, rank & 1
 
     chunks = rows // CHUNK
 
@@ -226,21 +224,53 @@
         collect(i, k, second_product(u, i))
     lax.fori_loop(ready, chunks, wait_chunk, 0)
     if last:
+        (stage,), (out,) = stages, give_out
 
         def emit(rz, _):
-            for rc in range(2):
-                for r in range(members):
-                    s = ((chip ^ rz) * 2 + (core ^ rc)) * (OWN * members) + (me ^ r) * OWN
-                    packed = pack_four([acc[s + x] for x in range(OWN)], width)
-                    for t in range(3):
-                        stages[rc][rz, r, t] = packed[t].astype(stages[rc].dtype)
-                copy = pltpu.make_async_copy(stages[rc].at[rz], out_refs[rc].at[rz], out_sem.at[rc])
-                copy.start()
+            pack_part(cfg, acc, stage, rz, 1)
+            pltpu.make_async_copy(stage.at[rz], out.at[rz], out_sem.at[0]).start()
             return 0
 
         lax.fori_loop(0, groups // 2, emit, 0)
-        for rc in range(2):
-            pltpu.make_async_copy(stages[rc], out_refs[rc], out_sem.at[rc]).wait()
+        pltpu.make_async_copy(stage, out, out_sem.at[0]).wait()
+
+
+def pack_part(cfg, acc, to, rz, rc):
+    members = cfg["members"]
+    me = lax.axis_index("blk").astype(jnp.int32)
+    rank = lax.axis_index("grp").astype(jnp.int32)
+    group = ((rank >> 1) ^ rz) * 2 + ((rank & 1) ^ rc)
+    for r in range(members):
+        s = group * (OWN * members) + (me ^ r) * OWN
+        packed = pack_four([acc[s + x] for x in range(OWN)], cfg["width"])
+        for t in range(3):
+            to[rz, r, t] = packed[t].astype(to.dtype)
+
+
+def keep_kernel(cfg, _, keep_ref, acc):
+    def emit(rz, _):
+        pack_part(cfg, acc, keep_ref, rz, 0)
+        return 0
+
+    lax.fori_loop(0, cfg["groups"] // 2, emit, 0)
+
+
+def keep_part(cfg, acc):
+    vmem = pl.BlockSpec(memory_space=pltpu.VMEM)
+    keep, _ = pl.pallas_call(
+        functools.partial(keep_kernel, cfg),
+        in_specs=[vmem],
+        out_specs=[vmem] * 2,
+        out_shape=[
+            pltpu.VMEM((cfg["groups"] // 2, cfg["members"], 3, cfg["width"], LANES), jnp.float32),
+            pltpu.VMEM(acc.shape, acc.dtype),
+        ],
+        input_output_aliases={0: 1},
+        compiler_params=pltpu.CompilerParams(vmem_limit_bytes=8 * 1024 * 1024),
+        cost_estimate=pl.CostEstimate(flops=4_000_000, bytes_accessed=4_000_000, transcendentals=0),
+        name="keep_part",
+    )(acc)
+    return keep
 
 
 def work(cfg, tables, a_rows, packed, acc=None, pt=None):
@@ -262,9 +292,8 @@
         in_specs += [vmem] * 2
     if last:
         whole = (groups // 2, members, 3, width, LANES)
-        made = [jax.ShapeDtypeStruct(whole, jnp.float32), jax.ShapeDtypeStruct(whole, jnp.bfloat16)]
-        stages = [pltpu.VMEM(x.shape, x.dtype) for x in made]
-        shapes, out_specs = made + shapes, [HBM] * 2 + out_specs
+        stages = [pltpu.VMEM(whole, jnp.bfloat16)]
+        shapes, out_specs = [jax.ShapeDtypeStruct(whole, jnp.bfloat16)] + shapes, [HBM] + out_specs
     if not first:
         aliases = {len(tables) + len(operands) - x: len(shapes) - x for x in (1, 2)}
     return pl.pallas_call(
@@ -282,7 +311,7 @@
             + [
                 pltpu.SemaphoreType.DMA((rows // CHUNK,)),
                 pltpu.SemaphoreType.DMA((len(packed),)),
-                pltpu.SemaphoreType.DMA((2,)),
+                pltpu.SemaphoreType.DMA((1,)),
             ]
             + stages,
         ),
@@ -355,8 +384,8 @@
             packed = {0: own, 1: near[:2], 2: near[2:]}
             packed[3] = [exchange(near[0], 2), exchange(near[3], 1)]
 
-    keep, give = outs[:2]
-    total = keep + exchange(give, 1, "grp", groups).astype(f32)
+    given = exchange(outs[0], 1, "grp", groups)
+    total = keep_part(cfg, acc) + given.astype(f32)
     got = [exchange(total[:, r].astype(bf16), r) for r in range(1, members)]
     total = total[:, 0]
     for part in got:

time: 95.7 us -> 92.9 us (0.971)
  other arithmetic: 5.5 us -> 3.84 us
  starting transfers between devices: 16.9 us -> 15.9 us
    another operation x2, other arithmetic: 2.3 us -> 0.64 us
    pallas_call x3, Pallas kernels: 47.1 us -> 45.7 us  [work(): pl.pallas_call(functools.partial(work_kernel, cfg), grid_spec=pltpu.Prefe...]
    ppermute x13, starting transfers between devices: 16.9 us -> 15.9 us  [exchange(): return lax.ppermute(x, axis, [(d, d ^ r) for d in range(size)])]
  transfers between devices with their start and end apart: 13 -> 13, of which waited for: 7 -> 7; matrix products, arithmetic and copies ran while one was open for 3% -> 3% of each run, Pallas kernels for 35% -> 37%
where the time goes in v9:
time: 92.9 us; the launch traced here: 91.8 us
  Pallas kernels  48.8 us (53%)
  waiting for transfers between devices  22.8 us (25%)
  starting transfers between devices  15.9 us (17%)
  other arithmetic  3.84 us (4%)
    pallas_call x3, Pallas kernels, work(): pl.pallas_call(functools.partial(work_kernel, cfg), grid_spec=pltpu.Prefe...  45.7 us
    ppermute x13, waiting for transfers between devices, exchange(): return lax.ppermute(x, axis, [(d, d ^ r) for d in range(size)])  22.8 us
    ppermute x13, starting transfers between devices, exchange(): return lax.ppermute(x, axis, [(d, d ^ r) for d in range(size)])  15.9 us
    pallas_call x1, Pallas kernels, pack_prolong(): pl.pallas_call(pack_kernel, in_specs=[HBM], out_specs=[HBM] * 2, out_shap...  2.22 us
  transfers between devices with their start and end apart: 13, of which 7 were waited for; matrix products, arithmetic and copies ran while one was open for 3% of the time, Pallas kernels for 37%

profile of v9, /device:TPU:0, one launch (start us, length us, event | category | flops | bytes accessed | tf_op | source)
XLA Modules:
  0.0 91.8 jit_solution(16915900156169522749)
XLA Ops:
  0.0 2.2 %pack_prolong.1 = (bf16[6,3,96,128]{3,2,1,0:T(8,128)(2,1)}, bf16[6,3,96,128]{3,2,1,0:T(8,128)(2,1)}) custom-call(bf16[12,4,96,96]{3,2,1,0:T(8,128)(2,1)} %bitcast.54), custom_call_target="tpu_custom_call" | custom-call | tf_op jit(solution)/shard_map/pack_prolong/pallas_call | solution.py:61
  2.2 3.0 %collective-permute-start.2 = (bf16[6,3,96,128]{3,2,1,0:T(8,128)(2,1)}, bf16[6,3,96,128]{3,2,1,0:T(8,128)(2,1)}, u32[]{:S(2)}, u32[]{:S(2)}) collective-permute-start(bf16[6,3,96,128]{3,2,1,0:T(8,128)(2,1)} %get-tuple-element.19.refs_4_), channel_id=1, source_target_pairs={{0,16},{8,24},{16,0},{24,8},{1,17},{9,25},{17,1},{25,9},{2,18},{10... | collective-permute-start | bytes 1327112 | tf_op jit(solution)/shard_map/ppermute | solution.py:358
  5.3 1.5 %collective-permute-start = (bf16[6,3,96,128]{3,2,1,0:T(8,128)(2,1)}, bf16[6,3,96,128]{3,2,1,0:T(8,128)(2,1)}, u32[]{:S(2)}, u32[]{:S(2)}) collective-permute-start(bf16[6,3,96,128]{3,2,1,0:T(8,128)(2,1)} %get-tuple-element.19.refs_4_), channel_id=1, source_target_pairs={{0,8},{8,0},{16,24},{24,16},{1,9},{9,1},{17,25},{25,17},{2,10},{10... | collective-permute-start | bytes 1327112 | tf_op jit(solution)/shard_map/ppermute | solution.py:358
  6.8 0.5 collective-permute-start.3
  7.4 0.7 add_add_fusion
  8.5 1.3 %select_reduce_fusion.refs_0_ = s32[3,704]{1,0:T(4,128)} fusion(s32[648]{0:T(1024)S(1)} %get-tuple-element.46, s32[3,704]{1,0:T(4,128)S(1)} %multiply_add_fusion, s32[648]{0:T(1024)S(1)} %get-tuple-element.47), kind=kLoop, calls=%fused_computation | loop fusion | flops 4103616 | bytes 22080 | tf_op jit(solution)/shard_map/reduce_sum | solution.py:343
  9.8 18.7 %work_0.1 = (f32[128,96,128]{2,1,0:T(8,128)S(1)}, bf16[24,192,96]{2,1,0:T(8,128)(2,1)S(1)}) custom-call(s32[3,704]{1,0:T(4,128)} %select_reduce_fusion.refs_0_, s32[24,27]{1,0:T(8,128)} %bitcast.55, s32[24,108]{1,0:T(8,128)} %bitcast.58, bf16[648,96,96]{2,1,0:T(8,128)(2,1)} %bitcast.50, bf16[6,3,96,128]{3,2,1,0:T(8,128)(2,1)} %get-tuple-element.19.refs_4_, ...), custom_call_target="tpu_custom_call" | custom-call | flops 2293235712 | bytes 20000000 | tf_op jit(solution)/shard_map/work_0/pallas_call | solution.py:299
  28.6 2.0 %collective-permute-start.4 = (bf16[6,3,96,128]{3,2,1,0:T(8,128)(2,1)}, bf16[6,3,96,128]{3,2,1,0:T(8,128)(2,1)}, u32[]{:S(2)}, u32[]{:S(2)}) collective-permute-start(bf16[6,3,96,128]{3,2,1,0:T(8,128)(2,1)} %collective-permute-done.refs_4_), channel_id=1, source_target_pairs={{0,16},{8,24},{16,0},{24,8},{1,17},{9,25},{17,1},{25,9},{2,18},{10... | collective-permute-start | bytes 1327112 | tf_op jit(solution)/shard_map/ppermute | solution.py:358
  30.7 14.3 %work_1.1 = (f32[128,96,128]{2,1,0:T(8,128)S(1)}, bf16[24,192,96]{2,1,0:T(8,128)(2,1)S(1)}) custom-call(s32[3,704]{1,0:T(4,128)} %select_reduce_fusion.refs_0_, s32[24,27]{1,0:T(8,128)} %bitcast.56, s32[24,108]{1,0:T(8,128)} %bitcast.59, bf16[648,96,96]{2,1,0:T(8,128)(2,1)} %bitcast.51, ...), custom_call_target="tpu_custom_call", output_to_operand_aliasing={{1}: (9, {}), {0}: (8, {})} | custom-call | flops 2293235712 | bytes 20000000 | tf_op jit(solution)/shard_map/work_1/pallas_call | solution.py:299
  45.0 12.6 %work_2.1 = (bf16[4,4,3,96,128]{4,3,2,1,0:T(8,128)(2,1)}, f32[128,96,128]{2,1,0:T(8,128)S(1)}, bf16[24,192,96]{2,1,0:T(8,128)(2,1)S(1)}) custom-call(s32[3,704]{1,0:T(4,128)} %select_reduce_fusion.refs_0_, s32[24,27]{1,0:T(8,128)} %bitcast.57, s32[24,108]{1,0:T(8,128)} %bitcast.60, ...), custom_call_target="tpu_custom_call", output_to_operand_aliasing={{2}: (7, {}), {1}: (6, {})} | custom-call | flops 2293235712 | bytes 20000000 | tf_op jit(solution)/shard_map/work_2/pallas_call | solution.py:299
  57.6 0.6 collective-permute-start.6
  58.3 0.9 keep_part.1
  59.2 1.8 %collective-permute-done.6 = bf16[4,4,3,96,128]{4,3,2,1,0:T(8,128)(2,1)S(1)} collective-permute-done((bf16[4,4,3,96,128]{4,3,2,1,0:T(8,128)(2,1)}, bf16[4,4,3,96,128]{4,3,2,1,0:T(8,128)(2,1)S(1)}, u32[]{:S(2)}, u32[]{:S(2)}) %collective-permute-start.6) | collective-permute-done | bytes 1179680 | tf_op jit(solution)/shard_map/ppermute | solution.py:358
  61.6 2.4 %collective-permute-start.7 = (bf16[4,3,96,128]{3,2,1,0:T(8,128)(2,1)S(1)}, bf16[4,3,96,128]{3,2,1,0:T(8,128)(2,1)S(1)}, u32[]{:S(2)}, u32[]{:S(2)}) collective-permute-start(bf16[4,3,96,128]{3,2,1,0:T(8,128)(2,1)S(1)} %get-tuple-element.37), channel_id=1, source_target_pairs={{0,8},{8,0},{16,24},{24,16},{1,9},{9,1},{17,25},{25,17},{2,10},{10... | collective-permute-start | bytes 884744 | tf_op jit(solution)/shard_map/ppermute | solution.py:358
  64.0 1.5 %collective-permute-start.9 = (bf16[4,3,96,128]{3,2,1,0:T(8,128)(2,1)S(1)}, bf16[4,3,96,128]{3,2,1,0:T(8,128)(2,1)S(1)}, u32[]{:S(2)}, u32[]{:S(2)}) collective-permute-start(bf16[4,3,96,128]{3,2,1,0:T(8,128)(2,1)S(1)} %get-tuple-element.38), channel_id=1, source_target_pairs={{0,24},{8,16},{16,8},{24,0},{1,25},{9,17},{17,9},{25,1},{2,26},{10... | collective-permute-start | bytes 884744 | tf_op jit(solution)/shard_map/ppermute | solution.py:358
  65.5 6.3 %collective-permute-done.7 = bf16[4,3,96,128]{3,2,1,0:T(8,128)(2,1)S(1)} collective-permute-done((bf16[4,3,96,128]{3,2,1,0:T(8,128)(2,1)S(1)}, bf16[4,3,96,128]{3,2,1,0:T(8,128)(2,1)S(1)}, u32[]{:S(2)}, u32[]{:S(2)}) %collective-permute-start.7) | collective-permute-done | bytes 294944 | tf_op jit(solution)/shard_map/ppermute | solution.py:358
  71.8 7.1 %collective-permute-done.9 = bf16[4,3,96,128]{3,2,1,0:T(8,128)(2,1)S(1)} collective-permute-done((bf16[4,3,96,128]{3,2,1,0:T(8,128)(2,1)S(1)}, bf16[4,3,96,128]{3,2,1,0:T(8,128)(2,1)S(1)}, u32[]{:S(2)}, u32[]{:S(2)}) %collective-permute-start.9) | collective-permute-done | bytes 294944 | tf_op jit(solution)/shard_map/ppermute | solution.py:358
  78.9 1.4 %collective-permute-done.8 = bf16[4,3,96,128]{3,2,1,0:T(8,128)(2,1)S(1)} collective-permute-done((bf16[4,3,96,128]{3,2,1,0:T(8,128)(2,1)S(1)}, bf16[4,3,96,128]{3,2,1,0:T(8,128)(2,1)S(1)}, u32[]{:S(2)}, u32[]{:S(2)}) %collective-permute-start.8) | collective-permute-done | bytes 294944 | tf_op jit(solution)/shard_map/ppermute | solution.py:358
  80.4 2.5 %collective-permute-start.10 = (bf16[3,96,128]{2,1,0:T(8,128)(2,1)S(1)}, bf16[3,96,128]{2,1,0:T(8,128)(2,1)S(1)}, u32[]{:S(2)}, u32[]{:S(2)}) collective-permute-start(bf16[3,96,128]{2,1,0:T(8,128)(2,1)S(1)} %get-tuple-element.40), channel_id=1, source_target_pairs={{0,2},{1,3},{2,0},{3,1},{4,6},{5,7},{6,4},{7,5},{8,10},{9,11},{10,... | collective-permute-start | bytes 221192 | tf_op jit(solution)/shard_map/ppermute | solution.py:358
  82.9 1.3 %collective-permute-start.12 = (bf16[3,96,128]{2,1,0:T(8,128)(2,1)S(1)}, bf16[3,96,128]{2,1,0:T(8,128)(2,1)S(1)}, u32[]{:S(2)}, u32[]{:S(2)}) collective-permute-start(bf16[3,96,128]{2,1,0:T(8,128)(2,1)S(1)} %get-tuple-element.41), channel_id=1, source_target_pairs={{0,6},{1,7},{2,4},{3,5},{4,2},{5,3},{6,0},{7,1},{8,14},{9,15},{10,... | collective-permute-start | bytes 221192 | tf_op jit(solution)/shard_map/ppermute | solution.py:358
  84.5 1.6 %collective-permute-done.10 = bf16[3,96,128]{2,1,0:T(8,128)(2,1)S(1)} collective-permute-done((bf16[3,96,128]{2,1,0:T(8,128)(2,1)S(1)}, bf16[3,96,128]{2,1,0:T(8,128)(2,1)S(1)}, u32[]{:S(2)}, u32[]{:S(2)}) %collective-permute-start.10) | collective-permute-done | bytes 73760 | tf_op jit(solution)/shard_map/ppermute | solution.py:358
  86.0 3.1 %collective-permute-done.12 = bf16[3,96,128]{2,1,0:T(8,128)(2,1)S(1)} collective-permute-done((bf16[3,96,128]{2,1,0:T(8,128)(2,1)S(1)}, bf16[3,96,128]{2,1,0:T(8,128)(2,1)S(1)}, u32[]{:S(2)}, u32[]{:S(2)}) %collective-permute-start.12) | collective-permute-done | bytes 73760 | tf_op jit(solution)/shard_map/ppermute | solution.py:358
  89.2 1.6 %collective-permute-done.11 = bf16[3,96,128]{2,1,0:T(8,128)(2,1)S(1)} collective-permute-done((bf16[3,96,128]{2,1,0:T(8,128)(2,1)S(1)}, bf16[3,96,128]{2,1,0:T(8,128)(2,1)S(1)}, u32[]{:S(2)}, u32[]{:S(2)}) %collective-permute-start.11) | collective-permute-done | bytes 73760 | tf_op jit(solution)/shard_map/ppermute | solution.py:358
  91.1 0.7 maximum_bitcast_fusion
  (24 shorter events, 2.1 us)
Async XLA Ops:
  2.2 26.3 %collective-permute-start.2 = (bf16[6,3,96,128]{3,2,1,0:T(8,128)(2,1)}, bf16[6,3,96,128]{3,2,1,0:T(8,128)(2,1)}, u32[]{:S(2)}, u32[]{:S(2)}) collective-permute-start(bf16[6,3,96,128]{3,2,1,0:T(8,128)(2,1)} %get-tuple-element.19.refs_4_), channel_id=1, source_target_pairs={{0,16},{8,24},{16,0},{24,8},{1,17},{9,25},{17,1},{25,9},{2,18},{10... | collective-permute-start | bytes 1327112 | tf_op jit(solution)/shard_map/ppermute | solution.py:358
  5.3 23.3 %collective-permute-start = (bf16[6,3,96,128]{3,2,1,0:T(8,128)(2,1)}, bf16[6,3,96,128]{3,2,1,0:T(8,128)(2,1)}, u32[]{:S(2)}, u32[]{:S(2)}) collective-permute-start(bf16[6,3,96,128]{3,2,1,0:T(8,128)(2,1)} %get-tuple-element.19.refs_4_), channel_id=1, source_target_pairs={{0,8},{8,0},{16,24},{24,16},{1,9},{9,1},{17,25},{25,17},{2,10},{10... | collective-permute-start | bytes 1327112 | tf_op jit(solution)/shard_map/ppermute | solution.py:358
  6.8 21.8 %collective-permute-start.3 = (bf16[6,3,96,128]{3,2,1,0:T(8,128)(2,1)}, bf16[6,3,96,128]{3,2,1,0:T(8,128)(2,1)}, u32[]{:S(2)}, u32[]{:S(2)}) collective-permute-start(bf16[6,3,96,128]{3,2,1,0:T(8,128)(2,1)} %get-tuple-element.20.refs_5_), channel_id=1, source_target_pairs={{0,16},{8,24},{16,0},{24,8},{1,17},{9,25},{17,1},{25,9},{2,18},{10... | collective-permute-start | bytes 1327112 | tf_op jit(solution)/shard_map/ppermute | solution.py:358
  7.3 21.3 %collective-permute-start.1 = (bf16[6,3,96,128]{3,2,1,0:T(8,128)(2,1)}, bf16[6,3,96,128]{3,2,1,0:T(8,128)(2,1)}, u32[]{:S(2)}, u32[]{:S(2)}) collective-permute-start(bf16[6,3,96,128]{3,2,1,0:T(8,128)(2,1)} %get-tuple-element.20.refs_5_), channel_id=1, source_target_pairs={{0,8},{8,0},{16,24},{24,16},{1,9},{9,1},{17,25},{25,17},{2,10},{10... | collective-permute-start | bytes 1327112 | tf_op jit(solution)/shard_map/ppermute | solution.py:358
  28.6 16.4 %collective-permute-start.4 = (bf16[6,3,96,128]{3,2,1,0:T(8,128)(2,1)}, bf16[6,3,96,128]{3,2,1,0:T(8,128)(2,1)}, u32[]{:S(2)}, u32[]{:S(2)}) collective-permute-start(bf16[6,3,96,128]{3,2,1,0:T(8,128)(2,1)} %collective-permute-done.refs_4_), channel_id=1, source_target_pairs={{0,16},{8,24},{16,0},{24,8},{1,17},{9,25},{17,1},{25,9},{2,18},{10... | collective-permute-start | bytes 1327112 | tf_op jit(solution)/shard_map/ppermute | solution.py:358
  30.6 14.4 %collective-permute-start.5 = (bf16[6,3,96,128]{3,2,1,0:T(8,128)(2,1)}, bf16[6,3,96,128]{3,2,1,0:T(8,128)(2,1)}, u32[]{:S(2)}, u32[]{:S(2)}) collective-permute-start(bf16[6,3,96,128]{3,2,1,0:T(8,128)(2,1)} %collective-permute-done.3.refs_7_), channel_id=1, source_target_pairs={{0,8},{8,0},{16,24},{24,16},{1,9},{9,1},{17,25},{25,17},{2,10},{10... | collective-permute-start | bytes 1327112 | tf_op jit(solution)/shard_map/ppermute | solution.py:358
  57.6 3.3 %collective-permute-start.6 = (bf16[4,4,3,96,128]{4,3,2,1,0:T(8,128)(2,1)}, bf16[4,4,3,96,128]{4,3,2,1,0:T(8,128)(2,1)S(1)}, u32[]{:S(2)}, u32[]{:S(2)}) collective-permute-start(bf16[4,4,3,96,128]{4,3,2,1,0:T(8,128)(2,1)} %get-tuple-element.32), channel_id=1, source_target_pairs={{0,1},{1,0},{2,3},{3,2},{4,5},{5,4},{6,7},{7,6},{8,9},{9,8},{10,11... | collective-permute-start | bytes 3538952 | tf_op jit(solution)/shard_map/ppermute | solution.py:358
  61.6 10.3 %collective-permute-start.7 = (bf16[4,3,96,128]{3,2,1,0:T(8,128)(2,1)S(1)}, bf16[4,3,96,128]{3,2,1,0:T(8,128)(2,1)S(1)}, u32[]{:S(2)}, u32[]{:S(2)}) collective-permute-start(bf16[4,3,96,128]{3,2,1,0:T(8,128)(2,1)S(1)} %get-tuple-element.37), channel_id=1, source_target_pairs={{0,8},{8,0},{16,24},{24,16},{1,9},{9,1},{17,25},{25,17},{2,10},{10... | collective-permute-start | bytes 884744 | tf_op jit(solution)/shard_map/ppermute | solution.py:358
  64.0 14.9 %collective-permute-start.9 = (bf16[4,3,96,128]{3,2,1,0:T(8,128)(2,1)S(1)}, bf16[4,3,96,128]{3,2,1,0:T(8,128)(2,1)S(1)}, u32[]{:S(2)}, u32[]{:S(2)}) collective-permute-start(bf16[4,3,96,128]{3,2,1,0:T(8,128)(2,1)S(1)} %get-tuple-element.38), channel_id=1, source_target_pairs={{0,24},{8,16},{16,8},{24,0},{1,25},{9,17},{17,9},{25,1},{2,26},{10... | collective-permute-start | bytes 884744 | tf_op jit(solution)/shard_map/ppermute | solution.py:358
  65.4 14.8 %collective-permute-start.8 = (bf16[4,3,96,128]{3,2,1,0:T(8,128)(2,1)S(1)}, bf16[4,3,96,128]{3,2,1,0:T(8,128)(2,1)S(1)}, u32[]{:S(2)}, u32[]{:S(2)}) collective-permute-start(bf16[4,3,96,128]{3,2,1,0:T(8,128)(2,1)S(1)} %get-tuple-element.39), channel_id=1, source_target_pairs={{0,16},{8,24},{16,0},{24,8},{1,17},{9,25},{17,1},{25,9},{2,18},{10... | collective-permute-start | bytes 884744 | tf_op jit(solution)/shard_map/ppermute | solution.py:358
  80.4 5.6 %collective-permute-start.10 = (bf16[3,96,128]{2,1,0:T(8,128)(2,1)S(1)}, bf16[3,96,128]{2,1,0:T(8,128)(2,1)S(1)}, u32[]{:S(2)}, u32[]{:S(2)}) collective-permute-start(bf16[3,96,128]{2,1,0:T(8,128)(2,1)S(1)} %get-tuple-element.40), channel_id=1, source_target_pairs={{0,2},{1,3},{2,0},{3,1},{4,6},{5,7},{6,4},{7,5},{8,10},{9,11},{10,... | collective-permute-start | bytes 221192 | tf_op jit(solution)/shard_map/ppermute | solution.py:358
  82.9 6.3 %collective-permute-start.12 = (bf16[3,96,128]{2,1,0:T(8,128)(2,1)S(1)}, bf16[3,96,128]{2,1,0:T(8,128)(2,1)S(1)}, u32[]{:S(2)}, u32[]{:S(2)}) collective-permute-start(bf16[3,96,128]{2,1,0:T(8,128)(2,1)S(1)} %get-tuple-element.41), channel_id=1, source_target_pairs={{0,6},{1,7},{2,4},{3,5},{4,2},{5,3},{6,0},{7,1},{8,14},{9,15},{10,... | collective-permute-start | bytes 221192 | tf_op jit(solution)/shard_map/ppermute | solution.py:358
  84.2 6.5 %collective-permute-start.11 = (bf16[3,96,128]{2,1,0:T(8,128)(2,1)S(1)}, bf16[3,96,128]{2,1,0:T(8,128)(2,1)S(1)}, u32[]{:S(2)}, u32[]{:S(2)}) collective-permute-start(bf16[3,96,128]{2,1,0:T(8,128)(2,1)S(1)} %get-tuple-element.42), channel_id=1, source_target_pairs={{0,4},{1,5},{2,6},{3,7},{4,0},{5,1},{6,2},{7,3},{8,12},{9,13},{10,... | collective-permute-start | bytes 221192 | tf_op jit(solution)/shard_map/ppermute | solution.py:358

commit v10 on v9

--- a/solution.py
+++ b/solution.py
@@ -8,10 +8,10 @@
 from jax.sharding import PartitionSpec as P
 
 OWN = 4
-UNROLL = 32
+UNROLL = 24
 LANES = 128
-CHUNK = 3
-AHEAD = 4
+CHUNK = 2
+AHEAD = 6
 VMEM = 64 * 1024 * 1024
 HBM = pl.BlockSpec(memory_space=pl.ANY)
 

time: 92.9 us -> 93.7 us (level); the launches traced: 91.8 us -> 94 us
  starting transfers between devices: 15.9 us -> 18.6 us
  waiting for transfers between devices: 22.8 us -> 21.5 us
    ppermute x13, starting transfers between devices: 15.9 us -> 18.6 us  [exchange(): return lax.ppermute(x, axis, [(d, d ^ r) for d in range(size)])]
    ppermute x13, waiting for transfers between devices: 22.8 us -> 21.5 us  [exchange(): return lax.ppermute(x, axis, [(d, d ^ r) for d in range(size)])]
  transfers between devices with their start and end apart: 13 -> 13, of which waited for: 7 -> 6; matrix products, arithmetic and copies ran while one was open for 3% -> 3% of each run, Pallas kernels for 37% -> 36%
where the time goes in v10:
time: 93.7 us; the launch traced here: 94 us
  Pallas kernels  49.5 us (53%)
  waiting for transfers between devices  21.5 us (23%)
  starting transfers between devices  18.6 us (20%)
  other arithmetic  3.84 us (4%)
    pallas_call x3, Pallas kernels, work(): pl.pallas_call(functools.partial(work_kernel, cfg), grid_spec=pltpu.Prefe...  46.4 us
    ppermute x13, waiting for transfers between devices, exchange(): return lax.ppermute(x, axis, [(d, d ^ r) for d in range(size)])  21.5 us
    ppermute x13, starting transfers between devices, exchange(): return lax.ppermute(x, axis, [(d, d ^ r) for d in range(size)])  18.6 us
    pallas_call x1, Pallas kernels, pack_prolong(): pl.pallas_call(pack_kernel, in_specs=[HBM], out_specs=[HBM] * 2, out_shap...  2.22 us
  transfers between devices with their start and end apart: 13, of which 6 were waited for; matrix products, arithmetic and copies ran while one was open for 3% of the time, Pallas kernels for 36%

profile of v10, /device:TPU:0, one launch (start us, length us, event | category | flops | bytes accessed | tf_op | source)
XLA Modules:
  0.0 94.0 jit_solution(13080883527472250332)
XLA Ops:
  0.0 2.2 %pack_prolong.1 = (bf16[6,3,96,128]{3,2,1,0:T(8,128)(2,1)}, bf16[6,3,96,128]{3,2,1,0:T(8,128)(2,1)}) custom-call(bf16[12,4,96,96]{3,2,1,0:T(8,128)(2,1)} %bitcast.54), custom_call_target="tpu_custom_call" | custom-call | tf_op jit(solution)/shard_map/pack_prolong/pallas_call | solution.py:61
  2.2 3.0 %collective-permute-start.2 = (bf16[6,3,96,128]{3,2,1,0:T(8,128)(2,1)}, bf16[6,3,96,128]{3,2,1,0:T(8,128)(2,1)}, u32[]{:S(2)}, u32[]{:S(2)}) collective-permute-start(bf16[6,3,96,128]{3,2,1,0:T(8,128)(2,1)} %get-tuple-element.19.refs_4_), channel_id=1, source_target_pairs={{0,16},{8,24},{16,0},{24,8},{1,17},{9,25},{17,1},{25,9},{2,18},{10... | collective-permute-start | bytes 1327112 | tf_op jit(solution)/shard_map/ppermute | solution.py:358
  5.3 1.5 %collective-permute-start = (bf16[6,3,96,128]{3,2,1,0:T(8,128)(2,1)}, bf16[6,3,96,128]{3,2,1,0:T(8,128)(2,1)}, u32[]{:S(2)}, u32[]{:S(2)}) collective-permute-start(bf16[6,3,96,128]{3,2,1,0:T(8,128)(2,1)} %get-tuple-element.19.refs_4_), channel_id=1, source_target_pairs={{0,8},{8,0},{16,24},{24,16},{1,9},{9,1},{17,25},{25,17},{2,10},{10... | collective-permute-start | bytes 1327112 | tf_op jit(solution)/shard_map/ppermute | solution.py:358
  6.8 0.5 collective-permute-start.3
  7.4 0.7 add_add_fusion
  8.5 1.3 %select_reduce_fusion.refs_0_ = s32[3,672]{1,0:T(4,128)} fusion(s32[648]{0:T(1024)S(1)} %get-tuple-element.46, s32[3,672]{1,0:T(4,128)S(1)} %multiply_add_fusion, s32[648]{0:T(1024)S(1)} %get-tuple-element.47), kind=kLoop, calls=%fused_computation | loop fusion | flops 3917088 | bytes 21312 | tf_op jit(solution)/shard_map/reduce_sum | solution.py:343
  9.8 17.7 %work_0.1 = (f32[128,96,128]{2,1,0:T(8,128)S(1)}, bf16[24,192,96]{2,1,0:T(8,128)(2,1)S(1)}) custom-call(s32[3,672]{1,0:T(4,128)} %select_reduce_fusion.refs_0_, s32[24,27]{1,0:T(8,128)} %bitcast.55, s32[24,108]{1,0:T(8,128)} %bitcast.58, bf16[648,96,96]{2,1,0:T(8,128)(2,1)} %bitcast.50, bf16[6,3,96,128]{3,2,1,0:T(8,128)(2,1)} %get-tuple-element.19.refs_4_, ...), custom_call_target="tpu_custom_call" | custom-call | flops 2293235712 | bytes 20000000 | tf_op jit(solution)/shard_map/work_0/pallas_call | solution.py:299
  27.6 2.0 %collective-permute-start.4 = (bf16[6,3,96,128]{3,2,1,0:T(8,128)(2,1)}, bf16[6,3,96,128]{3,2,1,0:T(8,128)(2,1)}, u32[]{:S(2)}, u32[]{:S(2)}) collective-permute-start(bf16[6,3,96,128]{3,2,1,0:T(8,128)(2,1)} %collective-permute-done.refs_4_), channel_id=1, source_target_pairs={{0,16},{8,24},{16,0},{24,8},{1,17},{9,25},{17,1},{25,9},{2,18},{10... | collective-permute-start | bytes 1327112 | tf_op jit(solution)/shard_map/ppermute | solution.py:358
  29.6 1.5 %collective-permute-start.5 = (bf16[6,3,96,128]{3,2,1,0:T(8,128)(2,1)}, bf16[6,3,96,128]{3,2,1,0:T(8,128)(2,1)}, u32[]{:S(2)}, u32[]{:S(2)}) collective-permute-start(bf16[6,3,96,128]{3,2,1,0:T(8,128)(2,1)} %collective-permute-done.3.refs_7_), channel_id=1, source_target_pairs={{0,8},{8,0},{16,24},{24,16},{1,9},{9,1},{17,25},{25,17},{2,10},{10... | collective-permute-start | bytes 1327112 | tf_op jit(solution)/shard_map/ppermute | solution.py:358
  31.1 14.8 %work_1.1 = (f32[128,96,128]{2,1,0:T(8,128)S(1)}, bf16[24,192,96]{2,1,0:T(8,128)(2,1)S(1)}) custom-call(s32[3,672]{1,0:T(4,128)} %select_reduce_fusion.refs_0_, s32[24,27]{1,0:T(8,128)} %bitcast.56, s32[24,108]{1,0:T(8,128)} %bitcast.59, bf16[648,96,96]{2,1,0:T(8,128)(2,1)} %bitcast.51, ...), custom_call_target="tpu_custom_call", output_to_operand_aliasing={{1}: (9, {}), {0}: (8, {})} | custom-call | flops 2293235712 | bytes 20000000 | tf_op jit(solution)/shard_map/work_1/pallas_call | solution.py:299
  45.9 13.9 %work_2.1 = (bf16[4,4,3,96,128]{4,3,2,1,0:T(8,128)(2,1)}, f32[128,96,128]{2,1,0:T(8,128)S(1)}, bf16[24,192,96]{2,1,0:T(8,128)(2,1)S(1)}) custom-call(s32[3,672]{1,0:T(4,128)} %select_reduce_fusion.refs_0_, s32[24,27]{1,0:T(8,128)} %bitcast.57, s32[24,108]{1,0:T(8,128)} %bitcast.60, ...), custom_call_target="tpu_custom_call", output_to_operand_aliasing={{2}: (7, {}), {1}: (6, {})} | custom-call | flops 2293235712 | bytes 20000000 | tf_op jit(solution)/shard_map/work_2/pallas_call | solution.py:299
  59.9 0.9 keep_part.1
  60.8 2.1 %collective-permute-done.6 = bf16[4,4,3,96,128]{4,3,2,1,0:T(8,128)(2,1)S(1)} collective-permute-done((bf16[4,4,3,96,128]{4,3,2,1,0:T(8,128)(2,1)}, bf16[4,4,3,96,128]{4,3,2,1,0:T(8,128)(2,1)S(1)}, u32[]{:S(2)}, u32[]{:S(2)}) %collective-permute-start.6) | collective-permute-done | bytes 1179680 | tf_op jit(solution)/shard_map/ppermute | solution.py:358
  62.9 0.5 fusion.19
  63.8 1.5 %collective-permute-start.9 = (bf16[4,3,96,128]{3,2,1,0:T(8,128)(2,1)S(1)}, bf16[4,3,96,128]{3,2,1,0:T(8,128)(2,1)S(1)}, u32[]{:S(2)}, u32[]{:S(2)}) collective-permute-start(bf16[4,3,96,128]{3,2,1,0:T(8,128)(2,1)S(1)} %get-tuple-element.38), channel_id=1, source_target_pairs={{0,24},{8,16},{16,8},{24,0},{1,25},{9,17},{17,9},{25,1},{2,26},{10... | collective-permute-start | bytes 884744 | tf_op jit(solution)/shard_map/ppermute | solution.py:358
  65.3 1.8 %collective-permute-start.8 = (bf16[4,3,96,128]{3,2,1,0:T(8,128)(2,1)S(1)}, bf16[4,3,96,128]{3,2,1,0:T(8,128)(2,1)S(1)}, u32[]{:S(2)}, u32[]{:S(2)}) collective-permute-start(bf16[4,3,96,128]{3,2,1,0:T(8,128)(2,1)S(1)} %get-tuple-element.39), channel_id=1, source_target_pairs={{0,16},{8,24},{16,0},{24,8},{1,17},{9,25},{17,1},{25,9},{2,18},{10... | collective-permute-start | bytes 884744 | tf_op jit(solution)/shard_map/ppermute | solution.py:358
  67.1 6.4 %collective-permute-done.7 = bf16[4,3,96,128]{3,2,1,0:T(8,128)(2,1)S(1)} collective-permute-done((bf16[4,3,96,128]{3,2,1,0:T(8,128)(2,1)S(1)}, bf16[4,3,96,128]{3,2,1,0:T(8,128)(2,1)S(1)}, u32[]{:S(2)}, u32[]{:S(2)}) %collective-permute-start.7) | collective-permute-done | bytes 294944 | tf_op jit(solution)/shard_map/ppermute | solution.py:358
  73.4 5.3 %collective-permute-done.9 = bf16[4,3,96,128]{3,2,1,0:T(8,128)(2,1)S(1)} collective-permute-done((bf16[4,3,96,128]{3,2,1,0:T(8,128)(2,1)S(1)}, bf16[4,3,96,128]{3,2,1,0:T(8,128)(2,1)S(1)}, u32[]{:S(2)}, u32[]{:S(2)}) %collective-permute-start.9) | collective-permute-done | bytes 294944 | tf_op jit(solution)/shard_map/ppermute | solution.py:358
  78.7 1.4 %collective-permute-done.8 = bf16[4,3,96,128]{3,2,1,0:T(8,128)(2,1)S(1)} collective-permute-done((bf16[4,3,96,128]{3,2,1,0:T(8,128)(2,1)S(1)}, bf16[4,3,96,128]{3,2,1,0:T(8,128)(2,1)S(1)}, u32[]{:S(2)}, u32[]{:S(2)}) %collective-permute-start.8) | collective-permute-done | bytes 294944 | tf_op jit(solution)/shard_map/ppermute | solution.py:358
  80.3 2.6 %collective-permute-start.10 = (bf16[3,96,128]{2,1,0:T(8,128)(2,1)S(1)}, bf16[3,96,128]{2,1,0:T(8,128)(2,1)S(1)}, u32[]{:S(2)}, u32[]{:S(2)}) collective-permute-start(bf16[3,96,128]{2,1,0:T(8,128)(2,1)S(1)} %get-tuple-element.40), channel_id=1, source_target_pairs={{0,2},{1,3},{2,0},{3,1},{4,6},{5,7},{6,4},{7,5},{8,10},{9,11},{10,... | collective-permute-start | bytes 221192 | tf_op jit(solution)/shard_map/ppermute | solution.py:358
  82.9 3.2 %collective-permute-start.12 = (bf16[3,96,128]{2,1,0:T(8,128)(2,1)S(1)}, bf16[3,96,128]{2,1,0:T(8,128)(2,1)S(1)}, u32[]{:S(2)}, u32[]{:S(2)}) collective-permute-start(bf16[3,96,128]{2,1,0:T(8,128)(2,1)S(1)} %get-tuple-element.41), channel_id=1, source_target_pairs={{0,6},{1,7},{2,4},{3,5},{4,2},{5,3},{6,0},{7,1},{8,14},{9,15},{10,... | collective-permute-start | bytes 221192 | tf_op jit(solution)/shard_map/ppermute | solution.py:358
  86.6 3.3 %collective-permute-done.12 = bf16[3,96,128]{2,1,0:T(8,128)(2,1)S(1)} collective-permute-done((bf16[3,96,128]{2,1,0:T(8,128)(2,1)S(1)}, bf16[3,96,128]{2,1,0:T(8,128)(2,1)S(1)}, u32[]{:S(2)}, u32[]{:S(2)}) %collective-permute-start.12) | collective-permute-done | bytes 73760 | tf_op jit(solution)/shard_map/ppermute | solution.py:358
  89.9 3.0 %collective-permute-done.11 = bf16[3,96,128]{2,1,0:T(8,128)(2,1)S(1)} collective-permute-done((bf16[3,96,128]{2,1,0:T(8,128)(2,1)S(1)}, bf16[3,96,128]{2,1,0:T(8,128)(2,1)S(1)}, u32[]{:S(2)}, u32[]{:S(2)}) %collective-permute-start.11) | collective-permute-done | bytes 73760 | tf_op jit(solution)/shard_map/ppermute | solution.py:358
  93.3 0.7 maximum_bitcast_fusion
  (24 shorter events, 2.0 us)
Async XLA Ops:
  2.2 25.4 %collective-permute-start.2 = (bf16[6,3,96,128]{3,2,1,0:T(8,128)(2,1)}, bf16[6,3,96,128]{3,2,1,0:T(8,128)(2,1)}, u32[]{:S(2)}, u32[]{:S(2)}) collective-permute-start(bf16[6,3,96,128]{3,2,1,0:T(8,128)(2,1)} %get-tuple-element.19.refs_4_), channel_id=1, source_target_pairs={{0,16},{8,24},{16,0},{24,8},{1,17},{9,25},{17,1},{25,9},{2,18},{10... | collective-permute-start | bytes 1327112 | tf_op jit(solution)/shard_map/ppermute | solution.py:358
  5.3 22.3 %collective-permute-start = (bf16[6,3,96,128]{3,2,1,0:T(8,128)(2,1)}, bf16[6,3,96,128]{3,2,1,0:T(8,128)(2,1)}, u32[]{:S(2)}, u32[]{:S(2)}) collective-permute-start(bf16[6,3,96,128]{3,2,1,0:T(8,128)(2,1)} %get-tuple-element.19.refs_4_), channel_id=1, source_target_pairs={{0,8},{8,0},{16,24},{24,16},{1,9},{9,1},{17,25},{25,17},{2,10},{10... | collective-permute-start | bytes 1327112 | tf_op jit(solution)/shard_map/ppermute | solution.py:358
  6.8 20.9 %collective-permute-start.3 = (bf16[6,3,96,128]{3,2,1,0:T(8,128)(2,1)}, bf16[6,3,96,128]{3,2,1,0:T(8,128)(2,1)}, u32[]{:S(2)}, u32[]{:S(2)}) collective-permute-start(bf16[6,3,96,128]{3,2,1,0:T(8,128)(2,1)} %get-tuple-element.20.refs_5_), channel_id=1, source_target_pairs={{0,16},{8,24},{16,0},{24,8},{1,17},{9,25},{17,1},{25,9},{2,18},{10... | collective-permute-start | bytes 1327112 | tf_op jit(solution)/shard_map/ppermute | solution.py:358
  7.3 20.4 %collective-permute-start.1 = (bf16[6,3,96,128]{3,2,1,0:T(8,128)(2,1)}, bf16[6,3,96,128]{3,2,1,0:T(8,128)(2,1)}, u32[]{:S(2)}, u32[]{:S(2)}) collective-permute-start(bf16[6,3,96,128]{3,2,1,0:T(8,128)(2,1)} %get-tuple-element.20.refs_5_), channel_id=1, source_target_pairs={{0,8},{8,0},{16,24},{24,16},{1,9},{9,1},{17,25},{25,17},{2,10},{10... | collective-permute-start | bytes 1327112 | tf_op jit(solution)/shard_map/ppermute | solution.py:358
  27.6 18.3 %collective-permute-start.4 = (bf16[6,3,96,128]{3,2,1,0:T(8,128)(2,1)}, bf16[6,3,96,128]{3,2,1,0:T(8,128)(2,1)}, u32[]{:S(2)}, u32[]{:S(2)}) collective-permute-start(bf16[6,3,96,128]{3,2,1,0:T(8,128)(2,1)} %collective-permute-done.refs_4_), channel_id=1, source_target_pairs={{0,16},{8,24},{16,0},{24,8},{1,17},{9,25},{17,1},{25,9},{2,18},{10... | collective-permute-start | bytes 1327112 | tf_op jit(solution)/shard_map/ppermute | solution.py:358
  29.6 16.3 %collective-permute-start.5 = (bf16[6,3,96,128]{3,2,1,0:T(8,128)(2,1)}, bf16[6,3,96,128]{3,2,1,0:T(8,128)(2,1)}, u32[]{:S(2)}, u32[]{:S(2)}) collective-permute-start(bf16[6,3,96,128]{3,2,1,0:T(8,128)(2,1)} %collective-permute-done.3.refs_7_), channel_id=1, source_target_pairs={{0,8},{8,0},{16,24},{24,16},{1,9},{9,1},{17,25},{25,17},{2,10},{10... | collective-permute-start | bytes 1327112 | tf_op jit(solution)/shard_map/ppermute | solution.py:358
  59.8 3.1 %collective-permute-start.6 = (bf16[4,4,3,96,128]{4,3,2,1,0:T(8,128)(2,1)}, bf16[4,4,3,96,128]{4,3,2,1,0:T(8,128)(2,1)S(1)}, u32[]{:S(2)}, u32[]{:S(2)}) collective-permute-start(bf16[4,4,3,96,128]{4,3,2,1,0:T(8,128)(2,1)} %get-tuple-element.32), channel_id=1, source_target_pairs={{0,1},{1,0},{2,3},{3,2},{4,5},{5,4},{6,7},{7,6},{8,9},{9,8},{10,11... | collective-permute-start | bytes 3538952 | tf_op jit(solution)/shard_map/ppermute | solution.py:358
  63.5 9.9 %collective-permute-start.7 = (bf16[4,3,96,128]{3,2,1,0:T(8,128)(2,1)S(1)}, bf16[4,3,96,128]{3,2,1,0:T(8,128)(2,1)S(1)}, u32[]{:S(2)}, u32[]{:S(2)}) collective-permute-start(bf16[4,3,96,128]{3,2,1,0:T(8,128)(2,1)S(1)} %get-tuple-element.37), channel_id=1, source_target_pairs={{0,8},{8,0},{16,24},{24,16},{1,9},{9,1},{17,25},{25,17},{2,10},{10... | collective-permute-start | bytes 884744 | tf_op jit(solution)/shard_map/ppermute | solution.py:358
  63.8 14.9 %collective-permute-start.9 = (bf16[4,3,96,128]{3,2,1,0:T(8,128)(2,1)S(1)}, bf16[4,3,96,128]{3,2,1,0:T(8,128)(2,1)S(1)}, u32[]{:S(2)}, u32[]{:S(2)}) collective-permute-start(bf16[4,3,96,128]{3,2,1,0:T(8,128)(2,1)S(1)} %get-tuple-element.38), channel_id=1, source_target_pairs={{0,24},{8,16},{16,8},{24,0},{1,25},{9,17},{17,9},{25,1},{2,26},{10... | collective-permute-start | bytes 884744 | tf_op jit(solution)/shard_map/ppermute | solution.py:358
  65.3 14.8 %collective-permute-start.8 = (bf16[4,3,96,128]{3,2,1,0:T(8,128)(2,1)S(1)}, bf16[4,3,96,128]{3,2,1,0:T(8,128)(2,1)S(1)}, u32[]{:S(2)}, u32[]{:S(2)}) collective-permute-start(bf16[4,3,96,128]{3,2,1,0:T(8,128)(2,1)S(1)} %get-tuple-element.39), channel_id=1, source_target_pairs={{0,16},{8,24},{16,0},{24,8},{1,17},{9,25},{17,1},{25,9},{2,18},{10... | collective-permute-start | bytes 884744 | tf_op jit(solution)/shard_map/ppermute | solution.py:358
  80.3 6.3 %collective-permute-start.10 = (bf16[3,96,128]{2,1,0:T(8,128)(2,1)S(1)}, bf16[3,96,128]{2,1,0:T(8,128)(2,1)S(1)}, u32[]{:S(2)}, u32[]{:S(2)}) collective-permute-start(bf16[3,96,128]{2,1,0:T(8,128)(2,1)S(1)} %get-tuple-element.40), channel_id=1, source_target_pairs={{0,2},{1,3},{2,0},{3,1},{4,6},{5,7},{6,4},{7,5},{8,10},{9,11},{10,... | collective-permute-start | bytes 221192 | tf_op jit(solution)/shard_map/ppermute | solution.py:358
  82.9 7.0 %collective-permute-start.12 = (bf16[3,96,128]{2,1,0:T(8,128)(2,1)S(1)}, bf16[3,96,128]{2,1,0:T(8,128)(2,1)S(1)}, u32[]{:S(2)}, u32[]{:S(2)}) collective-permute-start(bf16[3,96,128]{2,1,0:T(8,128)(2,1)S(1)} %get-tuple-element.41), channel_id=1, source_target_pairs={{0,6},{1,7},{2,4},{3,5},{4,2},{5,3},{6,0},{7,1},{8,14},{9,15},{10,... | collective-permute-start | bytes 221192 | tf_op jit(solution)/shard_map/ppermute | solution.py:358
  86.1 6.8 %collective-permute-start.11 = (bf16[3,96,128]{2,1,0:T(8,128)(2,1)S(1)}, bf16[3,96,128]{2,1,0:T(8,128)(2,1)S(1)}, u32[]{:S(2)}, u32[]{:S(2)}) collective-permute-start(bf16[3,96,128]{2,1,0:T(8,128)(2,1)S(1)} %get-tuple-element.42), channel_id=1, source_target_pairs={{0,4},{1,5},{2,6},{3,7},{4,0},{5,1},{6,2},{7,3},{8,12},{9,13},{10,... | collective-permute-start | bytes 221192 | tf_op jit(solution)/shard_map/ppermute | solution.py:358

commit v11 on v10

--- a/solution.py
+++ b/solution.py
@@ -88,9 +88,11 @@
     take = lambda n: [refs.pop(0) for _ in range(n)]
     list_ref, col_ref, tgt_ref, a_hbm = take(4)
     p_hbm = take(cfg["sources"])
-    take(0 if first else 2)
+    naccs = cfg["naccs"]
+    take(0 if first else naccs + 1)
     give_out = take(1 if last else 0)
-    acc, pt = take(2)
+    accs = take(naccs)
+    (pt,) = take(1)
     p_vmem, a_rows = take(2)
     aps = take(UNROLL)
     a_sem, sem, out_sem = take(3)
@@ -132,7 +134,8 @@
 
         def clear(s, _):
             for x in range(8):
-                acc[s * 8 + x] = jnp.zeros((width, LANES), acc.dtype)
+                for acc in accs:
+                    acc[s * 8 + x] = jnp.zeros((width, LANES), acc.dtype)
             return 0
 
         lax.fori_loop(0, slots // 8, clear, 0)
@@ -186,6 +189,7 @@
     def collect(i, k, partial):
         for n in range(per_row):
             for m in range(per_row):
+                acc = accs[m % naccs]
                 s = tgt_ref[i, n * nonzeros * per_row + k * per_row + m]
                 acc[s] = acc[s] + partial[
                     n * width : (n + 1) * width, m * LANES : (m + 1) * LANES
@@ -227,7 +231,7 @@
         (stage,), (out,) = stages, give_out
 
         def emit(rz, _):
-            pack_part(cfg, acc, stage, rz, 1)
+            pack_part(cfg, accs, stage, rz, 1)
             pltpu.make_async_copy(stage.at[rz], out.at[rz], out_sem.at[0]).start()
             return 0
 
@@ -235,45 +239,46 @@
         pltpu.make_async_copy(stage, out, out_sem.at[0]).wait()
 
 
-def pack_part(cfg, acc, to, rz, rc):
+def pack_part(cfg, accs, to, rz, rc):
     members = cfg["members"]
     me = lax.axis_index("blk").astype(jnp.int32)
     rank = lax.axis_index("grp").astype(jnp.int32)
     group = ((rank >> 1) ^ rz) * 2 + ((rank & 1) ^ rc)
     for r in range(members):
         s = group * (OWN * members) + (me ^ r) * OWN
-        packed = pack_four([acc[s + x] for x in range(OWN)], cfg["width"])
+        packed = pack_four([sum(acc[s + x] for acc in accs) for x in range(OWN)], cfg["width"])
         for t in range(3):
             to[rz, r, t] = packed[t].astype(to.dtype)
 
 
-def keep_kernel(cfg, _, keep_ref, acc):
+def keep_kernel(cfg, *refs):
+    keep_ref, *accs = refs[cfg["naccs"] :]
+
     def emit(rz, _):
-        pack_part(cfg, acc, keep_ref, rz, 0)
+        pack_part(cfg, accs, keep_ref, rz, 0)
         return 0
 
     lax.fori_loop(0, cfg["groups"] // 2, emit, 0)
 
 
-def keep_part(cfg, acc):
+def keep_part(cfg, accs):
     vmem = pl.BlockSpec(memory_space=pltpu.VMEM)
-    keep, _ = pl.pallas_call(
+    return pl.pallas_call(
         functools.partial(keep_kernel, cfg),
-        in_specs=[vmem],
-        out_specs=[vmem] * 2,
+        in_specs=[vmem] * len(accs),
+        out_specs=[vmem] * (1 + len(accs)),
         out_shape=[
             pltpu.VMEM((cfg["groups"] // 2, cfg["members"], 3, cfg["width"], LANES), jnp.float32),
-            pltpu.VMEM(acc.shape, acc.dtype),
+            *[pltpu.VMEM(acc.shape, acc.dtype) for acc in accs],
         ],
-        input_output_aliases={0: 1},
+        input_output_aliases={x: x + 1 for x in range(len(accs))},
         compiler_params=pltpu.CompilerParams(vmem_limit_bytes=8 * 1024 * 1024),
         cost_estimate=pl.CostEstimate(flops=4_000_000, bytes_accessed=4_000_000, transcendentals=0),
         name="keep_part",
-    )(acc)
-    return keep
-
-
-def work(cfg, tables, a_rows, packed, acc=None, pt=None):
+    )(*accs)[0]
+
+
+def work(cfg, tables, a_rows, packed, accs=None, pt=None):
     width, rows, nonzeros, per_row = cfg["width"], cfg["rows"], cfg["nonzeros"], cfg["per_row"]
     slots, members, groups = cfg["slots"], cfg["members"], cfg["groups"]
     first, last = cfg["first"], cfg["last"]
@@ -281,21 +286,21 @@
     quads = sum(x.shape[0] for x in packed)
     vmem = pl.BlockSpec(memory_space=pltpu.VMEM)
     operands = [a_rows.reshape(rows * nonzeros, width, width), *packed]
-    in_specs, out_specs = [HBM] * len(operands), [vmem] * 2
+    in_specs, out_specs = [HBM] * len(operands), [vmem] * (cfg["naccs"] + 1)
     shapes, stages, aliases = [
-        pltpu.VMEM((slots, width, LANES), jnp.float32),
+        *[pltpu.VMEM((slots, width, LANES), jnp.float32)] * cfg["naccs"],
         pltpu.VMEM((rows, per_row * width, width), jnp.bfloat16),
     ], [], {}
-    resident = slots * width * LANES * 4 + rows * per_row * width * LANES * 2
+    resident = cfg["naccs"] * slots * width * LANES * 4 + rows * per_row * width * LANES * 2
     if not first:
-        operands += [acc, pt]
-        in_specs += [vmem] * 2
+        operands += [*accs, pt]
+        in_specs += [vmem] * (cfg["naccs"] + 1)
     if last:
         whole = (groups // 2, members, 3, width, LANES)
         stages = [pltpu.VMEM(whole, jnp.bfloat16)]
         shapes, out_specs = [jax.ShapeDtypeStruct(whole, jnp.bfloat16)] + shapes, [HBM] + out_specs
     if not first:
-        aliases = {len(tables) + len(operands) - x: len(shapes) - x for x in (1, 2)}
+        aliases = {len(tables) + len(operands) - x: len(shapes) - x for x in range(1, cfg["naccs"] + 2)}
     return pl.pallas_call(
         functools.partial(work_kernel, cfg),
         grid_spec=pltpu.PrefetchScalarGridSpec(
@@ -371,21 +376,22 @@
     cfg = dict(
         width=width, rows=rows, nonzeros=nonzeros, per_row=per_row, slots=slots,
         members=members, groups=groups,
+        naccs=2 if slots <= 128 else 1,
     )
-    acc = pt = None
+    accs = pt = None
     for p in range(phases):
         outs = work(
             {**cfg, "phase": p, "first": p == 0, "last": p == phases - 1, "from": sources[p][0]},
-            (lists, col_index[0], target[0]), a_blocks[0], [x for r in sources[p] for x in packed[r]], acc, pt,
+            (lists, col_index[0], target[0]), a_blocks[0], [x for r in sources[p] for x in packed[r]], accs, pt,
         )
-        acc, pt = outs[-2:]
+        accs, pt = outs[-1 - cfg["naccs"] : -1], outs[-1]
         if p == 0 and members == 4:
-            near, acc = lax.optimization_barrier((packed[1] + packed[2], acc))
+            near, accs = lax.optimization_barrier((packed[1] + packed[2], accs))
             packed = {0: own, 1: near[:2], 2: near[2:]}
             packed[3] = [exchange(near[0], 2), exchange(near[3], 1)]
 
     given = exchange(outs[0], 1, "grp", groups)
-    total = keep_part(cfg, acc) + given.astype(f32)
+    total = keep_part(cfg, accs) + given.astype(f32)
     got = [exchange(total[:, r].astype(bf16), r) for r in range(1, members)]
     total = total[:, 0]
     for part in got:

time: 93.7 us -> 93 us (level)
  Pallas kernels: 49.5 us -> 48 us
  waiting for transfers between devices: 21.5 us -> 22.8 us
  starting transfers between devices: 18.6 us -> 17.6 us
    pallas_call x3, Pallas kernels: 46.4 us -> 44.8 us  [work(): pl.pallas_call(functools.partial(work_kernel, cfg), grid_spec=pltpu.Prefe...]
    ppermute x13, waiting for transfers between devices: 21.5 us -> 22.8 us  [exchange(): return lax.ppermute(x, axis, [(d, d ^ r) for d in range(size)])]
    ppermute x13, starting transfers between devices: 18.6 us -> 17.6 us  [exchange(): return lax.ppermute(x, axis, [(d, d ^ r) for d in range(size)])]
  transfers between devices with their start and end apart: 13 -> 13, of which waited for: 6 -> 7; matrix products, arithmetic and copies ran while one was open for 3% -> 3% of each run, Pallas kernels for 36% -> 36%
where the time goes in v11:
time: 93 us; the launch traced here: 92.8 us
  Pallas kernels  48 us (52%)
  waiting for transfers between devices  22.8 us (25%)
  starting transfers between devices  17.6 us (19%)
  other arithmetic  3.84 us (4%)
    pallas_call x3, Pallas kernels, work(): pl.pallas_call(functools.partial(work_kernel, cfg), grid_spec=pltpu.Prefe...  44.8 us
    ppermute x13, waiting for transfers between devices, exchange(): return lax.ppermute(x, axis, [(d, d ^ r) for d in range(size)])  22.8 us
    ppermute x13, starting transfers between devices, exchange(): return lax.ppermute(x, axis, [(d, d ^ r) for d in range(size)])  17.6 us
    pallas_call x1, Pallas kernels, pack_prolong(): pl.pallas_call(pack_kernel, in_specs=[HBM], out_specs=[HBM] * 2, out_shap...  2.22 us
  transfers between devices with their start and end apart: 13, of which 7 were waited for; matrix products, arithmetic and copies ran while one was open for 3% of the time, Pallas kernels for 36%

profile of v11, /device:TPU:0, one launch (start us, length us, event | category | flops | bytes accessed | tf_op | source)
XLA Modules:
  0.0 92.8 jit_solution(1861925058151146881)
XLA Ops:
  0.0 2.2 %pack_prolong.1 = (bf16[6,3,96,128]{3,2,1,0:T(8,128)(2,1)}, bf16[6,3,96,128]{3,2,1,0:T(8,128)(2,1)}) custom-call(bf16[12,4,96,96]{3,2,1,0:T(8,128)(2,1)} %bitcast.54), custom_call_target="tpu_custom_call" | custom-call | tf_op jit(solution)/shard_map/pack_prolong/pallas_call | solution.py:61
  2.2 3.0 %collective-permute-start.2 = (bf16[6,3,96,128]{3,2,1,0:T(8,128)(2,1)}, bf16[6,3,96,128]{3,2,1,0:T(8,128)(2,1)}, u32[]{:S(2)}, u32[]{:S(2)}) collective-permute-start(bf16[6,3,96,128]{3,2,1,0:T(8,128)(2,1)} %get-tuple-element.23.refs_4_), channel_id=1, source_target_pairs={{0,16},{8,24},{16,0},{24,8},{1,17},{9,25},{17,1},{25,9},{2,18},{10... | collective-permute-start | bytes 1327112 | tf_op jit(solution)/shard_map/ppermute | solution.py:363
  5.3 1.5 %collective-permute-start = (bf16[6,3,96,128]{3,2,1,0:T(8,128)(2,1)}, bf16[6,3,96,128]{3,2,1,0:T(8,128)(2,1)}, u32[]{:S(2)}, u32[]{:S(2)}) collective-permute-start(bf16[6,3,96,128]{3,2,1,0:T(8,128)(2,1)} %get-tuple-element.23.refs_4_), channel_id=1, source_target_pairs={{0,8},{8,0},{16,24},{24,16},{1,9},{9,1},{17,25},{25,17},{2,10},{10... | collective-permute-start | bytes 1327112 | tf_op jit(solution)/shard_map/ppermute | solution.py:363
  6.8 0.5 collective-permute-start.3
  7.4 0.7 add_add_fusion
  8.5 1.3 %select_reduce_fusion.refs_0_ = s32[3,672]{1,0:T(4,128)} fusion(s32[648]{0:T(1024)S(1)} %get-tuple-element.54, s32[3,672]{1,0:T(4,128)S(1)} %multiply_add_fusion, s32[648]{0:T(1024)S(1)} %get-tuple-element.55), kind=kLoop, calls=%fused_computation | loop fusion | flops 3917088 | bytes 21312 | tf_op jit(solution)/shard_map/reduce_sum | solution.py:348
  9.8 17.6 %work_0.1 = (f32[128,96,128]{2,1,0:T(8,128)S(1)}, f32[128,96,128]{2,1,0:T(8,128)S(1)}, bf16[24,192,96]{2,1,0:T(8,128)(2,1)S(1)}) custom-call(s32[3,672]{1,0:T(4,128)} %select_reduce_fusion.refs_0_, s32[24,27]{1,0:T(8,128)} %bitcast.55, s32[24,108]{1,0:T(8,128)} %bitcast.58, bf16[648,96,96]{2,1,0:T(8,128)(2,1)} %bitcast.50, ...), custom_call_target="tpu_custom_call" | custom-call | flops 2293235712 | bytes 20000000 | tf_op jit(solution)/shard_map/work_0/pallas_call | solution.py:304
  27.5 2.0 %collective-permute-start.4 = (bf16[6,3,96,128]{3,2,1,0:T(8,128)(2,1)}, bf16[6,3,96,128]{3,2,1,0:T(8,128)(2,1)}, u32[]{:S(2)}, u32[]{:S(2)}) collective-permute-start(bf16[6,3,96,128]{3,2,1,0:T(8,128)(2,1)} %collective-permute-done.refs_4_), channel_id=1, source_target_pairs={{0,16},{8,24},{16,0},{24,8},{1,17},{9,25},{17,1},{25,9},{2,18},{10... | collective-permute-start | bytes 1327112 | tf_op jit(solution)/shard_map/ppermute | solution.py:363
  29.5 2.6 %collective-permute-start.5 = (bf16[6,3,96,128]{3,2,1,0:T(8,128)(2,1)}, bf16[6,3,96,128]{3,2,1,0:T(8,128)(2,1)}, u32[]{:S(2)}, u32[]{:S(2)}) collective-permute-start(bf16[6,3,96,128]{3,2,1,0:T(8,128)(2,1)} %collective-permute-done.3.refs_7_), channel_id=1, source_target_pairs={{0,8},{8,0},{16,24},{24,16},{1,9},{9,1},{17,25},{25,17},{2,10},{10... | collective-permute-start | bytes 1327112 | tf_op jit(solution)/shard_map/ppermute | solution.py:363
  32.1 14.5 %work_1.1 = (f32[128,96,128]{2,1,0:T(8,128)S(1)}, f32[128,96,128]{2,1,0:T(8,128)S(1)}, bf16[24,192,96]{2,1,0:T(8,128)(2,1)S(1)}) custom-call(s32[3,672]{1,0:T(4,128)} %select_reduce_fusion.refs_0_, s32[24,27]{1,0:T(8,128)} %bitcast.56, s32[24,108]{1,0:T(8,128)} %bitcast.59, ...), custom_call_target="tpu_custom_call", output_to_operand_aliasing={{2}: (10, {}), {1}: (9, {}), {0}: (8, {})} | custom-call | flops 2293235712 | bytes 20000000 | tf_op jit(solution)/shard_map/work_1/pallas_call | solution.py:304
  46.7 12.7 %work_2.1 = (bf16[4,4,3,96,128]{4,3,2,1,0:T(8,128)(2,1)}, f32[128,96,128]{2,1,0:T(8,128)S(1)}, f32[128,96,128]{2,1,0:T(8,128)S(1)}, bf16[24,192,96]{2,1,0:T(8,128)(2,1)S(1)}) custom-call(s32[3,672]{1,0:T(4,128)} %select_reduce_fusion.refs_0_, s32[24,27]{1,0:T(8,128)} %bitcast.57, ...), custom_call_target="tpu_custom_call", output_to_operand_aliasing={{3}: (8, {}), {2}: (7, {}), {1}: (6, {})} | custom-call | flops 2293235712 | bytes 20000000 | tf_op jit(solution)/shard_map/work_2/pallas_call | solution.py:304
  59.4 0.9 keep_part.1
  60.4 2.1 %collective-permute-done.6 = bf16[4,4,3,96,128]{4,3,2,1,0:T(8,128)(2,1)S(1)} collective-permute-done((bf16[4,4,3,96,128]{4,3,2,1,0:T(8,128)(2,1)}, bf16[4,4,3,96,128]{4,3,2,1,0:T(8,128)(2,1)S(1)}, u32[]{:S(2)}, u32[]{:S(2)}) %collective-permute-start.6) | collective-permute-done | bytes 1179680 | tf_op jit(solution)/shard_map/ppermute | solution.py:363
  62.5 0.5 fusion.19
  63.1 1.5 %collective-permute-start.7 = (bf16[4,3,96,128]{3,2,1,0:T(8,128)(2,1)S(1)}, bf16[4,3,96,128]{3,2,1,0:T(8,128)(2,1)S(1)}, u32[]{:S(2)}, u32[]{:S(2)}) collective-permute-start(bf16[4,3,96,128]{3,2,1,0:T(8,128)(2,1)S(1)} %get-tuple-element.45), channel_id=1, source_target_pairs={{0,8},{8,0},{16,24},{24,16},{1,9},{9,1},{17,25},{25,17},{2,10},{10... | collective-permute-start | bytes 884744 | tf_op jit(solution)/shard_map/ppermute | solution.py:363
  64.5 1.7 %collective-permute-start.9 = (bf16[4,3,96,128]{3,2,1,0:T(8,128)(2,1)S(1)}, bf16[4,3,96,128]{3,2,1,0:T(8,128)(2,1)S(1)}, u32[]{:S(2)}, u32[]{:S(2)}) collective-permute-start(bf16[4,3,96,128]{3,2,1,0:T(8,128)(2,1)S(1)} %get-tuple-element.46), channel_id=1, source_target_pairs={{0,24},{8,16},{16,8},{24,0},{1,25},{9,17},{17,9},{25,1},{2,26},{10... | collective-permute-start | bytes 884744 | tf_op jit(solution)/shard_map/ppermute | solution.py:363
  66.6 6.4 %collective-permute-done.7 = bf16[4,3,96,128]{3,2,1,0:T(8,128)(2,1)S(1)} collective-permute-done((bf16[4,3,96,128]{3,2,1,0:T(8,128)(2,1)S(1)}, bf16[4,3,96,128]{3,2,1,0:T(8,128)(2,1)S(1)}, u32[]{:S(2)}, u32[]{:S(2)}) %collective-permute-start.7) | collective-permute-done | bytes 294944 | tf_op jit(solution)/shard_map/ppermute | solution.py:363
  73.0 6.7 %collective-permute-done.9 = bf16[4,3,96,128]{3,2,1,0:T(8,128)(2,1)S(1)} collective-permute-done((bf16[4,3,96,128]{3,2,1,0:T(8,128)(2,1)S(1)}, bf16[4,3,96,128]{3,2,1,0:T(8,128)(2,1)S(1)}, u32[]{:S(2)}, u32[]{:S(2)}) %collective-permute-start.9) | collective-permute-done | bytes 294944 | tf_op jit(solution)/shard_map/ppermute | solution.py:363
  79.7 1.4 %collective-permute-done.8 = bf16[4,3,96,128]{3,2,1,0:T(8,128)(2,1)S(1)} collective-permute-done((bf16[4,3,96,128]{3,2,1,0:T(8,128)(2,1)S(1)}, bf16[4,3,96,128]{3,2,1,0:T(8,128)(2,1)S(1)}, u32[]{:S(2)}, u32[]{:S(2)}) %collective-permute-start.8) | collective-permute-done | bytes 294944 | tf_op jit(solution)/shard_map/ppermute | solution.py:363
  81.2 0.8 collective-permute-start.10
  82.0 3.0 %collective-permute-start.12 = (bf16[3,96,128]{2,1,0:T(8,128)(2,1)S(1)}, bf16[3,96,128]{2,1,0:T(8,128)(2,1)S(1)}, u32[]{:S(2)}, u32[]{:S(2)}) collective-permute-start(bf16[3,96,128]{2,1,0:T(8,128)(2,1)S(1)} %get-tuple-element.49), channel_id=1, source_target_pairs={{0,6},{1,7},{2,4},{3,5},{4,2},{5,3},{6,0},{7,1},{8,14},{9,15},{10,... | collective-permute-start | bytes 221192 | tf_op jit(solution)/shard_map/ppermute | solution.py:363
  85.7 3.3 %collective-permute-done.12 = bf16[3,96,128]{2,1,0:T(8,128)(2,1)S(1)} collective-permute-done((bf16[3,96,128]{2,1,0:T(8,128)(2,1)S(1)}, bf16[3,96,128]{2,1,0:T(8,128)(2,1)S(1)}, u32[]{:S(2)}, u32[]{:S(2)}) %collective-permute-start.12) | collective-permute-done | bytes 73760 | tf_op jit(solution)/shard_map/ppermute | solution.py:363
  89.0 2.7 %collective-permute-done.11 = bf16[3,96,128]{2,1,0:T(8,128)(2,1)S(1)} collective-permute-done((bf16[3,96,128]{2,1,0:T(8,128)(2,1)S(1)}, bf16[3,96,128]{2,1,0:T(8,128)(2,1)S(1)}, u32[]{:S(2)}, u32[]{:S(2)}) %collective-permute-start.11) | collective-permute-done | bytes 73760 | tf_op jit(solution)/shard_map/ppermute | solution.py:363
  92.1 0.7 maximum_bitcast_fusion
  (24 shorter events, 2.3 us)
Async XLA Ops:
  2.2 25.2 %collective-permute-start.2 = (bf16[6,3,96,128]{3,2,1,0:T(8,128)(2,1)}, bf16[6,3,96,128]{3,2,1,0:T(8,128)(2,1)}, u32[]{:S(2)}, u32[]{:S(2)}) collective-permute-start(bf16[6,3,96,128]{3,2,1,0:T(8,128)(2,1)} %get-tuple-element.23.refs_4_), channel_id=1, source_target_pairs={{0,16},{8,24},{16,0},{24,8},{1,17},{9,25},{17,1},{25,9},{2,18},{10... | collective-permute-start | bytes 1327112 | tf_op jit(solution)/shard_map/ppermute | solution.py:363
  5.3 22.2 %collective-permute-start = (bf16[6,3,96,128]{3,2,1,0:T(8,128)(2,1)}, bf16[6,3,96,128]{3,2,1,0:T(8,128)(2,1)}, u32[]{:S(2)}, u32[]{:S(2)}) collective-permute-start(bf16[6,3,96,128]{3,2,1,0:T(8,128)(2,1)} %get-tuple-element.23.refs_4_), channel_id=1, source_target_pairs={{0,8},{8,0},{16,24},{24,16},{1,9},{9,1},{17,25},{25,17},{2,10},{10... | collective-permute-start | bytes 1327112 | tf_op jit(solution)/shard_map/ppermute | solution.py:363
  6.8 20.7 %collective-permute-start.3 = (bf16[6,3,96,128]{3,2,1,0:T(8,128)(2,1)}, bf16[6,3,96,128]{3,2,1,0:T(8,128)(2,1)}, u32[]{:S(2)}, u32[]{:S(2)}) collective-permute-start(bf16[6,3,96,128]{3,2,1,0:T(8,128)(2,1)} %get-tuple-element.24.refs_5_), channel_id=1, source_target_pairs={{0,16},{8,24},{16,0},{24,8},{1,17},{9,25},{17,1},{25,9},{2,18},{10... | collective-permute-start | bytes 1327112 | tf_op jit(solution)/shard_map/ppermute | solution.py:363
  7.3 20.2 %collective-permute-start.1 = (bf16[6,3,96,128]{3,2,1,0:T(8,128)(2,1)}, bf16[6,3,96,128]{3,2,1,0:T(8,128)(2,1)}, u32[]{:S(2)}, u32[]{:S(2)}) collective-permute-start(bf16[6,3,96,128]{3,2,1,0:T(8,128)(2,1)} %get-tuple-element.24.refs_5_), channel_id=1, source_target_pairs={{0,8},{8,0},{16,24},{24,16},{1,9},{9,1},{17,25},{25,17},{2,10},{10... | collective-permute-start | bytes 1327112 | tf_op jit(solution)/shard_map/ppermute | solution.py:363
  27.5 19.1 %collective-permute-start.4 = (bf16[6,3,96,128]{3,2,1,0:T(8,128)(2,1)}, bf16[6,3,96,128]{3,2,1,0:T(8,128)(2,1)}, u32[]{:S(2)}, u32[]{:S(2)}) collective-permute-start(bf16[6,3,96,128]{3,2,1,0:T(8,128)(2,1)} %collective-permute-done.refs_4_), channel_id=1, source_target_pairs={{0,16},{8,24},{16,0},{24,8},{1,17},{9,25},{17,1},{25,9},{2,18},{10... | collective-permute-start | bytes 1327112 | tf_op jit(solution)/shard_map/ppermute | solution.py:363
  29.5 17.1 %collective-permute-start.5 = (bf16[6,3,96,128]{3,2,1,0:T(8,128)(2,1)}, bf16[6,3,96,128]{3,2,1,0:T(8,128)(2,1)}, u32[]{:S(2)}, u32[]{:S(2)}) collective-permute-start(bf16[6,3,96,128]{3,2,1,0:T(8,128)(2,1)} %collective-permute-done.3.refs_7_), channel_id=1, source_target_pairs={{0,8},{8,0},{16,24},{24,16},{1,9},{9,1},{17,25},{25,17},{2,10},{10... | collective-permute-start | bytes 1327112 | tf_op jit(solution)/shard_map/ppermute | solution.py:363
  59.4 3.1 %collective-permute-start.6 = (bf16[4,4,3,96,128]{4,3,2,1,0:T(8,128)(2,1)}, bf16[4,4,3,96,128]{4,3,2,1,0:T(8,128)(2,1)S(1)}, u32[]{:S(2)}, u32[]{:S(2)}) collective-permute-start(bf16[4,4,3,96,128]{4,3,2,1,0:T(8,128)(2,1)} %get-tuple-element.40), channel_id=1, source_target_pairs={{0,1},{1,0},{2,3},{3,2},{4,5},{5,4},{6,7},{7,6},{8,9},{9,8},{10,11... | collective-permute-start | bytes 3538952 | tf_op jit(solution)/shard_map/ppermute | solution.py:363
  63.1 9.9 %collective-permute-start.7 = (bf16[4,3,96,128]{3,2,1,0:T(8,128)(2,1)S(1)}, bf16[4,3,96,128]{3,2,1,0:T(8,128)(2,1)S(1)}, u32[]{:S(2)}, u32[]{:S(2)}) collective-permute-start(bf16[4,3,96,128]{3,2,1,0:T(8,128)(2,1)S(1)} %get-tuple-element.45), channel_id=1, source_target_pairs={{0,8},{8,0},{16,24},{24,16},{1,9},{9,1},{17,25},{25,17},{2,10},{10... | collective-permute-start | bytes 884744 | tf_op jit(solution)/shard_map/ppermute | solution.py:363
  64.5 15.1 %collective-permute-start.9 = (bf16[4,3,96,128]{3,2,1,0:T(8,128)(2,1)S(1)}, bf16[4,3,96,128]{3,2,1,0:T(8,128)(2,1)S(1)}, u32[]{:S(2)}, u32[]{:S(2)}) collective-permute-start(bf16[4,3,96,128]{3,2,1,0:T(8,128)(2,1)S(1)} %get-tuple-element.46), channel_id=1, source_target_pairs={{0,24},{8,16},{16,8},{24,0},{1,25},{9,17},{17,9},{25,1},{2,26},{10... | collective-permute-start | bytes 884744 | tf_op jit(solution)/shard_map/ppermute | solution.py:363
  66.2 14.8 %collective-permute-start.8 = (bf16[4,3,96,128]{3,2,1,0:T(8,128)(2,1)S(1)}, bf16[4,3,96,128]{3,2,1,0:T(8,128)(2,1)S(1)}, u32[]{:S(2)}, u32[]{:S(2)}) collective-permute-start(bf16[4,3,96,128]{3,2,1,0:T(8,128)(2,1)S(1)} %get-tuple-element.47), channel_id=1, source_target_pairs={{0,16},{8,24},{16,0},{24,8},{1,17},{9,25},{17,1},{25,9},{2,18},{10... | collective-permute-start | bytes 884744 | tf_op jit(solution)/shard_map/ppermute | solution.py:363
  81.2 4.5 %collective-permute-start.10 = (bf16[3,96,128]{2,1,0:T(8,128)(2,1)S(1)}, bf16[3,96,128]{2,1,0:T(8,128)(2,1)S(1)}, u32[]{:S(2)}, u32[]{:S(2)}) collective-permute-start(bf16[3,96,128]{2,1,0:T(8,128)(2,1)S(1)} %get-tuple-element.48), channel_id=1, source_target_pairs={{0,2},{1,3},{2,0},{3,1},{4,6},{5,7},{6,4},{7,5},{8,10},{9,11},{10,... | collective-permute-start | bytes 221192 | tf_op jit(solution)/shard_map/ppermute | solution.py:363
  82.0 7.0 %collective-permute-start.12 = (bf16[3,96,128]{2,1,0:T(8,128)(2,1)S(1)}, bf16[3,96,128]{2,1,0:T(8,128)(2,1)S(1)}, u32[]{:S(2)}, u32[]{:S(2)}) collective-permute-start(bf16[3,96,128]{2,1,0:T(8,128)(2,1)S(1)} %get-tuple-element.49), channel_id=1, source_target_pairs={{0,6},{1,7},{2,4},{3,5},{4,2},{5,3},{6,0},{7,1},{8,14},{9,15},{10,... | collective-permute-start | bytes 221192 | tf_op jit(solution)/shard_map/ppermute | solution.py:363
  85.0 6.7 %collective-permute-start.11 = (bf16[3,96,128]{2,1,0:T(8,128)(2,1)S(1)}, bf16[3,96,128]{2,1,0:T(8,128)(2,1)S(1)}, u32[]{:S(2)}, u32[]{:S(2)}) collective-permute-start(bf16[3,96,128]{2,1,0:T(8,128)(2,1)S(1)} %get-tuple-element.50), channel_id=1, source_target_pairs={{0,4},{1,5},{2,6},{3,7},{4,0},{5,1},{6,2},{7,3},{8,12},{9,13},{10,... | collective-permute-start | bytes 221192 | tf_op jit(solution)/shard_map/ppermute | solution.py:363
